TPU v7x, 256 devices: a whole 4x4x8 slice. The times are simulated.
256 devices in a mesh: lat: 8 (over x, y_hi), lon: 32 (over y_lo, z, core).
Axes of the slice: x: 4, y: 4 (y_hi: 2, y_lo: 2; y = y_hi * 2 + y_lo), z: 8, core: 2. Of those that a mesh axis runs over, the one named last changes fastest.
Arguments:
- field: float32 [160, 640, 384], P('lat', 'lon'), may hold values from -6 to 6
- lat_kernel: float32 [41], replicated, may hold values from 0.0121951215 to 0.036585364
- lon_kernel: float32 [41], replicated, may hold values from 0.0121951215 to 0.036585364
- time_taps: float32 [129], replicated, may hold values from -0.0058139535 to 0.0058139535
Outputs:
- basis: float32 [160, 640, 256], P('lat', 'lon')
- merged_factor: float32 [256, 256], replicated
All inputs are finite; a program needn't handle non-finite values.
Results may differ from a plain program's by a relative error of at most 0.00016.
Values sent between devices are 32-bit elements; how exact they have to be, the bound alone decides.
No kernel may reach another device: no remote copies, remote signals or barrier semaphores. Data moves between devices by JAX's collectives and lax.ppermute only.
A program may use at most 64 MiB of HBM per device.

v0:
```python
import jax
import jax.numpy as jnp
from jax import lax
from jax.sharding import PartitionSpec as P

TH = 64
SH = 20


def extended_2(value, sides, width, wrap):
    for axis, dim in sides:
        peers, length = (lax.axis_size(axis), value.shape[dim])
        up = [(i, (i + 1) % peers) for i in range(peers if wrap else peers - 1)]
        down = [(j, i) for i, j in up]
        last = lax.slice_in_dim(value, length - width, length, axis=dim)
        initial = lax.slice_in_dim(value, 0, width, axis=dim)
        before = lax.ppermute(last, axis, up)
        after = lax.ppermute(initial, axis, down)
        value = jnp.concatenate([before, value, after], axis=dim)
    return value


def skewed(coeffs, count, width):
    period = jnp.pad(coeffs, (0, count))
    flat = jnp.tile(period, count)[: count * width]
    return flat.reshape(count, width)


def banded(kernel, count):
    return skewed(kernel, count, count + 2 * SH)


def smooth_rows(band, extended):
    rows_in, cols_in, hours = extended.shape
    flat = extended.reshape(rows_in, cols_in * hours)
    result = jnp.dot(
        band, flat, precision=lax.Precision.HIGHEST, preferred_element_type=jnp.float32
    )
    return result.reshape(band.shape[0], cols_in, hours)


def body(field, lat_kernel, lon_kernel, time_taps):
    rows_lat, rows_lon, length_in = field.shape
    steps_out = length_in - 2 * TH
    lat_place = lax.axis_index("lat")
    total_lat = rows_lat * lax.axis_size("lat")
    cells = total_lat * rows_lon * lax.axis_size("lon")
    centre = (jnp.arange(2 * TH + 1, dtype=jnp.int32) == TH).astype(jnp.float32)
    taps_full = time_taps + centre
    skew_time = skewed(taps_full, steps_out, length_in)
    filtered = lax.dot_general(
        field.reshape(-1, length_in),
        skew_time,
        (((1,), (1,)), ((), ())),
        precision=lax.Precision.HIGHEST,
        preferred_element_type=jnp.float32,
    ).reshape(rows_lat, rows_lon, steps_out)
    lat_band = banded(lat_kernel, rows_lat)
    lon_band = banded(lon_kernel, rows_lon)
    extended = extended_2(filtered, (("lat", 0),), SH, False)
    narrow = smooth_rows(lat_band, extended)
    lat_done = extended_2(narrow, (("lon", 1),), SH, True)
    smooth = jnp.einsum(
        "jk,ikt->ijt",
        lon_band,
        lat_done,
        precision=lax.Precision.HIGHEST,
        preferred_element_type=jnp.float32,
    )
    globrow = (lat_place * rows_lat + jnp.arange(rows_lat, dtype=jnp.int32)).astype(jnp.float32)
    latitude = jnp.pi * (globrow + 0.5) / total_lat - jnp.pi / 2
    weights = jnp.sqrt(jnp.cos(latitude))
    matrix = (smooth * weights[:, None, None]).reshape(-1, steps_out)
    local_gram = lax.dot_general(
        matrix,
        matrix,
        (((0,), (0,)), ((), ())),
        precision=lax.Precision.HIGHEST,
        preferred_element_type=jnp.float32,
    )
    gram = lax.psum(local_gram, ("lat", "lon"))
    lower = jnp.linalg.cholesky(gram)
    scale = jnp.sqrt(jnp.float32(cells))
    identity = jnp.eye(steps_out, dtype=jnp.float32)
    inverse = lax.linalg.triangular_solve(lower, identity, left_side=True, lower=True)
    solved = lax.dot_general(
        matrix,
        inverse,
        (((1,), (1,)), ((), ())),
        precision=lax.Precision.HIGHEST,
        preferred_element_type=jnp.float32,
    )
    basis = (solved * scale).reshape(rows_lat, rows_lon, steps_out)
    return (basis, lower.T / scale)


def solution(mesh):
    placed = (P("lat", "lon", None), P(), P(), P())
    return jax.shard_map(
        body, mesh=mesh, in_specs=placed, out_specs=(P("lat", "lon", None), P()), check_vma=False
    )
```

profile of v0, /device:TPU:1, one launch (start us, length us, event | category | flops | bytes accessed | tf_op | source)
XLA Modules:
  0.0 376.2 jit_solution(6721393998767442552)
XLA Ops:
  7.2 0.7 fusion.22
  8.0 0.5 tile.30
  8.6 0.4 copy-done
  9.1 0.8 convolution_bitcast_fusion
  10.0 5.7 %collective-permute-start = (f32[20,20,256]{2,1,0:T(8,128)S(1)}, f32[20,20,256]{2,1,0:T(8,128)S(1)}, u32[]{:S(2)}, u32[]{:S(2)}) collective-permute-start(f32[20,20,256]{2,1,0:T(8,128)S(1)} %reshape.65), channel_id=1, source_target_pairs={{0,32},{32,64},{64,96},{96,128},{128,160},{160,192},{192,224},{1,3... | collective-permute-start | bytes 1228808 | tf_op jit(solution)/shard_map/ppermute | solution.py:17
  15.7 1.3 collective-permute-start.1
  17.3 18.7 %collective-permute-done = f32[20,20,256]{2,1,0:T(8,128)S(1)} collective-permute-done((f32[20,20,256]{2,1,0:T(8,128)S(1)}, f32[20,20,256]{2,1,0:T(8,128)S(1)}, u32[]{:S(2)}, u32[]{:S(2)}) %collective-permute-start) | collective-permute-done | bytes 409632 | tf_op jit(solution)/shard_map/ppermute | solution.py:17
  36.8 1.1 fusion.2
  37.9 3.1 collective-permute-start.2
  41.3 5.5 %collective-permute-done.2 = f32[20,20,256]{2,0,1:T(8,128)S(1)} collective-permute-done((f32[20,20,256]{2,0,1:T(8,128)S(1)}, f32[20,20,256]{2,0,1:T(8,128)S(1)}, u32[]{:S(2)}, u32[]{:S(2)}) %collective-permute-start.2) | collective-permute-done | bytes 409632 | tf_op jit(solution)/shard_map/ppermute | solution.py:17
  46.8 2.8 collective-permute-done.3
  49.7 1.2 fusion.7
  50.9 1.7 convolution_bitcast_fusion.1
  52.8 251.7 %all-reduce.6.cloned.1.call-done = f32[256,256]{0,1:T(8,128)} async-done(((f32[256,256]{0,1:T(8,128)}), f32[256,256]{0,1:T(8,128)}) %all-reduce.6.cloned.1.call-update) | async-done | bytes 262160 | tf_op jit(solution)/shard_map/psum | solution.py:81
  304.5 1.1 copy.13
  305.6 1.0 fusion.13
  306.6 11.7 %cholesky.50 = f32[128,128]{1,0:T(8,128)S(1)} custom-call(f32[128,128]{1,0:T(8,128)S(1)} %cholesky.118), custom_call_target="Cholesky" | custom-call | tf_op jit(solution)/shard_map/jit(cholesky)/cholesky | solution.py:82
  318.3 9.8 %custom-call.14 = f32[1,128,128]{1,2,0:T(8,128)S(1)} custom-call(f32[1,128,128]{2,1,0:T(8,128)S(1)} %get-tuple-element.29), custom_call_target="InvertDiagBlocksLowerTriangular" | custom-call | tf_op jit(solution)/shard_map/jit(cholesky)/cholesky | solution.py:82
  328.4 0.3 convolution_subtract_fusion.1
  328.6 11.9 %cholesky.105 = f32[128,128]{1,0:T(8,128)S(1)} custom-call(f32[128,128]{1,0:T(8,128)S(1)} %convolution_subtract_fusion.1), custom_call_target="Cholesky" | custom-call | tf_op jit(solution)/shard_map/jit(cholesky)/cholesky | solution.py:82
  340.6 0.7 compare_reduce_fusion
  342.7 4.0 %while.1 = (s32[]{:T(128)}, f32[256,256]{1,0:T(8,128)S(1)}, s32[2,2]{1,0:T(2,128)S(1)}, f32[2,128,128]{2,1,0:T(8,128)S(1)}, s32[]{:T(128)}) while((s32[]{:T(128)}, f32[256,256]{1,0:T(8,128)S(1)}, s32[2,2]{1,0:T(2,128)S(1)}, f32[2,128,128]{2,1,0:T(8,128)S(1)}, s32[]{:T(128)}) %tuple.30), condition=%wide.while_cond, body=%wide.while_body.sunk | while | flops 2 | bytes 131181 | solution.py:85
  342.7 0.6 fusion.37
  343.3 1.4 bitcast_dynamic-update-slice_fusion.2
  344.7 0.6 fusion.37
  345.3 1.4 bitcast_dynamic-update-slice_fusion.2
  346.7 19.7 %custom-call.15 = f32[2,128,128]{1,2,0:T(8,128)S(1)} custom-call(f32[2,128,128]{2,1,0:T(8,128)S(1)} %get-tuple-element.9), custom_call_target="InvertDiagBlocksLowerTriangular" | custom-call | tf_op jit(solution)/shard_map/triangular_solve | solution.py:85
  366.4 0.3 fusion.15
  366.9 0.3 fusion.18
  367.2 0.5 convolution_multiply_fusion
  367.7 0.8 reshape.68
  368.6 0.8 copy.14
  (46 shorter events, 2.5 us)
Async XLA Ops:
  7.2 297.3 %all-reduce.6.cloned.1.call-start = ((), (), s32[]{:S(2)}) async-start(), calls=%async_computation | async-start | bytes 524288 | tf_op jit(solution)/shard_map/psum | solution.py:81
  7.9 1.1 copy-start
  9.1 8.0 %copy-start.1 = (f32[41]{0:T(128)S(1)}, f32[41]{0:T(128)}, u32[]{:S(2)}) copy-start(f32[41]{0:T(128)} %param.5) | copy-start | bytes 496
  10.0 26.1 %collective-permute-start = (f32[20,20,256]{2,1,0:T(8,128)S(1)}, f32[20,20,256]{2,1,0:T(8,128)S(1)}, u32[]{:S(2)}, u32[]{:S(2)}) collective-permute-start(f32[20,20,256]{2,1,0:T(8,128)S(1)} %reshape.65), channel_id=1, source_target_pairs={{0,32},{32,64},{64,96},{96,128},{128,160},{160,192},{192,224},{1,3... | collective-permute-start | bytes 1228808 | tf_op jit(solution)/shard_map/ppermute | solution.py:17
  15.7 20.6 %collective-permute-start.1 = (f32[20,20,256]{2,1,0:T(8,128)S(1)}, f32[20,20,256]{2,1,0:T(8,128)S(1)}, u32[]{:S(2)}, u32[]{:S(2)}) collective-permute-start(f32[20,20,256]{2,1,0:T(8,128)S(1)} %reshape.65), channel_id=1, source_target_pairs={{32,0},{64,32},{96,64},{128,96},{160,128},{192,160},{224,192},{33,... | collective-permute-start | bytes 1228808 | tf_op jit(solution)/shard_map/ppermute | solution.py:18
  36.8 4.2 %copy-start.2 = (f32[41]{0:T(128)S(1)}, f32[41]{0:T(128)}, u32[]{:S(2)}) copy-start(f32[41]{0:T(128)} %param.6) | copy-start | bytes 496
  37.9 8.9 %collective-permute-start.2 = (f32[20,20,256]{2,0,1:T(8,128)S(1)}, f32[20,20,256]{2,0,1:T(8,128)S(1)}, u32[]{:S(2)}, u32[]{:S(2)}) collective-permute-start(f32[20,20,256]{2,0,1:T(8,128)S(1)} %fusion.2), channel_id=1, source_target_pairs={{0,1},{1,2},{2,3},{3,4},{4,5},{5,6},{6,7},{7,8},{8,9},{9,10},{10,1... | collective-permute-start | bytes 1228808 | tf_op jit(solution)/shard_map/ppermute | solution.py:17
  41.0 8.6 %collective-permute-start.3 = (f32[20,20,256]{2,0,1:T(8,128)S(1)}, f32[20,20,256]{2,0,1:T(8,128)S(1)}, u32[]{:S(2)}, u32[]{:S(2)}) collective-permute-start(f32[20,20,256]{2,0,1:T(8,128)S(1)} %fusion.2), channel_id=1, source_target_pairs={{1,0},{2,1},{3,2},{4,3},{5,4},{6,5},{7,6},{8,7},{9,8},{10,9},{11,1... | collective-permute-start | bytes 1228808 | tf_op jit(solution)/shard_map/ppermute | solution.py:18
Sparse Core Ops, SparseCore 0:
  52.8 251.6 all-reduce.5
where the time goes:
time: 377 us; the launch traced here: 376 us
  waiting for transfers between devices  279 us (74%)
  other arithmetic  55.9 us (15%)
  between operations  15.7 us (4%)
  starting transfers between devices  10.2 us (3%)
  local copies, waits for them, and re-layouts  9.1 us (2%)
  matrix products  6.64 us (2%)
    psum x1, waiting for transfers between devices, body(): gram = lax.psum(local_gram, ('lat', 'lon'))  252 us
    another operation x6, other arithmetic, body(): lower = jnp.linalg.cholesky(gram)  34.2 us
    ppermute x2, waiting for transfers between devices, extended_2(): before = lax.ppermute(last, axis, up)  24.2 us
    another operation x2, other arithmetic, body(): lax.linalg.triangular_solve(lower, identity, left_side=True, lower=True)  19.7 us
    ppermute x2, starting transfers between devices, extended_2(): before = lax.ppermute(last, axis, up)  8.82 us
  transfers between devices with their start and end apart: 5, of which 4 were waited for; matrix products, arithmetic and copies ran while one was open for 0% of the time, Pallas kernels for 0%

commit v1 on v0

--- a/solution.py
+++ b/solution.py
@@ -5,6 +5,8 @@
 
 TH = 64
 SH = 20
+LAT = ("x", "yh")
+LON = ("yl", "z", "core")
 
 
 def extended_2(value, sides, width, wrap):
@@ -39,12 +41,39 @@
     return result.reshape(band.shape[0], cols_in, hours)
 
 
+PLANE = ("x", "yh", "yl")
+
+
+def shared(value, axes):
+    peers = lax.axis_size(axes)
+    copies = jnp.broadcast_to(value[None], (peers,) + value.shape)
+    return lax.all_to_all(copies, axes, 0, 0)
+
+
+def summed(value):
+    swap = [(0, 1), (1, 0)]
+    core = lax.axis_index("core")
+    rows, cols = value.shape
+    half = rows // 2
+    kept = lax.dynamic_slice_in_dim(value, core * half, half, 0)
+    given = lax.dynamic_slice_in_dim(value, (1 - core) * half, half, 0)
+    kept = kept + lax.ppermute(given, "core", swap)
+    peers = lax.axis_size(PLANE)
+    pieces = lax.all_to_all(kept.reshape(peers, half // peers, cols), PLANE, 0, 0)
+    piece = shared(pieces.sum(axis=0), ("z",)).sum(axis=0)
+    kept = shared(piece, PLANE).reshape(half, cols)
+    given = lax.ppermute(kept, "core", swap)
+    top = jnp.where(core == 0, kept, given)
+    bottom = jnp.where(core == 0, given, kept)
+    return jnp.concatenate([top, bottom], axis=0)
+
+
 def body(field, lat_kernel, lon_kernel, time_taps):
     rows_lat, rows_lon, length_in = field.shape
     steps_out = length_in - 2 * TH
-    lat_place = lax.axis_index("lat")
-    total_lat = rows_lat * lax.axis_size("lat")
-    cells = total_lat * rows_lon * lax.axis_size("lon")
+    lat_place = lax.axis_index(LAT)
+    total_lat = rows_lat * lax.axis_size(LAT)
+    cells = total_lat * rows_lon * lax.axis_size(LON)
     centre = (jnp.arange(2 * TH + 1, dtype=jnp.int32) == TH).astype(jnp.float32)
     taps_full = time_taps + centre
     skew_time = skewed(taps_full, steps_out, length_in)
@@ -57,9 +86,9 @@
     ).reshape(rows_lat, rows_lon, steps_out)
     lat_band = banded(lat_kernel, rows_lat)
     lon_band = banded(lon_kernel, rows_lon)
-    extended = extended_2(filtered, (("lat", 0),), SH, False)
+    extended = extended_2(filtered, ((LAT, 0),), SH, False)
     narrow = smooth_rows(lat_band, extended)
-    lat_done = extended_2(narrow, (("lon", 1),), SH, True)
+    lat_done = extended_2(narrow, ((LON, 1),), SH, True)
     smooth = jnp.einsum(
         "jk,ikt->ijt",
         lon_band,
@@ -78,7 +107,7 @@
         precision=lax.Precision.HIGHEST,
         preferred_element_type=jnp.float32,
     )
-    gram = lax.psum(local_gram, ("lat", "lon"))
+    gram = summed(local_gram)
     lower = jnp.linalg.cholesky(gram)
     scale = jnp.sqrt(jnp.float32(cells))
     identity = jnp.eye(steps_out, dtype=jnp.float32)
@@ -95,7 +124,8 @@
 
 
 def solution(mesh):
-    placed = (P("lat", "lon", None), P(), P(), P())
+    fine = jax.sharding.Mesh(mesh.devices.reshape(4, 2, 2, 8, 2), ("x", "yh", "yl", "z", "core"))
+    placed = (P(LAT, LON, None), P(), P(), P())
     return jax.shard_map(
-        body, mesh=mesh, in_specs=placed, out_specs=(P("lat", "lon", None), P()), check_vma=False
+        body, mesh=fine, in_specs=placed, out_specs=(P(LAT, LON, None), P()), check_vma=False
     )

time: 377 us -> 155 us (0.41)
  waiting for transfers between devices: 279 us -> 28.9 us
  blocking collectives: 0 us -> 38.3 us
  between operations: 15.7 us -> 2.39 us
  starting transfers between devices: 10.2 us -> 15.6 us
    psum x1 -> x0, waiting for transfers between devices: 252 us -> none  [body(): gram = lax.psum(local_gram, ('lat', 'lon'))]
    all_to_all x0 -> x3, blocking collectives: none -> 38.3 us  [the longest x2 23.7 us: shared(): return lax.all_to_all(copies, axes, 0, 0)]
    ppermute x0 -> x2, starting transfers between devices: none -> 5.49 us  [the longest x1 4.42 us: summed(): given = lax.ppermute(kept, 'core', swap)]
  transfers between devices with their start and end apart: 5 -> 6, of which waited for: 4 -> 5; matrix products, arithmetic and copies ran while one was open for 0% -> 1% of each run, Pallas kernels for 0% -> 0%
where the time goes in v1:
time: 155 us
  other arithmetic  54.8 us (35%)
  blocking collectives  38.3 us (25%)
  waiting for transfers between devices  28.9 us (19%)
  starting transfers between devices  15.6 us (10%)
  local copies, waits for them, and re-layouts  8.41 us (5%)
  matrix products  5.95 us (4%)
  between operations  2.39 us (2%)
    another operation x6, other arithmetic, body(): lower = jnp.linalg.cholesky(gram)  34 us
    ppermute x2, waiting for transfers between devices, extended_2(): before = lax.ppermute(last, axis, up)  24.2 us
    all_to_all x2, blocking collectives, shared(): return lax.all_to_all(copies, axes, 0, 0)  23.7 us
    another operation x2, other arithmetic, body(): lax.linalg.triangular_solve(lower, identity, left_side=True, lower=True)  19.7 us
    all_to_all x1, blocking collectives, summed(): lax.all_to_all(kept.reshape(peers, half // peers, cols), PLANE, 0, 0)  14.6 us
    ppermute x2, starting transfers between devices, extended_2(): before = lax.ppermute(last, axis, up)  8.82 us
    ppermute x1, starting transfers between devices, summed(): given = lax.ppermute(kept, 'core', swap)  4.42 us
    another operation x6, local copies, waits for them, and re-layouts  4.06 us
  transfers between devices with their start and end apart: 6, of which 5 were waited for; matrix products, arithmetic and copies ran while one was open for 1% of the time, Pallas kernels for 0%

profile of v1, /device:TPU:1, one launch (start us, length us, event | category | flops | bytes accessed | tf_op | source)
XLA Modules:
  0.0 154.6 jit_solution(18271428235321330749)
XLA Ops:
  0.6 0.7 fusion.22
  1.4 0.5 tile.30
  2.5 0.8 convolution_bitcast_fusion
  3.4 5.7 %collective-permute-start = (f32[20,20,256]{2,1,0:T(8,128)S(1)}, f32[20,20,256]{2,1,0:T(8,128)S(1)}, u32[]{:S(2)}, u32[]{:S(2)}) collective-permute-start(f32[20,20,256]{2,1,0:T(8,128)S(1)} %reshape.73), channel_id=1, source_target_pairs={{0,32},{32,64},{64,96},{96,128},{128,160},{160,192},{192,224},{1,3... | collective-permute-start | bytes 1228808 | tf_op jit(solution)/shard_map/ppermute | solution.py:19
  9.1 1.3 collective-permute-start.1
  10.7 18.7 %collective-permute-done = f32[20,20,256]{2,1,0:T(8,128)S(1)} collective-permute-done((f32[20,20,256]{2,1,0:T(8,128)S(1)}, f32[20,20,256]{2,1,0:T(8,128)S(1)}, u32[]{:S(2)}, u32[]{:S(2)}) %collective-permute-start) | collective-permute-done | bytes 409632 | tf_op jit(solution)/shard_map/ppermute | solution.py:19
  30.2 1.1 fusion.2
  31.3 3.1 %collective-permute-start.2 = (f32[20,20,256]{2,0,1:T(8,128)S(1)}, f32[20,20,256]{2,0,1:T(8,128)S(1)}, u32[]{:S(2)}, u32[]{:S(2)}) collective-permute-start(f32[20,20,256]{2,0,1:T(8,128)S(1)} %fusion.2), channel_id=1, source_target_pairs={{0,1},{1,2},{2,3},{3,4},{4,5},{5,6},{6,7},{7,8},{8,9},{9,10},{10,1... | collective-permute-start | bytes 1228808 | tf_op jit(solution)/shard_map/ppermute | solution.py:19
  34.7 5.5 %collective-permute-done.2 = f32[20,20,256]{2,0,1:T(8,128)S(1)} collective-permute-done((f32[20,20,256]{2,0,1:T(8,128)S(1)}, f32[20,20,256]{2,0,1:T(8,128)S(1)}, u32[]{:S(2)}, u32[]{:S(2)}) %collective-permute-start.2) | collective-permute-done | bytes 409632 | tf_op jit(solution)/shard_map/ppermute | solution.py:19
  40.2 2.8 %collective-permute-done.3 = f32[20,20,256]{2,0,1:T(8,128)S(1)} collective-permute-done((f32[20,20,256]{2,0,1:T(8,128)S(1)}, f32[20,20,256]{2,0,1:T(8,128)S(1)}, u32[]{:S(2)}, u32[]{:S(2)}) %collective-permute-start.3) | collective-permute-done | bytes 409632 | tf_op jit(solution)/shard_map/ppermute | solution.py:20
  43.1 1.2 fusion.7
  44.3 1.0 convolution_bitcast_fusion.1
  45.4 1.1 collective-permute-start.4
  46.4 1.0 collective-permute-done.4
  47.5 14.6 %all_to_all.15 = f32[16,8,256]{2,1,0:T(8,128)S(1)} all-to-all(f32[16,8,256]{2,1,0:T(8,128)S(1)} %add_bitcast_fusion), channel_id=1, replica_groups=mesh['x'=4,'yh'=2,'yl'=2,'z'=8,'core'=2] {'x','yh','yl'}, dimensions={0} | all-to-all | bytes 262144 | tf_op jit(solution)/shard_map/all_to_all | solution.py:62
  62.1 13.7 %all_to_all.16 = f32[8,8,256]{2,1,0:T(8,128)S(1)} all-to-all(f32[8,8,256]{2,1,0:T(8,128)S(1)} %broadcast_in_dim.5), channel_id=1, replica_groups=mesh['x'=4,'yh'=2,'yl'=2,'z'=8,'core'=2] {'z'}, dimensions={0} | all-to-all | bytes 131072 | tf_op jit(solution)/shard_map/all_to_all | solution.py:50
  75.9 9.9 %all_to_all.17 = f32[16,8,256]{2,1,0:T(8,128)S(1)} all-to-all(f32[16,8,256]{2,1,0:T(8,128)S(1)} %broadcast_in_dim.6), channel_id=1, replica_groups=mesh['x'=4,'yh'=2,'yl'=2,'z'=8,'core'=2] {'x','yh','yl'}, dimensions={0} | all-to-all | bytes 262144 | tf_op jit(solution)/shard_map/all_to_all | solution.py:50
  85.9 4.4 %collective-permute-start.5 = (f32[128,256]{0,1:T(8,128)S(1)}, f32[128,256]{0,1:T(8,128)S(1)}, u32[]{:S(2)}, u32[]{:S(2)}) collective-permute-start(f32[128,256]{0,1:T(8,128)S(1)} %copy.19), channel_id=1, source_target_pairs={{0,1},{1,0},{2,3},{3,2},{4,5},{5,4},{6,7},{7,6},{8,9},{9,8},{10,11... | collective-permute-start | bytes 393224 | tf_op jit(solution)/shard_map/ppermute | solution.py:65
  90.4 0.9 collective-permute-done.5
  91.6 11.7 %cholesky.50 = f32[128,128]{1,0:T(8,128)S(1)} custom-call(f32[128,128]{1,0:T(8,128)S(1)} %cholesky.118), custom_call_target="Cholesky" | custom-call | tf_op jit(solution)/shard_map/jit(cholesky)/cholesky | solution.py:111
  103.3 9.8 %custom-call.14 = f32[1,128,128]{1,2,0:T(8,128)S(1)} custom-call(f32[1,128,128]{2,1,0:T(8,128)S(1)} %get-tuple-element.33), custom_call_target="InvertDiagBlocksLowerTriangular" | custom-call | tf_op jit(solution)/shard_map/jit(cholesky)/cholesky | solution.py:111
  113.6 11.7 %cholesky.105 = f32[128,128]{1,0:T(8,128)S(1)} custom-call(f32[128,128]{1,0:T(8,128)S(1)} %convolution_subtract_fusion.1), custom_call_target="Cholesky" | custom-call | tf_op jit(solution)/shard_map/jit(cholesky)/cholesky | solution.py:111
  125.4 0.7 compare_reduce_fusion
  127.6 4.3 %while.1 = (s32[]{:T(128)}, f32[256,256]{1,0:T(8,128)S(1)}, s32[2,2]{1,0:T(2,128)S(1)}, f32[2,128,128]{2,1,0:T(8,128)S(1)}, s32[]{:T(128)}) while((s32[]{:T(128)}, f32[256,256]{1,0:T(8,128)S(1)}, s32[2,2]{1,0:T(2,128)S(1)}, f32[2,128,128]{2,1,0:T(8,128)S(1)}, s32[]{:T(128)}) %tuple.32), condition=%wide.while_cond, body=%wide.while_body.sunk | while | flops 2 | bytes 131181 | solution.py:114
  127.8 0.6 fusion.37
  128.4 1.4 bitcast_dynamic-update-slice_fusion.2
  129.8 0.6 fusion.37
  130.4 1.4 bitcast_dynamic-update-slice_fusion.2
  131.9 19.7 %custom-call.15 = f32[2,128,128]{1,2,0:T(8,128)S(1)} custom-call(f32[2,128,128]{2,1,0:T(8,128)S(1)} %get-tuple-element.9), custom_call_target="InvertDiagBlocksLowerTriangular" | custom-call | tf_op jit(solution)/shard_map/triangular_solve | solution.py:114
  152.4 0.5 convolution_multiply_fusion
  152.9 0.8 reshape.78
  153.8 0.8 copy.22
  (59 shorter events, 4.0 us)
Async XLA Ops:
  1.3 1.1 copy-start
  2.5 8.0 %copy-start.1 = (f32[41]{0:T(128)S(1)}, f32[41]{0:T(128)}, u32[]{:S(2)}) copy-start(f32[41]{0:T(128)} %param.5) | copy-start | bytes 496
  3.4 26.1 %collective-permute-start = (f32[20,20,256]{2,1,0:T(8,128)S(1)}, f32[20,20,256]{2,1,0:T(8,128)S(1)}, u32[]{:S(2)}, u32[]{:S(2)}) collective-permute-start(f32[20,20,256]{2,1,0:T(8,128)S(1)} %reshape.73), channel_id=1, source_target_pairs={{0,32},{32,64},{64,96},{96,128},{128,160},{160,192},{192,224},{1,3... | collective-permute-start | bytes 1228808 | tf_op jit(solution)/shard_map/ppermute | solution.py:19
  9.1 20.6 %collective-permute-start.1 = (f32[20,20,256]{2,1,0:T(8,128)S(1)}, f32[20,20,256]{2,1,0:T(8,128)S(1)}, u32[]{:S(2)}, u32[]{:S(2)}) collective-permute-start(f32[20,20,256]{2,1,0:T(8,128)S(1)} %reshape.73), channel_id=1, source_target_pairs={{32,0},{64,32},{96,64},{128,96},{160,128},{192,160},{224,192},{33,... | collective-permute-start | bytes 1228808 | tf_op jit(solution)/shard_map/ppermute | solution.py:20
  30.2 4.2 %copy-start.2 = (f32[41]{0:T(128)S(1)}, f32[41]{0:T(128)}, u32[]{:S(2)}) copy-start(f32[41]{0:T(128)} %param.6) | copy-start | bytes 496
  31.3 8.9 %collective-permute-start.2 = (f32[20,20,256]{2,0,1:T(8,128)S(1)}, f32[20,20,256]{2,0,1:T(8,128)S(1)}, u32[]{:S(2)}, u32[]{:S(2)}) collective-permute-start(f32[20,20,256]{2,0,1:T(8,128)S(1)} %fusion.2), channel_id=1, source_target_pairs={{0,1},{1,2},{2,3},{3,4},{4,5},{5,6},{6,7},{7,8},{8,9},{9,10},{10,1... | collective-permute-start | bytes 1228808 | tf_op jit(solution)/shard_map/ppermute | solution.py:19
  34.4 8.6 %collective-permute-start.3 = (f32[20,20,256]{2,0,1:T(8,128)S(1)}, f32[20,20,256]{2,0,1:T(8,128)S(1)}, u32[]{:S(2)}, u32[]{:S(2)}) collective-permute-start(f32[20,20,256]{2,0,1:T(8,128)S(1)} %fusion.2), channel_id=1, source_target_pairs={{1,0},{2,1},{3,2},{4,3},{5,4},{6,5},{7,6},{8,7},{9,8},{10,9},{11,1... | collective-permute-start | bytes 1228808 | tf_op jit(solution)/shard_map/ppermute | solution.py:20
  45.4 2.1 %collective-permute-start.4 = (f32[128,256]{1,0:T(8,128)S(1)}, f32[128,256]{1,0:T(8,128)S(1)}, u32[]{:S(2)}, u32[]{:S(2)}) collective-permute-start(f32[128,256]{1,0:T(8,128)S(1)} %constant_dynamic-slice_fusion.1), channel_id=1, source_target_pairs={{0,1},{1,0},{2,3},{3,2},{4,5},{5,4},{6,7},{7,6},{8,9},{9,8},{10,11... | collective-permute-start | bytes 393224 | tf_op jit(solution)/shard_map/ppermute | solution.py:60
  85.9 5.4 %collective-permute-start.5 = (f32[128,256]{0,1:T(8,128)S(1)}, f32[128,256]{0,1:T(8,128)S(1)}, u32[]{:S(2)}, u32[]{:S(2)}) collective-permute-start(f32[128,256]{0,1:T(8,128)S(1)} %copy.19), channel_id=1, source_target_pairs={{0,1},{1,0},{2,3},{3,2},{4,5},{5,4},{6,7},{7,6},{8,9},{9,8},{10,11... | collective-permute-start | bytes 393224 | tf_op jit(solution)/shard_map/ppermute | solution.py:65

commit v2 on v1

--- a/solution.py
+++ b/solution.py
@@ -1,6 +1,10 @@
+import functools
+
 import jax
 import jax.numpy as jnp
 from jax import lax
+from jax.experimental import pallas as pl
+from jax.experimental.pallas import tpu as pltpu
 from jax.sharding import PartitionSpec as P
 
 TH = 64
@@ -68,6 +72,100 @@
     return jnp.concatenate([top, bottom], axis=0)
 
 
+TILE = 128
+STEP = 8
+
+def product(left, right, over):
+    return lax.dot_general(
+        left,
+        right,
+        (over, ((), ())),
+        precision=lax.Precision.HIGHEST,
+        preferred_element_type=jnp.float32,
+    )
+
+
+def wide(value):
+    return jnp.broadcast_to(value, (STEP, TILE))
+
+
+def eliminate(work):
+    for top in range(0, TILE, STEP):
+        own = work[top:top + STEP, :TILE]
+        cols = [wide(own[:, top + j:top + j + 1]) for j in range(STEP)]
+        left = {(i, j): wide(cols[j][i:i + 1, :]) for j in range(STEP) for i in range(j + 1)}
+        rows = [[wide(work[top + i:top + i + 1, s:s + TILE]) for s in (0, TILE)] for i in range(STEP)]
+        root, upper = [], {}
+        for j in range(STEP):
+            root.append(lax.rsqrt(left[j, j]))
+            for i in range(j + 1, STEP):
+                upper[j, i] = left[j, i] * root[j]
+            for i in range(j + 1, STEP):
+                for n in range(i, STEP):
+                    left[i, n] = left[i, n] - upper[j, i] * upper[j, n]
+        for j in range(STEP):
+            rows[j] = [value * root[j] for value in rows[j]]
+            for i in range(j + 1, STEP):
+                rows[i] = [value - upper[j, i] * done for value, done in zip(rows[i], rows[j])]
+        for j in range(STEP):
+            for half in range(2):
+                work[top + j:top + j + 1, half * TILE:(half + 1) * TILE] = rows[j][half][:1, :]
+        for below in range(top + STEP, TILE, STEP):
+            parts = [work[below:below + STEP, s:s + TILE] for s in (0, TILE)]
+            factors = [wide(parts[0][:, top + j:top + j + 1]) for j in range(STEP)]
+            for j in range(STEP):
+                factors[j] = factors[j] * root[j]
+                for i in range(j + 1, STEP):
+                    factors[i] = factors[i] - upper[j, i] * factors[j]
+            for j in range(STEP):
+                parts = [value - factors[j] * done for value, done in zip(parts, rows[j])]
+            for half in range(2):
+                work[below:below + STEP, half * TILE:(half + 1) * TILE] = parts[half]
+
+
+ROWS = ((0,), (0,))
+COLS = ((1,), (1,))
+PLAIN = ((1,), (0,))
+
+
+def factor_kernel(cells, gram, matrix, basis, merged, work):
+    row = lax.broadcasted_iota(jnp.int32, (TILE, TILE), 0)
+    col = lax.broadcasted_iota(jnp.int32, (TILE, TILE), 1)
+    eye = jnp.where(row == col, 1.0, 0.0).astype(jnp.float32)
+    scale = float(cells) ** 0.5
+
+    def solve(block):
+        work[:, :TILE] = block
+        work[:, TILE:] = eye
+        eliminate(work)
+        upper = jnp.where(row <= col, work[:, :TILE], 0.0)
+        lower = jnp.where(row >= col, work[:, TILE:], 0.0)
+        return upper, lower
+
+    r11, w11 = solve(gram[:TILE, :TILE])
+    r12 = product(w11, gram[:TILE, TILE:], PLAIN)
+    r22, w22 = solve(gram[TILE:, TILE:] - product(r12, r12, ROWS))
+    w21 = -product(w22, product(r12, w11, ROWS), PLAIN)
+    merged[:TILE, :TILE] = r11 * (1.0 / scale)
+    merged[:TILE, TILE:] = r12 * (1.0 / scale)
+    merged[TILE:, :TILE] = jnp.zeros((TILE, TILE), jnp.float32)
+    merged[TILE:, TILE:] = r22 * (1.0 / scale)
+    first, second = (matrix[:, :TILE], matrix[:, TILE:])
+    basis[:, :TILE] = product(first, w11 * scale, COLS)
+    basis[:, TILE:] = product(first, w21 * scale, COLS) + product(second, w22 * scale, COLS)
+
+
+def factored(gram, matrix, cells):
+    like = jax.ShapeDtypeStruct
+    return pl.pallas_call(
+        functools.partial(factor_kernel, cells),
+        out_shape=(like(matrix.shape, jnp.float32), like(gram.shape, jnp.float32)),
+        scratch_shapes=[pltpu.VMEM((TILE, 2 * TILE), jnp.float32)],
+        compiler_params=pltpu.CompilerParams(vmem_limit_bytes=32 * 1024 * 1024),
+        name="factor",
+    )(gram, matrix)
+
+
 def body(field, lat_kernel, lon_kernel, time_taps):
     rows_lat, rows_lon, length_in = field.shape
     steps_out = length_in - 2 * TH
@@ -108,19 +206,8 @@
         preferred_element_type=jnp.float32,
     )
     gram = summed(local_gram)
-    lower = jnp.linalg.cholesky(gram)
-    scale = jnp.sqrt(jnp.float32(cells))
-    identity = jnp.eye(steps_out, dtype=jnp.float32)
-    inverse = lax.linalg.triangular_solve(lower, identity, left_side=True, lower=True)
-    solved = lax.dot_general(
-        matrix,
-        inverse,
-        (((1,), (1,)), ((), ())),
-        precision=lax.Precision.HIGHEST,
-        preferred_element_type=jnp.float32,
-    )
-    basis = (solved * scale).reshape(rows_lat, rows_lon, steps_out)
-    return (basis, lower.T / scale)
+    basis, merged = factored(gram, matrix, cells)
+    return (basis.reshape(rows_lat, rows_lon, steps_out), merged)
 
 
 def solution(mesh):

time: 155 us -> 104 us (0.67)
  other arithmetic: 54.8 us -> 1.07 us
  Pallas kernels: 0 us -> 10.7 us
  local copies, waits for them, and re-layouts: 8.41 us -> 3.2 us
  matrix products: 5.95 us -> 4.12 us
    another operation x8 -> x0, other arithmetic: 53.7 us -> none  [the longest x6 34 us: body(): lower = jnp.linalg.cholesky(gram)]
    pallas_call x0 -> x1, Pallas kernels: none -> 10.7 us  [factored(): pl.pallas_call(functools.partial(factor_kernel, cells), out_shape=(like(m...]
    ppermute x2, waiting for transfers between devices: 2.78 us -> 9.26 us  [extended_2(): after = lax.ppermute(initial, axis, down)]
    ppermute x2, waiting for transfers between devices: 24.2 us -> 18.9 us  [extended_2(): before = lax.ppermute(last, axis, up)]
    another operation x9 -> x0, local copies, waits for them, and re-layouts: 4.15 us -> none
  transfers between devices with their start and end apart: 6 -> 6, of which waited for: 5 -> 6; matrix products, arithmetic and copies ran while one was open for 1% -> 1% of each run, Pallas kernels for 0% -> 0%
where the time goes in v2:
time: 104 us; the launch traced here: 103 us
  blocking collectives  37.2 us (36%)
  waiting for transfers between devices  30 us (29%)
  starting transfers between devices  16 us (15%)
  Pallas kernels  10.7 us (10%)
  matrix products  4.12 us (4%)
  local copies, waits for them, and re-layouts  3.2 us (3%)
  other arithmetic  1.07 us (1%)
    all_to_all x2, blocking collectives, shared(): return lax.all_to_all(copies, axes, 0, 0)  22.6 us
    ppermute x2, waiting for transfers between devices, extended_2(): before = lax.ppermute(last, axis, up)  18.9 us
    all_to_all x1, blocking collectives, summed(): lax.all_to_all(kept.reshape(peers, half // peers, cols), PLANE, 0, 0)  14.6 us
    pallas_call x1, Pallas kernels, factored(): pl.pallas_call(functools.partial(factor_kernel, cells), out_shape=(like(m...  10.7 us
    ppermute x2, waiting for transfers between devices, extended_2(): after = lax.ppermute(initial, axis, down)  9.26 us
    ppermute x2, starting transfers between devices, extended_2(): before = lax.ppermute(last, axis, up)  8.4 us
    ppermute x1, starting transfers between devices, summed(): given = lax.ppermute(kept, 'core', swap)  4.16 us
    ppermute x1, starting transfers between devices, summed(): kept = kept + lax.ppermute(given, 'core', swap)  2.12 us
  transfers between devices with their start and end apart: 6, of which 6 were waited for; matrix products, arithmetic and copies ran while one was open for 1% of the time, Pallas kernels for 0%

profile of v2, /device:TPU:1, one launch (start us, length us, event | category | flops | bytes accessed | tf_op | source)
XLA Modules:
  0.0 103.2 jit_solution(10556952712457403576)
XLA Ops:
  0.6 0.7 fusion.10
  1.4 0.5 tile.30
  1.9 0.1 reshape.54
  2.0 0.4 copy-done
  2.5 0.8 convolution_bitcast_fusion
  3.4 1.3 %collective-permute-start.1 = (f32[20,20,256]{2,1,0:T(8,128)S(1)}, f32[20,20,256]{2,1,0:T(8,128)S(1)}, u32[]{:S(2)}, u32[]{:S(2)}) collective-permute-start(f32[20,20,256]{2,1,0:T(8,128)S(1)} %reshape.56), channel_id=1, source_target_pairs={{32,0},{64,32},{96,64},{128,96},{160,128},{192,160},{224,192},{33,... | collective-permute-start | bytes 1228808 | tf_op jit(solution)/shard_map/ppermute | solution.py:24
  4.7 6.3 %collective-permute-start = (f32[20,20,256]{2,1,0:T(8,128)S(1)}, f32[20,20,256]{2,1,0:T(8,128)S(1)}, u32[]{:S(2)}, u32[]{:S(2)}) collective-permute-start(f32[20,20,256]{2,1,0:T(8,128)S(1)} %reshape.56), channel_id=1, source_target_pairs={{0,32},{32,64},{64,96},{96,128},{128,160},{160,192},{192,224},{1,3... | collective-permute-start | bytes 1228808 | tf_op jit(solution)/shard_map/ppermute | solution.py:23
  11.0 0.1 concatenate.17
  11.3 0.1 reshape.62
  11.3 6.5 %collective-permute-done.1 = f32[20,20,256]{2,1,0:T(8,128)S(1)} collective-permute-done((f32[20,20,256]{2,1,0:T(8,128)S(1)}, f32[20,20,256]{2,1,0:T(8,128)S(1)}, u32[]{:S(2)}, u32[]{:S(2)}) %collective-permute-start.1) | collective-permute-done | bytes 409632 | tf_op jit(solution)/shard_map/ppermute | solution.py:24
  17.9 0.2 copy.12
  18.0 13.4 %collective-permute-done = f32[20,20,256]{2,1,0:T(8,128)S(1)} collective-permute-done((f32[20,20,256]{2,1,0:T(8,128)S(1)}, f32[20,20,256]{2,1,0:T(8,128)S(1)}, u32[]{:S(2)}, u32[]{:S(2)}) %collective-permute-start) | collective-permute-done | bytes 409632 | tf_op jit(solution)/shard_map/ppermute | solution.py:23
  31.4 0.2 copy.11
  31.6 0.2 maximum_bitcast_fusion
  31.8 0.2 dot_general.21
  32.0 1.1 %fusion.2 = f32[20,20,256]{2,0,1:T(8,128)S(1)} fusion(f32[20,60,1]{1,0,2:T(8,128)S(1)} %reshape.62, f32[20,256,60]{1,0,2:T(8,128)S(1)} %dot_general.21), kind=kOutput, calls=%fused_computation.4 | convolution fusion | flops 73728000 | bytes 1643200 | tf_op jit(solution)/shard_map/dot_general | solution.py:42
  33.1 2.1 %collective-permute-start.2 = (f32[20,20,256]{2,0,1:T(8,128)S(1)}, f32[20,20,256]{2,0,1:T(8,128)S(1)}, u32[]{:S(2)}, u32[]{:S(2)}) collective-permute-start(f32[20,20,256]{2,0,1:T(8,128)S(1)} %fusion.2), channel_id=1, source_target_pairs={{0,1},{1,2},{2,3},{3,4},{4,5},{5,6},{6,7},{7,8},{8,9},{9,10},{10,1... | collective-permute-start | bytes 1228808 | tf_op jit(solution)/shard_map/ppermute | solution.py:23
  35.3 0.1 reshape.63
  35.4 5.5 %collective-permute-done.2 = f32[20,20,256]{2,0,1:T(8,128)S(1)} collective-permute-done((f32[20,20,256]{2,0,1:T(8,128)S(1)}, f32[20,20,256]{2,0,1:T(8,128)S(1)}, u32[]{:S(2)}, u32[]{:S(2)}) %collective-permute-start.2) | collective-permute-done | bytes 409632 | tf_op jit(solution)/shard_map/ppermute | solution.py:23
  40.9 2.8 %collective-permute-done.3 = f32[20,20,256]{2,0,1:T(8,128)S(1)} collective-permute-done((f32[20,20,256]{2,0,1:T(8,128)S(1)}, f32[20,20,256]{2,0,1:T(8,128)S(1)}, u32[]{:S(2)}, u32[]{:S(2)}) %collective-permute-start.3) | collective-permute-done | bytes 409632 | tf_op jit(solution)/shard_map/ppermute | solution.py:24
  43.7 0.1 pad_maximum_fusion
  43.8 1.2 %fusion.7 = f32[20,20,256]{2,1,0:T(8,128)S(1)} fusion(f32[20,60,1]{1,0,2:T(8,128)S(1)} %reshape.63, f32[20,60,256]{2,0,1:T(8,128)S(1)} %pad_maximum_fusion, f32[20]{0:T(128)S(1)} %cosine_sqrt_fusion), kind=kOutput, calls=%fused_computation.7 | convolution fusion | flops 73830400 | bytes 1643280 | tf_op jit(solution)/shard_map/jk,ikt->ijt/dot_general | solution.py:190
  45.0 1.0 convolution_bitcast_fusion.1
  46.1 2.1 %collective-permute-start.4 = (f32[128,256]{1,0:T(8,128)S(1)}, f32[128,256]{1,0:T(8,128)S(1)}, u32[]{:S(2)}, u32[]{:S(2)}) collective-permute-start(f32[128,256]{1,0:T(8,128)S(1)} %constant_dynamic-slice_fusion), channel_id=1, source_target_pairs={{0,1},{1,0},{2,3},{3,2},{4,5},{5,4},{6,7},{7,6},{8,9},{9,8},{10,11... | collective-permute-start | bytes 393224 | tf_op jit(solution)/shard_map/ppermute | solution.py:64
  48.2 1.0 collective-permute-done.4
  49.2 14.6 %all_to_all.15 = f32[16,8,256]{2,1,0:T(8,128)S(1)} all-to-all(f32[16,8,256]{2,1,0:T(8,128)S(1)} %add_bitcast_fusion), channel_id=1, replica_groups=mesh['x'=4,'yh'=2,'yl'=2,'z'=8,'core'=2] {'x','yh','yl'}, dimensions={0} | all-to-all | bytes 262144 | tf_op jit(solution)/shard_map/all_to_all | solution.py:66
  63.9 12.7 %all_to_all.16 = f32[8,8,256]{2,1,0:T(8,128)S(1)} all-to-all(f32[8,8,256]{2,1,0:T(8,128)S(1)} %broadcast_in_dim.4), channel_id=1, replica_groups=mesh['x'=4,'yh'=2,'yl'=2,'z'=8,'core'=2] {'z'}, dimensions={0} | all-to-all | bytes 131072 | tf_op jit(solution)/shard_map/all_to_all | solution.py:54
  76.6 9.9 %all_to_all.17 = f32[16,8,256]{2,1,0:T(8,128)S(1)} all-to-all(f32[16,8,256]{2,1,0:T(8,128)S(1)} %broadcast_in_dim.5), channel_id=1, replica_groups=mesh['x'=4,'yh'=2,'yl'=2,'z'=8,'core'=2] {'x','yh','yl'}, dimensions={0} | all-to-all | bytes 262144 | tf_op jit(solution)/shard_map/all_to_all | solution.py:54
  86.5 4.2 %collective-permute-start.5 = (f32[128,256]{1,0:T(8,128)S(1)}, f32[128,256]{1,0:T(8,128)S(1)}, u32[]{:S(2)}, u32[]{:S(2)}) collective-permute-start(f32[128,256]{1,0:T(8,128)S(1)} %bitcast.33), channel_id=1, source_target_pairs={{0,1},{1,0},{2,3},{3,2},{4,5},{5,4},{6,7},{7,6},{8,9},{9,8},{10,11... | collective-permute-start | bytes 393224 | tf_op jit(solution)/shard_map/ppermute | solution.py:69
  90.7 0.9 collective-permute-done.5
  91.7 10.7 %factor.1 = (f32[400,256]{1,0:T(8,128)S(1)}, f32[256,256]{1,0:T(8,128)}) custom-call(f32[256,256]{1,0:T(8,128)S(1)} %pad_maximum_fusion.1.gram, f32[400,256]{1,0:T(8,128)S(1)} %reshape.60.matrix), custom_call_target="tpu_custom_call" | custom-call | tf_op jit(solution)/shard_map/factor/pallas_call | solution.py:160
  102.4 0.8 reshape.61
  (29 shorter events, 0.7 us)
Async XLA Ops:
  1.3 1.1 %copy-start = (f32[20,20,384]{2,1,0:T(8,128)S(1)}, f32[20,20,384]{2,1,0:T(8,128)}, u32[]{:S(2)}) copy-start(f32[20,20,384]{2,1,0:T(8,128)} %param.4) | copy-start | bytes 1843204
  2.5 8.6 %copy-start.1 = (f32[41]{0:T(128)S(1)}, f32[41]{0:T(128)}, u32[]{:S(2)}) copy-start(f32[41]{0:T(128)} %param.5) | copy-start | bytes 496
  3.4 14.4 %collective-permute-start.1 = (f32[20,20,256]{2,1,0:T(8,128)S(1)}, f32[20,20,256]{2,1,0:T(8,128)S(1)}, u32[]{:S(2)}, u32[]{:S(2)}) collective-permute-start(f32[20,20,256]{2,1,0:T(8,128)S(1)} %reshape.56), channel_id=1, source_target_pairs={{32,0},{64,32},{96,64},{128,96},{160,128},{192,160},{224,192},{33,... | collective-permute-start | bytes 1228808 | tf_op jit(solution)/shard_map/ppermute | solution.py:24
  4.7 26.7 %collective-permute-start = (f32[20,20,256]{2,1,0:T(8,128)S(1)}, f32[20,20,256]{2,1,0:T(8,128)S(1)}, u32[]{:S(2)}, u32[]{:S(2)}) collective-permute-start(f32[20,20,256]{2,1,0:T(8,128)S(1)} %reshape.56), channel_id=1, source_target_pairs={{0,32},{32,64},{64,96},{96,128},{128,160},{160,192},{192,224},{1,3... | collective-permute-start | bytes 1228808 | tf_op jit(solution)/shard_map/ppermute | solution.py:23
  32.0 3.2 %copy-start.2 = (f32[41]{0:T(128)S(1)}, f32[41]{0:T(128)}, u32[]{:S(2)}) copy-start(f32[41]{0:T(128)} %param.6) | copy-start | bytes 496
  33.1 7.9 %collective-permute-start.2 = (f32[20,20,256]{2,0,1:T(8,128)S(1)}, f32[20,20,256]{2,0,1:T(8,128)S(1)}, u32[]{:S(2)}, u32[]{:S(2)}) collective-permute-start(f32[20,20,256]{2,0,1:T(8,128)S(1)} %fusion.2), channel_id=1, source_target_pairs={{0,1},{1,2},{2,3},{3,4},{4,5},{5,6},{6,7},{7,8},{8,9},{9,10},{10,1... | collective-permute-start | bytes 1228808 | tf_op jit(solution)/shard_map/ppermute | solution.py:23
  35.2 8.6 %collective-permute-start.3 = (f32[20,20,256]{2,0,1:T(8,128)S(1)}, f32[20,20,256]{2,0,1:T(8,128)S(1)}, u32[]{:S(2)}, u32[]{:S(2)}) collective-permute-start(f32[20,20,256]{2,0,1:T(8,128)S(1)} %fusion.2), channel_id=1, source_target_pairs={{1,0},{2,1},{3,2},{4,3},{5,4},{6,5},{7,6},{8,7},{9,8},{10,9},{11,1... | collective-permute-start | bytes 1228808 | tf_op jit(solution)/shard_map/ppermute | solution.py:24
  46.1 3.1 %collective-permute-start.4 = (f32[128,256]{1,0:T(8,128)S(1)}, f32[128,256]{1,0:T(8,128)S(1)}, u32[]{:S(2)}, u32[]{:S(2)}) collective-permute-start(f32[128,256]{1,0:T(8,128)S(1)} %constant_dynamic-slice_fusion), channel_id=1, source_target_pairs={{0,1},{1,0},{2,3},{3,2},{4,5},{5,4},{6,7},{7,6},{8,9},{9,8},{10,11... | collective-permute-start | bytes 393224 | tf_op jit(solution)/shard_map/ppermute | solution.py:64
  86.5 5.1 %collective-permute-start.5 = (f32[128,256]{1,0:T(8,128)S(1)}, f32[128,256]{1,0:T(8,128)S(1)}, u32[]{:S(2)}, u32[]{:S(2)}) collective-permute-start(f32[128,256]{1,0:T(8,128)S(1)} %bitcast.33), channel_id=1, source_target_pairs={{0,1},{1,0},{2,3},{3,2},{4,5},{5,4},{6,7},{7,6},{8,9},{9,8},{10,11... | collective-permute-start | bytes 393224 | tf_op jit(solution)/shard_map/ppermute | solution.py:69

commit v3 on v2

--- a/solution.py
+++ b/solution.py
@@ -11,38 +11,6 @@
 SH = 20
 LAT = ("x", "yh")
 LON = ("yl", "z", "core")
-
-
-def extended_2(value, sides, width, wrap):
-    for axis, dim in sides:
-        peers, length = (lax.axis_size(axis), value.shape[dim])
-        up = [(i, (i + 1) % peers) for i in range(peers if wrap else peers - 1)]
-        down = [(j, i) for i, j in up]
-        last = lax.slice_in_dim(value, length - width, length, axis=dim)
-        initial = lax.slice_in_dim(value, 0, width, axis=dim)
-        before = lax.ppermute(last, axis, up)
-        after = lax.ppermute(initial, axis, down)
-        value = jnp.concatenate([before, value, after], axis=dim)
-    return value
-
-
-def skewed(coeffs, count, width):
-    period = jnp.pad(coeffs, (0, count))
-    flat = jnp.tile(period, count)[: count * width]
-    return flat.reshape(count, width)
-
-
-def banded(kernel, count):
-    return skewed(kernel, count, count + 2 * SH)
-
-
-def smooth_rows(band, extended):
-    rows_in, cols_in, hours = extended.shape
-    flat = extended.reshape(rows_in, cols_in * hours)
-    result = jnp.dot(
-        band, flat, precision=lax.Precision.HIGHEST, preferred_element_type=jnp.float32
-    )
-    return result.reshape(band.shape[0], cols_in, hours)
 
 
 PLANE = ("x", "yh", "yl")
@@ -151,19 +119,106 @@
     merged[TILE:, :TILE] = jnp.zeros((TILE, TILE), jnp.float32)
     merged[TILE:, TILE:] = r22 * (1.0 / scale)
     first, second = (matrix[:, :TILE], matrix[:, TILE:])
-    basis[:, :TILE] = product(first, w11 * scale, COLS)
-    basis[:, TILE:] = product(first, w21 * scale, COLS) + product(second, w22 * scale, COLS)
-
-
-def factored(gram, matrix, cells):
-    like = jax.ShapeDtypeStruct
+    left = product(first, w11 * scale, COLS)
+    right = product(first, w21 * scale, COLS) + product(second, w22 * scale, COLS)
+    lines, side, _ = basis.shape
+    for line in range(lines):
+        part = slice(line * side, (line + 1) * side)
+        basis[line, :, :TILE] = left[part]
+        basis[line, :, TILE:] = right[part]
+
+
+def shifted(kernel, rows, start):
+    flat = jnp.concatenate([kernel, jnp.zeros((1, TILE - kernel.shape[1]), jnp.float32)], axis=1)
+    return pltpu.roll(jnp.broadcast_to(flat, (rows, TILE)), start, 1, stride=1, stride_axis=0)
+
+
+def smoother(kernel, side):
+    pair = 2 * side
+    row = lax.broadcasted_iota(jnp.int32, (pair, TILE), 0)
+    lane = lax.broadcasted_iota(jnp.int32, (pair, TILE), 1)
+    total = jnp.zeros((pair, TILE), jnp.float32)
+    for part in range(3):
+        place = lane - part * pair
+        inside = (place >= 0) & (place < pair) & ((place >= side) == (row >= side))
+        total = jnp.where(inside, shifted(kernel, pair, part * side), total)
+    return total[:, : 3 * pair]
+
+
+def stacked(before, own, after, first, count):
+    part = slice(first, first + count)
+    halves = range(own.shape[0])
+    return jnp.concatenate(
+        [
+            jnp.concatenate([lines[half, part, :] for half in halves], axis=1)
+            for lines in (before, own, after)
+        ],
+        axis=0,
+    )
+
+
+def turned(out, line, side, value):
+    for half in range(out.shape[0]):
+        out.at[half][pl.ds(line, side, stride=out.shape[1] // side), :] = value[
+            :, half * TILE : (half + 1) * TILE
+        ]
+
+
+def filter_kernel(taps, field, out, padded):
+    rows, cols, hours = field.shape
+    steps = out.shape[0] * TILE
+    count = taps.shape[1]
+    lane = lax.broadcasted_iota(jnp.int32, (1, count), 1)
+    full = taps[...] + jnp.where(lane == TH, 1.0, 0.0)
+    full = jnp.concatenate([full, jnp.zeros((1, hours - count), jnp.float32)], axis=1)
+    skew = pltpu.roll(jnp.broadcast_to(full, (steps, hours)), 0, 1, stride=1, stride_axis=0)
+    padded[...] = jnp.zeros_like(padded)
+    padded[:, :cols, :] = field[...]
+    stride = padded.shape[1]
+    result = product(padded[...].reshape(rows * stride, hours), skew, COLS)
+    for row in range(rows):
+        turned(out, row, cols, result[row * stride : row * stride + cols])
+
+
+def lat_kernel_body(side, kernel, before, own, after, out):
+    band = smoother(kernel[...], side)
+    pair = 2 * side
+    for first in range(0, own.shape[1], pair):
+        result = product(band, stacked(before, own, after, first, pair), PLAIN)
+        for line in range(2):
+            turned(out, first // side + line, side, result[line * side : (line + 1) * side])
+
+
+def lon_kernel_body(side, weights, kernel, before, own, after, out, gram):
+    band = smoother(kernel[...], side)
+    pair = 2 * side
+    row = lax.broadcasted_iota(jnp.int32, (pair, 1), 0)
+    for first in range(0, own.shape[1], pair):
+        line = first // side
+        weight = jnp.where(row < side, weights[line], weights[line + 1])
+        result = product(band, stacked(before, own, after, first, pair), PLAIN)
+        out[first : first + pair, :] = result * weight
+    gram[...] = product(out[...], out[...], ROWS)
+
+
+def called(kernel, name, shapes, scratch, scalars, *args):
+    spaces = [pltpu.SMEM] * scalars + [pltpu.VMEM] * (len(args) - scalars)
     return pl.pallas_call(
-        functools.partial(factor_kernel, cells),
-        out_shape=(like(matrix.shape, jnp.float32), like(gram.shape, jnp.float32)),
-        scratch_shapes=[pltpu.VMEM((TILE, 2 * TILE), jnp.float32)],
-        compiler_params=pltpu.CompilerParams(vmem_limit_bytes=32 * 1024 * 1024),
-        name="factor",
-    )(gram, matrix)
+        kernel,
+        out_shape=[jax.ShapeDtypeStruct(shape, jnp.float32) for shape in shapes],
+        in_specs=[pl.BlockSpec(memory_space=space) for space in spaces],
+        out_specs=[pl.BlockSpec(memory_space=pltpu.VMEM)] * len(shapes),
+        scratch_shapes=scratch,
+        compiler_params=pltpu.CompilerParams(vmem_limit_bytes=24 * 1024 * 1024),
+        name=name,
+    )(*args)
+
+
+def neighbours(value, axes, wrap):
+    peers = lax.axis_size(axes)
+    up = [(i, (i + 1) % peers) for i in range(peers if wrap else peers - 1)]
+    down = [(j, i) for i, j in up]
+    return lax.ppermute(value, axes, up), lax.ppermute(value, axes, down)
 
 
 def body(field, lat_kernel, lon_kernel, time_taps):
@@ -171,43 +226,51 @@
     steps_out = length_in - 2 * TH
     lat_place = lax.axis_index(LAT)
     total_lat = rows_lat * lax.axis_size(LAT)
-    cells = total_lat * rows_lon * lax.axis_size(LON)
-    centre = (jnp.arange(2 * TH + 1, dtype=jnp.int32) == TH).astype(jnp.float32)
-    taps_full = time_taps + centre
-    skew_time = skewed(taps_full, steps_out, length_in)
-    filtered = lax.dot_general(
-        field.reshape(-1, length_in),
-        skew_time,
-        (((1,), (1,)), ((), ())),
-        precision=lax.Precision.HIGHEST,
-        preferred_element_type=jnp.float32,
-    ).reshape(rows_lat, rows_lon, steps_out)
-    lat_band = banded(lat_kernel, rows_lat)
-    lon_band = banded(lon_kernel, rows_lon)
-    extended = extended_2(filtered, ((LAT, 0),), SH, False)
-    narrow = smooth_rows(lat_band, extended)
-    lat_done = extended_2(narrow, ((LON, 1),), SH, True)
-    smooth = jnp.einsum(
-        "jk,ikt->ijt",
-        lon_band,
-        lat_done,
-        precision=lax.Precision.HIGHEST,
-        preferred_element_type=jnp.float32,
-    )
+    local = rows_lat * rows_lon
+    cells = local * lax.axis_size(LAT) * lax.axis_size(LON)
+    tall = -(-rows_lon // STEP) * STEP
     globrow = (lat_place * rows_lat + jnp.arange(rows_lat, dtype=jnp.int32)).astype(jnp.float32)
     latitude = jnp.pi * (globrow + 0.5) / total_lat - jnp.pi / 2
     weights = jnp.sqrt(jnp.cos(latitude))
-    matrix = (smooth * weights[:, None, None]).reshape(-1, steps_out)
-    local_gram = lax.dot_general(
+    flat = (local, steps_out)
+    halves = (steps_out // TILE, local, TILE)
+    (filtered,) = called(
+        filter_kernel,
+        "filter",
+        [halves],
+        [pltpu.VMEM((rows_lat, tall, length_in), jnp.float32)],
+        0,
+        time_taps[None],
+        field,
+    )
+    before, after = neighbours(filtered, LAT, False)
+    (lat_done,) = called(
+        functools.partial(lat_kernel_body, SH), "lat", [halves], [], 0, lat_kernel[None], before, filtered, after
+    )
+    before, after = neighbours(lat_done, LON, True)
+    matrix, local_gram = called(
+        functools.partial(lon_kernel_body, SH),
+        "lon",
+        [flat, (steps_out, steps_out)],
+        [],
+        1,
+        weights,
+        lon_kernel[None],
+        before,
+        lat_done,
+        after,
+    )
+    gram = summed(local_gram)
+    basis, merged = called(
+        functools.partial(factor_kernel, cells),
+        "factor",
+        [(rows_lat, rows_lon, steps_out), (steps_out, steps_out)],
+        [pltpu.VMEM((TILE, 2 * TILE), jnp.float32)],
+        0,
+        gram,
         matrix,
-        matrix,
-        (((0,), (0,)), ((), ())),
-        precision=lax.Precision.HIGHEST,
-        preferred_element_type=jnp.float32,
-    )
-    gram = summed(local_gram)
-    basis, merged = factored(gram, matrix, cells)
-    return (basis.reshape(rows_lat, rows_lon, steps_out), merged)
+    )
+    return (basis, merged)
 
 
 def solution(mesh):

time: 104 us -> 96.9 us (0.932)
  waiting for transfers between devices: 30 us -> 25.1 us
  Pallas kernels: 10.7 us -> 15.1 us
  matrix products: 4.12 us -> 0 us
  local copies, waits for them, and re-layouts: 3.2 us -> 1.84 us
  blocking collectives: 37.2 us -> 38.3 us
    ppermute x4, waiting for transfers between devices: 28.1 us -> 23.2 us  [neighbours(): return (lax.ppermute(value, axes, up), lax.ppermute(value, axes, down))]
    pallas_call x1 -> x4, Pallas kernels: 10.7 us -> 15.1 us  [called(): pl.pallas_call(kernel, out_shape=[jax.ShapeDtypeStruct(shape, jnp.float32...]
    dot_general x4 -> x0, matrix products: 4.12 us -> none  [the longest x1 1.22 us: body(): jnp.einsum('jk,ikt->ijt', lon_band, lat_done, precision=lax.Precision.HIG...]
    reshape x7 -> x0, local copies, waits for them, and re-layouts: 1.24 us -> none  [the longest x1 0.82 us: body(): return (basis.reshape(rows_lat, rows_lon, steps_out), merged)]
    all_to_all x2, blocking collectives: 22.6 us -> 23.7 us  [shared(): return lax.all_to_all(copies, axes, 0, 0)]
    ppermute x1, starting transfers between devices: 2.12 us -> 1.07 us  [summed(): kept = kept + lax.ppermute(given, 'core', swap)]
  transfers between devices with their start and end apart: 6 -> 6, of which waited for: 6 -> 5; matrix products, arithmetic and copies ran while one was open for 1% -> 0% of each run, Pallas kernels for 0% -> 0%
where the time goes in v3:
time: 96.9 us; the launch traced here: 96.6 us
  blocking collectives  38.3 us (40%)
  waiting for transfers between devices  25.1 us (26%)
  starting transfers between devices  15.3 us (16%)
  Pallas kernels  15.1 us (16%)
  local copies, waits for them, and re-layouts  1.84 us (2%)
    all_to_all x2, blocking collectives, shared(): return lax.all_to_all(copies, axes, 0, 0)  23.7 us
    ppermute x4, waiting for transfers between devices, neighbours(): return (lax.ppermute(value, axes, up), lax.ppermute(value, axes, down))  23.2 us
    pallas_call x4, Pallas kernels, called(): pl.pallas_call(kernel, out_shape=[jax.ShapeDtypeStruct(shape, jnp.float32...  15.1 us
    all_to_all x1, blocking collectives, summed(): lax.all_to_all(kept.reshape(peers, half // peers, cols), PLANE, 0, 0)  14.6 us
    ppermute x4, starting transfers between devices, neighbours(): return (lax.ppermute(value, axes, up), lax.ppermute(value, axes, down))  10.1 us
    ppermute x1, starting transfers between devices, summed(): given = lax.ppermute(kept, 'core', swap)  4.16 us
  transfers between devices with their start and end apart: 6, of which 5 were waited for; matrix products, arithmetic and copies ran while one was open for 0% of the time, Pallas kernels for 0%

profile of v3, /device:TPU:1, one launch (start us, length us, event | category | flops | bytes accessed | tf_op | source)
XLA Modules:
  0.0 96.6 jit_solution(11735281377767782224)
XLA Ops:
  0.6 0.0 copy-start.1
  0.6 0.7 copy-done.1
  1.3 0.0 copy-start
  1.3 1.1 %copy-done = f32[20,20,384]{2,1,0:T(8,128)S(1)} copy-done((f32[20,20,384]{2,1,0:T(8,128)S(1)}, f32[20,20,384]{2,1,0:T(8,128)}, u32[]{:S(2)}) %copy-start) | copy-done | bytes 614424
  2.4 1.0 %filter.1.own = f32[2,400,128]{2,1,0:T(8,128)S(1)} custom-call(f32[1,129]{1,0:T(1,128)S(1)} %bitcast.8, f32[20,20,384]{2,1,0:T(8,128)S(1)} %copy-done), custom_call_target="tpu_custom_call" | custom-call | tf_op jit(solution)/shard_map/filter/pallas_call | solution.py:206
  3.5 0.0 copy-start.2
  3.5 5.7 %collective-permute-start = (f32[2,400,128]{2,1,0:T(8,128)S(1)}, f32[2,400,128]{2,1,0:T(8,128)S(1)}, u32[]{:S(2)}, u32[]{:S(2)}) collective-permute-start(f32[2,400,128]{2,1,0:T(8,128)S(1)} %filter.1.own), channel_id=1, source_target_pairs={{0,32},{32,64},{64,96},{96,128},{128,160},{160,192},{192,224},{1,3... | collective-permute-start | bytes 1228808 | tf_op jit(solution)/shard_map/ppermute | solution.py:221
  9.2 1.3 %collective-permute-start.1 = (f32[2,400,128]{2,1,0:T(8,128)S(1)}, f32[2,400,128]{2,1,0:T(8,128)S(1)}, u32[]{:S(2)}, u32[]{:S(2)}) collective-permute-start(f32[2,400,128]{2,1,0:T(8,128)S(1)} %filter.1.own), channel_id=1, source_target_pairs={{32,0},{64,32},{96,64},{128,96},{160,128},{192,160},{224,192},{33,... | collective-permute-start | bytes 1228808 | tf_op jit(solution)/shard_map/ppermute | solution.py:221
  10.5 15.6 %collective-permute-done.before = f32[2,400,128]{2,1,0:T(8,128)S(1)} collective-permute-done((f32[2,400,128]{2,1,0:T(8,128)S(1)}, f32[2,400,128]{2,1,0:T(8,128)S(1)}, u32[]{:S(2)}, u32[]{:S(2)}) %collective-permute-start) | collective-permute-done | bytes 409632 | tf_op jit(solution)/shard_map/ppermute | solution.py:221
  26.0 0.0 collective-permute-done.1.after
  26.0 0.0 copy-done.2
  26.0 0.7 lat.1.own
  26.8 3.2 %collective-permute-start.2 = (f32[2,400,128]{2,1,0:T(8,128)S(1)}, f32[2,400,128]{2,1,0:T(8,128)S(1)}, u32[]{:S(2)}, u32[]{:S(2)}) collective-permute-start(f32[2,400,128]{2,1,0:T(8,128)S(1)} %lat.1.own), channel_id=1, source_target_pairs={{0,1},{1,2},{2,3},{3,4},{4,5},{5,6},{6,7},{7,8},{8,9},{9,10},{10,1... | collective-permute-start | bytes 1228808 | tf_op jit(solution)/shard_map/ppermute | solution.py:221
  29.9 0.0 collective-permute-start.3
  30.0 0.0 copy-start.3
  30.0 4.8 %collective-permute-done.2.before = f32[2,400,128]{2,1,0:T(8,128)S(1)} collective-permute-done((f32[2,400,128]{2,1,0:T(8,128)S(1)}, f32[2,400,128]{2,1,0:T(8,128)S(1)}, u32[]{:S(2)}, u32[]{:S(2)}) %collective-permute-start.2) | collective-permute-done | bytes 409632 | tf_op jit(solution)/shard_map/ppermute | solution.py:221
  34.8 2.8 %collective-permute-done.3.after = f32[2,400,128]{2,1,0:T(8,128)S(1)} collective-permute-done((f32[2,400,128]{2,1,0:T(8,128)S(1)}, f32[2,400,128]{2,1,0:T(8,128)S(1)}, u32[]{:S(2)}, u32[]{:S(2)}) %collective-permute-start.3) | collective-permute-done | bytes 409632 | tf_op jit(solution)/shard_map/ppermute | solution.py:221
  37.6 0.0 copy-done.3
  37.6 1.9 %lon.1 = (f32[400,256]{1,0:T(8,128)S(1)}, f32[256,256]{1,0:T(8,128)S(1)}) custom-call(f32[20]{0:T(128)S(1)} %cosine_sqrt_fusion.weights, f32[1,41]{1,0:T(1,128)S(1)} %bitcast.10, f32[2,400,128]{2,1,0:T(8,128)S(1)} %collective-permute-done.2.before, f32[2,400,128]{2,1,0:T(8,128)S(1)} %lat.1.own, f32[2,400,128]{2,1,0:T(8,128)S(1)} %collective-permute-done.3.after), custom_call_target="tpu_custom_call" | custom-call | tf_op jit(solution)/shard_map/lon/pallas_call | solution.py:206
  39.5 1.1 %collective-permute-start.4 = (f32[128,256]{1,0:T(8,128)S(1)}, f32[128,256]{1,0:T(8,128)S(1)}, u32[]{:S(2)}, u32[]{:S(2)}) collective-permute-start(f32[128,256]{1,0:T(8,128)S(1)} %constant_dynamic-slice_fusion), channel_id=1, source_target_pairs={{0,1},{1,0},{2,3},{3,2},{4,5},{5,4},{6,7},{7,6},{8,9},{9,8},{10,11... | collective-permute-start | bytes 393224 | tf_op jit(solution)/shard_map/ppermute | solution.py:32
  40.6 1.0 %collective-permute-done.4 = f32[128,256]{1,0:T(8,128)S(1)} collective-permute-done((f32[128,256]{1,0:T(8,128)S(1)}, f32[128,256]{1,0:T(8,128)S(1)}, u32[]{:S(2)}, u32[]{:S(2)}) %collective-permute-start.4) | collective-permute-done | bytes 131104 | tf_op jit(solution)/shard_map/ppermute | solution.py:32
  41.6 14.6 %all_to_all.15 = f32[16,8,256]{2,1,0:T(8,128)S(1)} all-to-all(f32[16,8,256]{2,1,0:T(8,128)S(1)} %add_bitcast_fusion), channel_id=1, replica_groups=mesh['x'=4,'yh'=2,'yl'=2,'z'=8,'core'=2] {'x','yh','yl'}, dimensions={0} | all-to-all | bytes 262144 | tf_op jit(solution)/shard_map/all_to_all | solution.py:34
  56.3 13.7 %all_to_all.16 = f32[8,8,256]{2,1,0:T(8,128)S(1)} all-to-all(f32[8,8,256]{2,1,0:T(8,128)S(1)} %broadcast_in_dim.24), channel_id=1, replica_groups=mesh['x'=4,'yh'=2,'yl'=2,'z'=8,'core'=2] {'z'}, dimensions={0} | all-to-all | bytes 131072 | tf_op jit(solution)/shard_map/all_to_all | solution.py:22
  70.0 9.9 %all_to_all.17 = f32[16,8,256]{2,1,0:T(8,128)S(1)} all-to-all(f32[16,8,256]{2,1,0:T(8,128)S(1)} %broadcast_in_dim.25), channel_id=1, replica_groups=mesh['x'=4,'yh'=2,'yl'=2,'z'=8,'core'=2] {'x','yh','yl'}, dimensions={0} | all-to-all | bytes 262144 | tf_op jit(solution)/shard_map/all_to_all | solution.py:22
  79.9 4.2 %collective-permute-start.5 = (f32[128,256]{1,0:T(8,128)S(1)}, f32[128,256]{1,0:T(8,128)S(1)}, u32[]{:S(2)}, u32[]{:S(2)}) collective-permute-start(f32[128,256]{1,0:T(8,128)S(1)} %bitcast.11), channel_id=1, source_target_pairs={{0,1},{1,0},{2,3},{3,2},{4,5},{5,4},{6,7},{7,6},{8,9},{9,8},{10,11... | collective-permute-start | bytes 393224 | tf_op jit(solution)/shard_map/ppermute | solution.py:37
  84.1 1.0 %collective-permute-done.5 = f32[128,256]{1,0:T(8,128)S(1)} collective-permute-done((f32[128,256]{1,0:T(8,128)S(1)}, f32[128,256]{1,0:T(8,128)S(1)}, u32[]{:S(2)}, u32[]{:S(2)}) %collective-permute-start.5) | collective-permute-done | bytes 131104 | tf_op jit(solution)/shard_map/ppermute | solution.py:37
  85.1 11.4 %factor.1 = (f32[20,20,256]{2,1,0:T(8,128)}, f32[256,256]{1,0:T(8,128)}) custom-call(f32[256,256]{1,0:T(8,128)S(1)} %pad_maximum_fusion.gram, f32[400,256]{1,0:T(8,128)S(1)} %get-tuple-element.5.matrix), custom_call_target="tpu_custom_call" | custom-call | tf_op jit(solution)/shard_map/factor/pallas_call | solution.py:206
  (9 shorter events, 0.2 us)
Async XLA Ops:
  0.6 0.7 copy-start.1
  1.3 1.1 %copy-start = (f32[20,20,384]{2,1,0:T(8,128)S(1)}, f32[20,20,384]{2,1,0:T(8,128)}, u32[]{:S(2)}) copy-start(f32[20,20,384]{2,1,0:T(8,128)} %field.1) | copy-start | bytes 1843204
  3.5 22.6 %copy-start.2 = (f32[41]{0:T(128)S(1)}, f32[41]{0:T(128)}, u32[]{:S(2)}) copy-start(f32[41]{0:T(128)} %param.5) | copy-start | bytes 496
  3.5 22.5 %collective-permute-start = (f32[2,400,128]{2,1,0:T(8,128)S(1)}, f32[2,400,128]{2,1,0:T(8,128)S(1)}, u32[]{:S(2)}, u32[]{:S(2)}) collective-permute-start(f32[2,400,128]{2,1,0:T(8,128)S(1)} %filter.1.own), channel_id=1, source_target_pairs={{0,32},{32,64},{64,96},{96,128},{128,160},{160,192},{192,224},{1,3... | collective-permute-start | bytes 1228808 | tf_op jit(solution)/shard_map/ppermute | solution.py:221
  9.2 16.9 %collective-permute-start.1 = (f32[2,400,128]{2,1,0:T(8,128)S(1)}, f32[2,400,128]{2,1,0:T(8,128)S(1)}, u32[]{:S(2)}, u32[]{:S(2)}) collective-permute-start(f32[2,400,128]{2,1,0:T(8,128)S(1)} %filter.1.own), channel_id=1, source_target_pairs={{32,0},{64,32},{96,64},{128,96},{160,128},{192,160},{224,192},{33,... | collective-permute-start | bytes 1228808 | tf_op jit(solution)/shard_map/ppermute | solution.py:221
  26.8 8.0 %collective-permute-start.2 = (f32[2,400,128]{2,1,0:T(8,128)S(1)}, f32[2,400,128]{2,1,0:T(8,128)S(1)}, u32[]{:S(2)}, u32[]{:S(2)}) collective-permute-start(f32[2,400,128]{2,1,0:T(8,128)S(1)} %lat.1.own), channel_id=1, source_target_pairs={{0,1},{1,2},{2,3},{3,4},{4,5},{5,6},{6,7},{7,8},{8,9},{9,10},{10,1... | collective-permute-start | bytes 1228808 | tf_op jit(solution)/shard_map/ppermute | solution.py:221
  29.9 7.7 %collective-permute-start.3 = (f32[2,400,128]{2,1,0:T(8,128)S(1)}, f32[2,400,128]{2,1,0:T(8,128)S(1)}, u32[]{:S(2)}, u32[]{:S(2)}) collective-permute-start(f32[2,400,128]{2,1,0:T(8,128)S(1)} %lat.1.own), channel_id=1, source_target_pairs={{1,0},{2,1},{3,2},{4,3},{5,4},{6,5},{7,6},{8,7},{9,8},{10,9},{11,1... | collective-permute-start | bytes 1228808 | tf_op jit(solution)/shard_map/ppermute | solution.py:221
  30.0 7.6 %copy-start.3 = (f32[41]{0:T(128)S(1)}, f32[41]{0:T(128)}, u32[]{:S(2)}) copy-start(f32[41]{0:T(128)} %param.6) | copy-start | bytes 496
  39.5 2.1 %collective-permute-start.4 = (f32[128,256]{1,0:T(8,128)S(1)}, f32[128,256]{1,0:T(8,128)S(1)}, u32[]{:S(2)}, u32[]{:S(2)}) collective-permute-start(f32[128,256]{1,0:T(8,128)S(1)} %constant_dynamic-slice_fusion), channel_id=1, source_target_pairs={{0,1},{1,0},{2,3},{3,2},{4,5},{5,4},{6,7},{7,6},{8,9},{9,8},{10,11... | collective-permute-start | bytes 393224 | tf_op jit(solution)/shard_map/ppermute | solution.py:32
  79.9 5.1 %collective-permute-start.5 = (f32[128,256]{1,0:T(8,128)S(1)}, f32[128,256]{1,0:T(8,128)S(1)}, u32[]{:S(2)}, u32[]{:S(2)}) collective-permute-start(f32[128,256]{1,0:T(8,128)S(1)} %bitcast.11), channel_id=1, source_target_pairs={{0,1},{1,0},{2,3},{3,2},{4,5},{5,4},{6,7},{7,6},{8,9},{9,8},{10,11... | collective-permute-start | bytes 393224 | tf_op jit(solution)/shard_map/ppermute | solution.py:37

commit v4 on v3

--- a/solution.py
+++ b/solution.py
@@ -147,26 +147,16 @@
 
 def stacked(before, own, after, first, count):
     part = slice(first, first + count)
-    halves = range(own.shape[0])
-    return jnp.concatenate(
-        [
-            jnp.concatenate([lines[half, part, :] for half in halves], axis=1)
-            for lines in (before, own, after)
-        ],
-        axis=0,
-    )
+    return jnp.concatenate([lines[part, :] for lines in (before, own, after)], axis=0)
 
 
 def turned(out, line, side, value):
-    for half in range(out.shape[0]):
-        out.at[half][pl.ds(line, side, stride=out.shape[1] // side), :] = value[
-            :, half * TILE : (half + 1) * TILE
-        ]
-
-
-def filter_kernel(taps, field, out, padded):
+    out[pl.ds(line, side, stride=out.shape[0] // side), :] = value
+
+
+def filter_kernel(taps, field, first, second, padded):
     rows, cols, hours = field.shape
-    steps = out.shape[0] * TILE
+    steps = 2 * TILE
     count = taps.shape[1]
     lane = lax.broadcasted_iota(jnp.int32, (1, count), 1)
     full = taps[...] + jnp.where(lane == TH, 1.0, 0.0)
@@ -177,26 +167,33 @@
     stride = padded.shape[1]
     result = product(padded[...].reshape(rows * stride, hours), skew, COLS)
     for row in range(rows):
-        turned(out, row, cols, result[row * stride : row * stride + cols])
-
-
-def lat_kernel_body(side, kernel, before, own, after, out):
-    band = smoother(kernel[...], side)
+        line = slice(row * stride, row * stride + cols)
+        turned(first, row, cols, result[line, :TILE])
+        turned(second, row, cols, result[line, TILE:])
+
+
+def lat_kernel_body(side, low, kernel, near, own, far, out):
     pair = 2 * side
-    for first in range(0, own.shape[1], pair):
-        result = product(band, stacked(before, own, after, first, pair), PLAIN)
+    plain = smoother(kernel[...], side)
+    lead, middle, trail = (plain[:, at : at + pair] for at in (0, pair, 2 * pair))
+    swapped = jnp.concatenate([trail, middle, lead], axis=1)
+    band = jnp.where(low[0] == 1, swapped, plain)
+    for first in range(0, own.shape[0], pair):
+        result = product(band, stacked(near, own, far, first, pair), PLAIN)
         for line in range(2):
             turned(out, first // side + line, side, result[line * side : (line + 1) * side])
 
 
-def lon_kernel_body(side, weights, kernel, before, own, after, out, gram):
+def lon_kernel_body(side, weights, kernel, *refs):
+    parts, (out, gram) = (refs[:-2], refs[-2:])
     band = smoother(kernel[...], side)
     pair = 2 * side
     row = lax.broadcasted_iota(jnp.int32, (pair, 1), 0)
-    for first in range(0, own.shape[1], pair):
+    for first in range(0, out.shape[0], pair):
         line = first // side
         weight = jnp.where(row < side, weights[line], weights[line + 1])
-        result = product(band, stacked(before, own, after, first, pair), PLAIN)
+        cells = [stacked(*parts[at : at + 3], first, pair) for at in (0, 3)]
+        result = product(band, jnp.concatenate(cells, axis=1), PLAIN)
         out[first : first + pair, :] = result * weight
     gram[...] = product(out[...], out[...], ROWS)
 
@@ -219,6 +216,14 @@
     up = [(i, (i + 1) % peers) for i in range(peers if wrap else peers - 1)]
     down = [(j, i) for i, j in up]
     return lax.ppermute(value, axes, up), lax.ppermute(value, axes, down)
+
+
+def passed_on(value):
+    spots, halves = (lax.axis_size("x"), lax.axis_size("yh"))
+    near = lax.ppermute(value, "yh", [(0, 1), (1, 0)])
+    up = [(x * halves, (x + 1) * halves) for x in range(spots - 1)]
+    down = [((x + 1) * halves + 1, x * halves + 1) for x in range(spots - 1)]
+    return near, lax.ppermute(near, LAT, up + down)
 
 
 def body(field, lat_kernel, lon_kernel, time_taps):
@@ -233,21 +238,25 @@
     latitude = jnp.pi * (globrow + 0.5) / total_lat - jnp.pi / 2
     weights = jnp.sqrt(jnp.cos(latitude))
     flat = (local, steps_out)
-    halves = (steps_out // TILE, local, TILE)
-    (filtered,) = called(
+    half = (local, TILE)
+    filtered = called(
         filter_kernel,
         "filter",
-        [halves],
+        [half, half],
         [pltpu.VMEM((rows_lat, tall, length_in), jnp.float32)],
         0,
         time_taps[None],
         field,
     )
-    before, after = neighbours(filtered, LAT, False)
-    (lat_done,) = called(
-        functools.partial(lat_kernel_body, SH), "lat", [halves], [], 0, lat_kernel[None], before, filtered, after
-    )
-    before, after = neighbours(lat_done, LON, True)
+    low = (lax.axis_index("yh") == 0).astype(jnp.int32)[None]
+    parts = []
+    for own in filtered:
+        near, far = passed_on(own)
+        (lat_done,) = called(
+            functools.partial(lat_kernel_body, SH), "lat", [half], [], 1, low, lat_kernel[None], near, own, far
+        )
+        before, after = neighbours(lat_done, LON, True)
+        parts += [before, lat_done, after]
     matrix, local_gram = called(
         functools.partial(lon_kernel_body, SH),
         "lon",
@@ -256,9 +265,7 @@
         1,
         weights,
         lon_kernel[None],
-        before,
-        lat_done,
-        after,
+        *parts,
     )
     gram = summed(local_gram)
     basis, merged = called(

time: 96.9 us -> 93.9 us (0.969)
  waiting for transfers between devices: 25.1 us -> 10.7 us
  starting transfers between devices: 15.3 us -> 25.8 us
    ppermute x4, waiting for transfers between devices: 23.2 us -> 4.17 us  [neighbours(): return (lax.ppermute(value, axes, up), lax.ppermute(value, axes, down))]
    ppermute x0 -> x4, starting transfers between devices: none -> 11.3 us  [the longest x2 7.35 us: passed_on(): return (near, lax.ppermute(near, LAT, up + down))]
    ppermute x0 -> x4, waiting for transfers between devices: none -> 4.58 us  [the longest x2 4.58 us: passed_on(): near = lax.ppermute(value, 'yh', [(0, 1), (1, 0)])]
    ppermute x4, starting transfers between devices: 10.1 us -> 7.32 us  [neighbours(): return (lax.ppermute(value, axes, up), lax.ppermute(value, axes, down))]
    ppermute x1, starting transfers between devices: 1.07 us -> 3.05 us  [summed(): kept = kept + lax.ppermute(given, 'core', swap)]
    pallas_call x4 -> x5, Pallas kernels: 15.1 us -> 15.9 us  [called(): pl.pallas_call(kernel, out_shape=[jax.ShapeDtypeStruct(shape, jnp.float32...]
  transfers between devices with their start and end apart: 6 -> 10, of which waited for: 5 -> 6; matrix products, arithmetic and copies ran while one was open for 0% -> 0% of each run, Pallas kernels for 0% -> 2%
where the time goes in v4:
time: 93.9 us; the launch traced here: 93.6 us
  blocking collectives  37.8 us (40%)
  starting transfers between devices  25.8 us (27%)
  Pallas kernels  15.9 us (17%)
  waiting for transfers between devices  10.7 us (11%)
  local copies, waits for them, and re-layouts  2.48 us (3%)
    all_to_all x2, blocking collectives, shared(): return lax.all_to_all(copies, axes, 0, 0)  24 us
    pallas_call x5, Pallas kernels, called(): pl.pallas_call(kernel, out_shape=[jax.ShapeDtypeStruct(shape, jnp.float32...  15.9 us
    all_to_all x1, blocking collectives, summed(): lax.all_to_all(kept.reshape(peers, half // peers, cols), PLANE, 0, 0)  13.7 us
    ppermute x2, starting transfers between devices, passed_on(): return (near, lax.ppermute(near, LAT, up + down))  7.35 us
    ppermute x4, starting transfers between devices, neighbours(): return (lax.ppermute(value, axes, up), lax.ppermute(value, axes, down))  7.32 us
    ppermute x2, waiting for transfers between devices, passed_on(): near = lax.ppermute(value, 'yh', [(0, 1), (1, 0)])  4.58 us
    ppermute x4, waiting for transfers between devices, neighbours(): return (lax.ppermute(value, axes, up), lax.ppermute(value, axes, down))  4.17 us
    ppermute x1, starting transfers between devices, summed(): given = lax.ppermute(kept, 'core', swap)  4.16 us
  transfers between devices with their start and end apart: 10, of which 6 were waited for; matrix products, arithmetic and copies ran while one was open for 0% of the time, Pallas kernels for 2%

profile of v4, /device:TPU:1, one launch (start us, length us, event | category | flops | bytes accessed | tf_op | source)
XLA Modules:
  0.0 93.6 jit_solution(10198326666003362674)
XLA Ops:
  0.6 0.7 copy-done.2
  1.3 1.1 %copy-done = f32[20,20,384]{2,1,0:T(8,128)S(1)} copy-done((f32[20,20,384]{2,1,0:T(8,128)S(1)}, f32[20,20,384]{2,1,0:T(8,128)}, u32[]{:S(2)}) %copy-start) | copy-done | bytes 614424
  2.4 1.0 %filter.1 = (f32[400,128]{1,0:T(8,128)S(1)}, f32[400,128]{1,0:T(8,128)S(1)}) custom-call(f32[1,129]{1,0:T(1,128)S(1)} %bitcast.11, f32[20,20,384]{2,1,0:T(8,128)S(1)} %copy-done), custom_call_target="tpu_custom_call" | custom-call | tf_op jit(solution)/shard_map/filter/pallas_call | solution.py:203
  3.5 3.8 %collective-permute-start.4 = (f32[400,128]{1,0:T(8,128)S(1)}, f32[400,128]{1,0:T(8,128)S(1)}, u32[]{:S(2)}, u32[]{:S(2)}) collective-permute-start(f32[400,128]{1,0:T(8,128)S(1)} %get-tuple-element.7.own), channel_id=1, source_target_pairs={{0,32},{32,0},{1,33},{33,1},{2,34},{34,2},{3,35},{35,3},{4,36},{36... | collective-permute-start | bytes 614408 | tf_op jit(solution)/shard_map/ppermute | solution.py:223
  7.3 0.1 collective-permute-start
  7.4 3.6 %collective-permute-done.4.near = f32[400,128]{1,0:T(8,128)S(1)} collective-permute-done((f32[400,128]{1,0:T(8,128)S(1)}, f32[400,128]{1,0:T(8,128)S(1)}, u32[]{:S(2)}, u32[]{:S(2)}) %collective-permute-start.4) | collective-permute-done | bytes 204832 | tf_op jit(solution)/shard_map/ppermute | solution.py:223
  11.1 3.9 %collective-permute-start.5 = (f32[400,128]{1,0:T(8,128)S(1)}, f32[400,128]{1,0:T(8,128)S(1)}, u32[]{:S(2)}, u32[]{:S(2)}) collective-permute-start(f32[400,128]{1,0:T(8,128)S(1)} %collective-permute-done.4.near), channel_id=1, source_target_pairs={{0,64},{64,128},{128,192},{96,32},{160,96},{224,160},{1,65},{65,12... | collective-permute-start | bytes 614408 | tf_op jit(solution)/shard_map/ppermute | solution.py:226
  15.0 0.9 %collective-permute-done.near = f32[400,128]{1,0:T(8,128)S(1)} collective-permute-done((f32[400,128]{1,0:T(8,128)S(1)}, f32[400,128]{1,0:T(8,128)S(1)}, u32[]{:S(2)}, u32[]{:S(2)}) %collective-permute-start) | collective-permute-done | bytes 204832 | tf_op jit(solution)/shard_map/ppermute | solution.py:223
  15.9 3.4 %collective-permute-start.1 = (f32[400,128]{1,0:T(8,128)S(1)}, f32[400,128]{1,0:T(8,128)S(1)}, u32[]{:S(2)}, u32[]{:S(2)}) collective-permute-start(f32[400,128]{1,0:T(8,128)S(1)} %collective-permute-done.near), channel_id=1, source_target_pairs={{0,64},{64,128},{128,192},{96,32},{160,96},{224,160},{1,65},{65,12... | collective-permute-start | bytes 614408 | tf_op jit(solution)/shard_map/ppermute | solution.py:226
  19.4 0.0 collective-permute-done.5.far
  19.4 0.0 copy-start.1
  19.4 0.6 copy-done.1
  20.0 0.7 lat.3.refs_4_
  20.8 4.3 %collective-permute-start.6 = (f32[400,128]{1,0:T(8,128)S(1)}, f32[400,128]{1,0:T(8,128)S(1)}, u32[]{:S(2)}, u32[]{:S(2)}) collective-permute-start(f32[400,128]{1,0:T(8,128)S(1)} %lat.3.refs_4_), channel_id=1, source_target_pairs={{0,1},{1,2},{2,3},{3,4},{4,5},{5,6},{6,7},{7,8},{8,9},{9,10},{10,1... | collective-permute-start | bytes 614408 | tf_op jit(solution)/shard_map/ppermute | solution.py:218
  25.1 0.0 collective-permute-start.7
  25.1 0.0 collective-permute-done.1.far
  25.1 0.8 lat.2.refs_1_
  25.9 2.0 %collective-permute-start.2 = (f32[400,128]{1,0:T(8,128)S(1)}, f32[400,128]{1,0:T(8,128)S(1)}, u32[]{:S(2)}, u32[]{:S(2)}) collective-permute-start(f32[400,128]{1,0:T(8,128)S(1)} %lat.2.refs_1_), channel_id=1, source_target_pairs={{0,1},{1,2},{2,3},{3,4},{4,5},{5,6},{6,7},{7,8},{8,9},{9,10},{10,1... | collective-permute-start | bytes 614408 | tf_op jit(solution)/shard_map/ppermute | solution.py:218
  27.9 0.9 %collective-permute-start.3 = (f32[400,128]{1,0:T(8,128)S(1)}, f32[400,128]{1,0:T(8,128)S(1)}, u32[]{:S(2)}, u32[]{:S(2)}) collective-permute-start(f32[400,128]{1,0:T(8,128)S(1)} %lat.2.refs_1_), channel_id=1, source_target_pairs={{1,0},{2,1},{3,2},{4,3},{5,4},{6,5},{7,6},{8,7},{9,8},{10,9},{11,1... | collective-permute-start | bytes 614408 | tf_op jit(solution)/shard_map/ppermute | solution.py:218
  28.9 0.0 copy-start.3
  28.9 1.7 %collective-permute-done.7.refs_5_ = f32[400,128]{1,0:T(8,128)S(1)} collective-permute-done((f32[400,128]{1,0:T(8,128)S(1)}, f32[400,128]{1,0:T(8,128)S(1)}, u32[]{:S(2)}, u32[]{:S(2)}) %collective-permute-start.7) | collective-permute-done | bytes 204832 | tf_op jit(solution)/shard_map/ppermute | solution.py:218
  30.6 0.0 collective-permute-done.2.refs_0_
  30.6 2.5 %collective-permute-done.3.refs_2_ = f32[400,128]{1,0:T(8,128)S(1)} collective-permute-done((f32[400,128]{1,0:T(8,128)S(1)}, f32[400,128]{1,0:T(8,128)S(1)}, u32[]{:S(2)}, u32[]{:S(2)}) %collective-permute-start.3) | collective-permute-done | bytes 204832 | tf_op jit(solution)/shard_map/ppermute | solution.py:218
  33.1 1.9 %lon.1 = (f32[400,256]{1,0:T(8,128)S(1)}, f32[256,256]{1,0:T(8,128)S(1)}) custom-call(f32[20]{0:T(128)S(1)} %cosine_sqrt_fusion.weights, f32[1,41]{1,0:T(1,128)S(1)} %bitcast.12, f32[400,128]{1,0:T(8,128)S(1)} %collective-permute-done.2.refs_0_, f32[400,128]{1,0:T(8,128)S(1)} %lat.2.refs_1_, f32[400,128]{1,0:T(8,128)S(1)} %collective-permute-done.3.refs_2_, ...), custom_call_target="tpu_custom_call" | custom-call | tf_op jit(solution)/shard_map/lon/pallas_call | solution.py:203
  35.0 3.0 %collective-permute-start.8 = (f32[128,256]{1,0:T(8,128)S(1)}, f32[128,256]{1,0:T(8,128)S(1)}, u32[]{:S(2)}, u32[]{:S(2)}) collective-permute-start(f32[128,256]{1,0:T(8,128)S(1)} %constant_dynamic-slice_fusion), channel_id=1, source_target_pairs={{0,1},{1,0},{2,3},{3,2},{4,5},{5,4},{6,7},{7,6},{8,9},{9,8},{10,11... | collective-permute-start | bytes 393224 | tf_op jit(solution)/shard_map/ppermute | solution.py:32
  38.1 1.0 %collective-permute-done.8 = f32[128,256]{1,0:T(8,128)S(1)} collective-permute-done((f32[128,256]{1,0:T(8,128)S(1)}, f32[128,256]{1,0:T(8,128)S(1)}, u32[]{:S(2)}, u32[]{:S(2)}) %collective-permute-start.8) | collective-permute-done | bytes 131104 | tf_op jit(solution)/shard_map/ppermute | solution.py:32
  39.1 13.7 %all_to_all.15 = f32[16,8,256]{2,1,0:T(8,128)S(1)} all-to-all(f32[16,8,256]{2,1,0:T(8,128)S(1)} %add_bitcast_fusion), channel_id=1, replica_groups=mesh['x'=4,'yh'=2,'yl'=2,'z'=8,'core'=2] {'x','yh','yl'}, dimensions={0} | all-to-all | bytes 262144 | tf_op jit(solution)/shard_map/all_to_all | solution.py:34
  52.9 14.1 %all_to_all.16 = f32[8,8,256]{2,1,0:T(8,128)S(1)} all-to-all(f32[8,8,256]{2,1,0:T(8,128)S(1)} %broadcast_in_dim.32), channel_id=1, replica_groups=mesh['x'=4,'yh'=2,'yl'=2,'z'=8,'core'=2] {'z'}, dimensions={0} | all-to-all | bytes 131072 | tf_op jit(solution)/shard_map/all_to_all | solution.py:22
  67.0 9.9 %all_to_all.17 = f32[16,8,256]{2,1,0:T(8,128)S(1)} all-to-all(f32[16,8,256]{2,1,0:T(8,128)S(1)} %broadcast_in_dim.33), channel_id=1, replica_groups=mesh['x'=4,'yh'=2,'yl'=2,'z'=8,'core'=2] {'x','yh','yl'}, dimensions={0} | all-to-all | bytes 262144 | tf_op jit(solution)/shard_map/all_to_all | solution.py:22
  77.0 4.2 %collective-permute-start.9 = (f32[128,256]{1,0:T(8,128)S(1)}, f32[128,256]{1,0:T(8,128)S(1)}, u32[]{:S(2)}, u32[]{:S(2)}) collective-permute-start(f32[128,256]{1,0:T(8,128)S(1)} %bitcast.13), channel_id=1, source_target_pairs={{0,1},{1,0},{2,3},{3,2},{4,5},{5,4},{6,7},{7,6},{8,9},{9,8},{10,11... | collective-permute-start | bytes 393224 | tf_op jit(solution)/shard_map/ppermute | solution.py:37
  81.1 1.0 %collective-permute-done.9 = f32[128,256]{1,0:T(8,128)S(1)} collective-permute-done((f32[128,256]{1,0:T(8,128)S(1)}, f32[128,256]{1,0:T(8,128)S(1)}, u32[]{:S(2)}, u32[]{:S(2)}) %collective-permute-start.9) | collective-permute-done | bytes 131104 | tf_op jit(solution)/shard_map/ppermute | solution.py:37
  82.2 11.4 %factor.1 = (f32[20,20,256]{2,1,0:T(8,128)}, f32[256,256]{1,0:T(8,128)}) custom-call(f32[256,256]{1,0:T(8,128)S(1)} %pad_maximum_fusion.gram, f32[400,256]{1,0:T(8,128)S(1)} %get-tuple-element.9.matrix), custom_call_target="tpu_custom_call" | custom-call | tf_op jit(solution)/shard_map/factor/pallas_call | solution.py:203
  (13 shorter events, 0.2 us)
Async XLA Ops:
  0.6 0.7 copy-start.2
  1.3 1.1 %copy-start = (f32[20,20,384]{2,1,0:T(8,128)S(1)}, f32[20,20,384]{2,1,0:T(8,128)}, u32[]{:S(2)}) copy-start(f32[20,20,384]{2,1,0:T(8,128)} %field.1) | copy-start | bytes 1843204
  3.5 7.6 %collective-permute-start.4 = (f32[400,128]{1,0:T(8,128)S(1)}, f32[400,128]{1,0:T(8,128)S(1)}, u32[]{:S(2)}, u32[]{:S(2)}) collective-permute-start(f32[400,128]{1,0:T(8,128)S(1)} %get-tuple-element.7.own), channel_id=1, source_target_pairs={{0,32},{32,0},{1,33},{33,1},{2,34},{34,2},{3,35},{35,3},{4,36},{36... | collective-permute-start | bytes 614408 | tf_op jit(solution)/shard_map/ppermute | solution.py:223
  7.3 8.6 %collective-permute-start = (f32[400,128]{1,0:T(8,128)S(1)}, f32[400,128]{1,0:T(8,128)S(1)}, u32[]{:S(2)}, u32[]{:S(2)}) collective-permute-start(f32[400,128]{1,0:T(8,128)S(1)} %get-tuple-element.6.own), channel_id=1, source_target_pairs={{0,32},{32,0},{1,33},{33,1},{2,34},{34,2},{3,35},{35,3},{4,36},{36... | collective-permute-start | bytes 614408 | tf_op jit(solution)/shard_map/ppermute | solution.py:223
  11.1 8.3 %collective-permute-start.5 = (f32[400,128]{1,0:T(8,128)S(1)}, f32[400,128]{1,0:T(8,128)S(1)}, u32[]{:S(2)}, u32[]{:S(2)}) collective-permute-start(f32[400,128]{1,0:T(8,128)S(1)} %collective-permute-done.4.near), channel_id=1, source_target_pairs={{0,64},{64,128},{128,192},{96,32},{160,96},{224,160},{1,65},{65,12... | collective-permute-start | bytes 614408 | tf_op jit(solution)/shard_map/ppermute | solution.py:226
  15.9 9.2 %collective-permute-start.1 = (f32[400,128]{1,0:T(8,128)S(1)}, f32[400,128]{1,0:T(8,128)S(1)}, u32[]{:S(2)}, u32[]{:S(2)}) collective-permute-start(f32[400,128]{1,0:T(8,128)S(1)} %collective-permute-done.near), channel_id=1, source_target_pairs={{0,64},{64,128},{128,192},{96,32},{160,96},{224,160},{1,65},{65,12... | collective-permute-start | bytes 614408 | tf_op jit(solution)/shard_map/ppermute | solution.py:226
  19.4 0.7 copy-start.1
  20.8 8.1 %collective-permute-start.6 = (f32[400,128]{1,0:T(8,128)S(1)}, f32[400,128]{1,0:T(8,128)S(1)}, u32[]{:S(2)}, u32[]{:S(2)}) collective-permute-start(f32[400,128]{1,0:T(8,128)S(1)} %lat.3.refs_4_), channel_id=1, source_target_pairs={{0,1},{1,2},{2,3},{3,4},{4,5},{5,6},{6,7},{7,8},{8,9},{9,10},{10,1... | collective-permute-start | bytes 614408 | tf_op jit(solution)/shard_map/ppermute | solution.py:218
  25.1 5.5 %collective-permute-start.7 = (f32[400,128]{1,0:T(8,128)S(1)}, f32[400,128]{1,0:T(8,128)S(1)}, u32[]{:S(2)}, u32[]{:S(2)}) collective-permute-start(f32[400,128]{1,0:T(8,128)S(1)} %lat.3.refs_4_), channel_id=1, source_target_pairs={{1,0},{2,1},{3,2},{4,3},{5,4},{6,5},{7,6},{8,7},{9,8},{10,9},{11,1... | collective-permute-start | bytes 614408 | tf_op jit(solution)/shard_map/ppermute | solution.py:218
  25.9 4.8 %collective-permute-start.2 = (f32[400,128]{1,0:T(8,128)S(1)}, f32[400,128]{1,0:T(8,128)S(1)}, u32[]{:S(2)}, u32[]{:S(2)}) collective-permute-start(f32[400,128]{1,0:T(8,128)S(1)} %lat.2.refs_1_), channel_id=1, source_target_pairs={{0,1},{1,2},{2,3},{3,4},{4,5},{5,6},{6,7},{7,8},{8,9},{9,10},{10,1... | collective-permute-start | bytes 614408 | tf_op jit(solution)/shard_map/ppermute | solution.py:218
  27.9 5.2 %collective-permute-start.3 = (f32[400,128]{1,0:T(8,128)S(1)}, f32[400,128]{1,0:T(8,128)S(1)}, u32[]{:S(2)}, u32[]{:S(2)}) collective-permute-start(f32[400,128]{1,0:T(8,128)S(1)} %lat.2.refs_1_), channel_id=1, source_target_pairs={{1,0},{2,1},{3,2},{4,3},{5,4},{6,5},{7,6},{8,7},{9,8},{10,9},{11,1... | collective-permute-start | bytes 614408 | tf_op jit(solution)/shard_map/ppermute | solution.py:218
  28.9 4.2 %copy-start.3 = (f32[41]{0:T(128)S(1)}, f32[41]{0:T(128)}, u32[]{:S(2)}) copy-start(f32[41]{0:T(128)} %param.6) | copy-start | bytes 496
  35.0 4.0 %collective-permute-start.8 = (f32[128,256]{1,0:T(8,128)S(1)}, f32[128,256]{1,0:T(8,128)S(1)}, u32[]{:S(2)}, u32[]{:S(2)}) collective-permute-start(f32[128,256]{1,0:T(8,128)S(1)} %constant_dynamic-slice_fusion), channel_id=1, source_target_pairs={{0,1},{1,0},{2,3},{3,2},{4,5},{5,4},{6,7},{7,6},{8,9},{9,8},{10,11... | collective-permute-start | bytes 393224 | tf_op jit(solution)/shard_map/ppermute | solution.py:32
  77.0 5.1 %collective-permute-start.9 = (f32[128,256]{1,0:T(8,128)S(1)}, f32[128,256]{1,0:T(8,128)S(1)}, u32[]{:S(2)}, u32[]{:S(2)}) collective-permute-start(f32[128,256]{1,0:T(8,128)S(1)} %bitcast.13), channel_id=1, source_target_pairs={{0,1},{1,0},{2,3},{3,2},{4,5},{5,4},{6,7},{7,6},{8,9},{9,8},{10,11... | collective-permute-start | bytes 393224 | tf_op jit(solution)/shard_map/ppermute | solution.py:37

commit v5 on v4

--- a/solution.py
+++ b/solution.py
@@ -172,27 +172,35 @@
         turned(second, row, cols, result[line, TILE:])
 
 
-def lat_kernel_body(side, low, kernel, near, own, far, out):
+def ordered(first, kernel, side):
     pair = 2 * side
     plain = smoother(kernel[...], side)
     lead, middle, trail = (plain[:, at : at + pair] for at in (0, pair, 2 * pair))
     swapped = jnp.concatenate([trail, middle, lead], axis=1)
-    band = jnp.where(low[0] == 1, swapped, plain)
-    for first in range(0, own.shape[0], pair):
-        result = product(band, stacked(near, own, far, first, pair), PLAIN)
-        for line in range(2):
-            turned(out, first // side + line, side, result[line * side : (line + 1) * side])
-
-
-def lon_kernel_body(side, weights, kernel, *refs):
-    parts, (out, gram) = (refs[:-2], refs[-2:])
-    band = smoother(kernel[...], side)
+    return jnp.where(first[0] == 1, swapped, plain)
+
+
+def lat_kernel_body(side, low, kernel, *refs):
+    parts, out = (refs[:-1], refs[-1])
+    band = ordered(low, kernel, side)
+    pair = 2 * side
+    for half in range(out.shape[0]):
+        lines = parts[3 * half : 3 * half + 3]
+        for first in range(0, out.shape[1], pair):
+            result = product(band, stacked(*lines, first, pair), PLAIN)
+            for line in range(2):
+                part = result[line * side : (line + 1) * side]
+                turned(out.at[half], first // side + line, side, part)
+
+
+def lon_kernel_body(side, weights, low, kernel, near, own, far, out, gram):
+    band = ordered(low, kernel, side)
     pair = 2 * side
     row = lax.broadcasted_iota(jnp.int32, (pair, 1), 0)
     for first in range(0, out.shape[0], pair):
         line = first // side
         weight = jnp.where(row < side, weights[line], weights[line + 1])
-        cells = [stacked(*parts[at : at + 3], first, pair) for at in (0, 3)]
+        cells = [stacked(near.at[at], own.at[at], far.at[at], first, pair) for at in range(2)]
         result = product(band, jnp.concatenate(cells, axis=1), PLAIN)
         out[first : first + pair, :] = result * weight
     gram[...] = product(out[...], out[...], ROWS)
@@ -211,11 +219,11 @@
     )(*args)
 
 
-def neighbours(value, axes, wrap):
-    peers = lax.axis_size(axes)
-    up = [(i, (i + 1) % peers) for i in range(peers if wrap else peers - 1)]
-    down = [(j, i) for i, j in up]
-    return lax.ppermute(value, axes, up), lax.ppermute(value, axes, down)
+def around(value):
+    peers = lax.axis_size(LON)
+    near = lax.ppermute(value, "core", [(0, 1), (1, 0)])
+    across = [(i, (i + 1) % peers) for i in range(1, peers, 2)]
+    return near, lax.ppermute(value, LON, across + [(j, i) for i, j in across])
 
 
 def passed_on(value):
@@ -252,20 +260,23 @@
     parts = []
     for own in filtered:
         near, far = passed_on(own)
-        (lat_done,) = called(
-            functools.partial(lat_kernel_body, SH), "lat", [half], [], 1, low, lat_kernel[None], near, own, far
-        )
-        before, after = neighbours(lat_done, LON, True)
-        parts += [before, lat_done, after]
+        parts += [near, own, far]
+    (lat_done,) = called(
+        functools.partial(lat_kernel_body, SH), "lat", [(2, local, TILE)], [], 1, low, lat_kernel[None], *parts
+    )
+    near, far = around(lat_done)
     matrix, local_gram = called(
         functools.partial(lon_kernel_body, SH),
         "lon",
         [flat, (steps_out, steps_out)],
         [],
-        1,
+        2,
         weights,
+        (lax.axis_index("core") == 0).astype(jnp.int32)[None],
         lon_kernel[None],
-        *parts,
+        near,
+        lat_done,
+        far,
     )
     gram = summed(local_gram)
     basis, merged = called(

time: 93.9 us -> 96.8 us (1.031)
  waiting for transfers between devices: 10.7 us -> 16.8 us
  blocking collectives: 37.8 us -> 35.7 us
  starting transfers between devices: 25.8 us -> 24.3 us
    ppermute x2, waiting for transfers between devices: 0.01 us -> 4.52 us  [passed_on(): return (near, lax.ppermute(near, LAT, up + down))]
    ppermute x4 -> x2, starting transfers between devices: 7.32 us -> 3.4 us  [the longest x1 1.78 us: around(): near = lax.ppermute(value, 'core', [(0, 1), (1, 0)])]
    ppermute x1, starting transfers between devices: 3.05 us -> 5.33 us  [summed(): kept = kept + lax.ppermute(given, 'core', swap)]
    all_to_all x2, blocking collectives: 24 us -> 21.8 us  [shared(): return lax.all_to_all(copies, axes, 0, 0)]
    ppermute x4 -> x2, waiting for transfers between devices: 4.17 us -> 5.7 us  [the longest x1 5.69 us: around(): lax.ppermute(value, LON, across + [(j, i) for i, j in across])]
    pallas_call x5 -> x4, Pallas kernels: 15.9 us -> 15.7 us  [called(): pl.pallas_call(kernel, out_shape=[jax.ShapeDtypeStruct(shape, jnp.float32...]
  transfers between devices with their start and end apart: 10 -> 8, of which waited for: 6 -> 6; matrix products, arithmetic and copies ran while one was open for 0% -> 0% of each run, Pallas kernels for 2% -> 0%
where the time goes in v5:
time: 96.8 us; the launch traced here: 96.5 us
  blocking collectives  35.7 us (37%)
  starting transfers between devices  24.3 us (25%)
  waiting for transfers between devices  16.8 us (17%)
  Pallas kernels  15.7 us (16%)
  local copies, waits for them, and re-layouts  3.13 us (3%)
    all_to_all x2, blocking collectives, shared(): return lax.all_to_all(copies, axes, 0, 0)  21.8 us
    pallas_call x4, Pallas kernels, called(): pl.pallas_call(kernel, out_shape=[jax.ShapeDtypeStruct(shape, jnp.float32...  15.7 us
    all_to_all x1, blocking collectives, summed(): lax.all_to_all(kept.reshape(peers, half // peers, cols), PLANE, 0, 0)  13.9 us
    ppermute x2, starting transfers between devices, passed_on(): return (near, lax.ppermute(near, LAT, up + down))  7.35 us
    ppermute x1, waiting for transfers between devices, around(): lax.ppermute(value, LON, across + [(j, i) for i, j in across])  5.69 us
    ppermute x1, starting transfers between devices, summed(): kept = kept + lax.ppermute(given, 'core', swap)  5.33 us
    ppermute x2, waiting for transfers between devices, passed_on(): near = lax.ppermute(value, 'yh', [(0, 1), (1, 0)])  4.58 us
    ppermute x2, waiting for transfers between devices, passed_on(): return (near, lax.ppermute(near, LAT, up + down))  4.52 us
  transfers between devices with their start and end apart: 8, of which 6 were waited for; matrix products, arithmetic and copies ran while one was open for 0% of the time, Pallas kernels for 0%

profile of v5, /device:TPU:1, one launch (start us, length us, event | category | flops | bytes accessed | tf_op | source)
XLA Modules:
  0.0 96.5 jit_solution(12172508747296675794)
XLA Ops:
  0.6 0.0 copy-start.1
  0.6 0.7 copy-done.1
  1.3 0.0 copy-start
  1.3 1.1 %copy-done = f32[20,20,384]{2,1,0:T(8,128)S(1)} copy-done((f32[20,20,384]{2,1,0:T(8,128)S(1)}, f32[20,20,384]{2,1,0:T(8,128)}, u32[]{:S(2)}) %copy-start) | copy-done | bytes 614424
  2.4 1.0 %filter.1 = (f32[400,128]{1,0:T(8,128)S(1)}, f32[400,128]{1,0:T(8,128)S(1)}) custom-call(f32[1,129]{1,0:T(1,128)S(1)} %bitcast.10, f32[20,20,384]{2,1,0:T(8,128)S(1)} %copy-done), custom_call_target="tpu_custom_call" | custom-call | tf_op jit(solution)/shard_map/filter/pallas_call | solution.py:211
  3.5 3.8 %collective-permute-start = (f32[400,128]{1,0:T(8,128)S(1)}, f32[400,128]{1,0:T(8,128)S(1)}, u32[]{:S(2)}, u32[]{:S(2)}) collective-permute-start(f32[400,128]{1,0:T(8,128)S(1)} %get-tuple-element.6.refs_1_), channel_id=1, source_target_pairs={{0,32},{32,0},{1,33},{33,1},{2,34},{34,2},{3,35},{35,3},{4,36},{36... | collective-permute-start | bytes 614408 | tf_op jit(solution)/shard_map/ppermute | solution.py:231
  7.3 0.1 collective-permute-start.2
  7.4 3.6 %collective-permute-done.refs_0_ = f32[400,128]{1,0:T(8,128)S(1)} collective-permute-done((f32[400,128]{1,0:T(8,128)S(1)}, f32[400,128]{1,0:T(8,128)S(1)}, u32[]{:S(2)}, u32[]{:S(2)}) %collective-permute-start) | collective-permute-done | bytes 204832 | tf_op jit(solution)/shard_map/ppermute | solution.py:231
  11.1 3.9 %collective-permute-start.1 = (f32[400,128]{1,0:T(8,128)S(1)}, f32[400,128]{1,0:T(8,128)S(1)}, u32[]{:S(2)}, u32[]{:S(2)}) collective-permute-start(f32[400,128]{1,0:T(8,128)S(1)} %collective-permute-done.refs_0_), channel_id=1, source_target_pairs={{0,64},{64,128},{128,192},{96,32},{160,96},{224,160},{1,65},{65,12... | collective-permute-start | bytes 614408 | tf_op jit(solution)/shard_map/ppermute | solution.py:234
  15.0 0.9 collective-permute-done.2.refs_3_
  15.9 3.4 %collective-permute-start.3 = (f32[400,128]{1,0:T(8,128)S(1)}, f32[400,128]{1,0:T(8,128)S(1)}, u32[]{:S(2)}, u32[]{:S(2)}) collective-permute-start(f32[400,128]{1,0:T(8,128)S(1)} %collective-permute-done.2.refs_3_), channel_id=1, source_target_pairs={{0,64},{64,128},{128,192},{96,32},{160,96},{224,160},{1,65},{65,12... | collective-permute-start | bytes 614408 | tf_op jit(solution)/shard_map/ppermute | solution.py:234
  19.4 0.0 collective-permute-done.1.refs_2_
  19.4 4.5 %collective-permute-done.3.refs_5_ = f32[400,128]{1,0:T(8,128)S(1)} collective-permute-done((f32[400,128]{1,0:T(8,128)S(1)}, f32[400,128]{1,0:T(8,128)S(1)}, u32[]{:S(2)}, u32[]{:S(2)}) %collective-permute-start.3) | collective-permute-done | bytes 204832 | tf_op jit(solution)/shard_map/ppermute | solution.py:234
  23.9 0.0 copy-start.2
  23.9 0.7 copy-done.2
  24.5 1.2 %lat.1.own = f32[2,400,128]{2,1,0:T(8,128)S(1)} custom-call(s32[1]{0:T(128)} %bitcast.2.low, f32[1,41]{1,0:T(1,128)S(1)} %bitcast.11, f32[400,128]{1,0:T(8,128)S(1)} %collective-permute-done.refs_0_, f32[400,128]{1,0:T(8,128)S(1)} %get-tuple-element.6.refs_1_, f32[400,128]{1,0:T(8,128)S(1)} %collective-permute-done.1.refs_2_, ...), custom_call_target="tpu_custom_call" | custom-call | tf_op jit(solution)/shard_map/lat/pallas_call | solution.py:211
  25.8 1.8 %collective-permute-start.4 = (f32[2,400,128]{2,1,0:T(8,128)S(1)}, f32[2,400,128]{2,1,0:T(8,128)S(1)}, u32[]{:S(2)}, u32[]{:S(2)}) collective-permute-start(f32[2,400,128]{2,1,0:T(8,128)S(1)} %lat.1.own), channel_id=1, source_target_pairs={{0,1},{1,0},{2,3},{3,2},{4,5},{5,4},{6,7},{7,6},{8,9},{9,8},{10,11... | collective-permute-start | bytes 1228808 | tf_op jit(solution)/shard_map/ppermute | solution.py:224
  27.6 1.6 %collective-permute-start.5 = (f32[2,400,128]{2,1,0:T(8,128)S(1)}, f32[2,400,128]{2,1,0:T(8,128)S(1)}, u32[]{:S(2)}, u32[]{:S(2)}) collective-permute-start(f32[2,400,128]{2,1,0:T(8,128)S(1)} %lat.1.own), channel_id=1, source_target_pairs={{1,2},{3,4},{5,6},{7,8},{9,10},{11,12},{13,14},{15,16},{17,18},{19... | collective-permute-start | bytes 1228808 | tf_op jit(solution)/shard_map/ppermute | solution.py:226
  29.2 0.0 collective-permute-done.4.near
  29.3 5.7 %collective-permute-done.5.far = f32[2,400,128]{2,1,0:T(8,128)S(1)} collective-permute-done((f32[2,400,128]{2,1,0:T(8,128)S(1)}, f32[2,400,128]{2,1,0:T(8,128)S(1)}, u32[]{:S(2)}, u32[]{:S(2)}) %collective-permute-start.5) | collective-permute-done | bytes 409632 | tf_op jit(solution)/shard_map/ppermute | solution.py:226
  34.9 0.0 copy-start.3
  35.0 0.7 copy-done.3
  35.6 1.9 %lon.1 = (f32[400,256]{1,0:T(8,128)S(1)}, f32[256,256]{1,0:T(8,128)S(1)}) custom-call(f32[20]{0:T(128)S(1)} %cosine_sqrt_fusion.weights, s32[1]{0:T(128)} %bitcast.low, f32[1,41]{1,0:T(1,128)S(1)} %bitcast.12, f32[2,400,128]{2,1,0:T(8,128)S(1)} %collective-permute-done.4.near, f32[2,400,128]{2,1,0:T(8,128)S(1)} %lat.1.own, ...), custom_call_target="tpu_custom_call" | custom-call | tf_op jit(solution)/shard_map/lon/pallas_call | solution.py:211
  37.6 5.3 %collective-permute-start.6 = (f32[128,256]{1,0:T(8,128)S(1)}, f32[128,256]{1,0:T(8,128)S(1)}, u32[]{:S(2)}, u32[]{:S(2)}) collective-permute-start(f32[128,256]{1,0:T(8,128)S(1)} %constant_dynamic-slice_fusion), channel_id=1, source_target_pairs={{0,1},{1,0},{2,3},{3,2},{4,5},{5,4},{6,7},{7,6},{8,9},{9,8},{10,11... | collective-permute-start | bytes 393224 | tf_op jit(solution)/shard_map/ppermute | solution.py:32
  42.9 1.0 %collective-permute-done.6 = f32[128,256]{1,0:T(8,128)S(1)} collective-permute-done((f32[128,256]{1,0:T(8,128)S(1)}, f32[128,256]{1,0:T(8,128)S(1)}, u32[]{:S(2)}, u32[]{:S(2)}) %collective-permute-start.6) | collective-permute-done | bytes 131104 | tf_op jit(solution)/shard_map/ppermute | solution.py:32
  43.9 13.9 %all_to_all.15 = f32[16,8,256]{2,1,0:T(8,128)S(1)} all-to-all(f32[16,8,256]{2,1,0:T(8,128)S(1)} %add_bitcast_fusion), channel_id=1, replica_groups=mesh['x'=4,'yh'=2,'yl'=2,'z'=8,'core'=2] {'x','yh','yl'}, dimensions={0} | all-to-all | bytes 262144 | tf_op jit(solution)/shard_map/all_to_all | solution.py:34
  57.9 11.6 %all_to_all.16 = f32[8,8,256]{2,1,0:T(8,128)S(1)} all-to-all(f32[8,8,256]{2,1,0:T(8,128)S(1)} %broadcast_in_dim.38), channel_id=1, replica_groups=mesh['x'=4,'yh'=2,'yl'=2,'z'=8,'core'=2] {'z'}, dimensions={0} | all-to-all | bytes 131072 | tf_op jit(solution)/shard_map/all_to_all | solution.py:22
  69.5 10.2 %all_to_all.17 = f32[16,8,256]{2,1,0:T(8,128)S(1)} all-to-all(f32[16,8,256]{2,1,0:T(8,128)S(1)} %broadcast_in_dim.39), channel_id=1, replica_groups=mesh['x'=4,'yh'=2,'yl'=2,'z'=8,'core'=2] {'x','yh','yl'}, dimensions={0} | all-to-all | bytes 262144 | tf_op jit(solution)/shard_map/all_to_all | solution.py:22
  79.7 4.3 %collective-permute-start.7 = (f32[128,256]{1,0:T(8,128)S(1)}, f32[128,256]{1,0:T(8,128)S(1)}, u32[]{:S(2)}, u32[]{:S(2)}) collective-permute-start(f32[128,256]{1,0:T(8,128)S(1)} %bitcast.13), channel_id=1, source_target_pairs={{0,1},{1,0},{2,3},{3,2},{4,5},{5,4},{6,7},{7,6},{8,9},{9,8},{10,11... | collective-permute-start | bytes 393224 | tf_op jit(solution)/shard_map/ppermute | solution.py:37
  84.0 1.0 %collective-permute-done.7 = f32[128,256]{1,0:T(8,128)S(1)} collective-permute-done((f32[128,256]{1,0:T(8,128)S(1)}, f32[128,256]{1,0:T(8,128)S(1)}, u32[]{:S(2)}, u32[]{:S(2)}) %collective-permute-start.7) | collective-permute-done | bytes 131104 | tf_op jit(solution)/shard_map/ppermute | solution.py:37
  85.0 11.4 %factor.1 = (f32[20,20,256]{2,1,0:T(8,128)}, f32[256,256]{1,0:T(8,128)}) custom-call(f32[256,256]{1,0:T(8,128)S(1)} %pad_maximum_fusion.gram, f32[400,256]{1,0:T(8,128)S(1)} %get-tuple-element.9.matrix), custom_call_target="tpu_custom_call" | custom-call | tf_op jit(solution)/shard_map/factor/pallas_call | solution.py:211
  (9 shorter events, 0.2 us)
Async XLA Ops:
  0.6 0.7 copy-start.1
  1.3 1.1 %copy-start = (f32[20,20,384]{2,1,0:T(8,128)S(1)}, f32[20,20,384]{2,1,0:T(8,128)}, u32[]{:S(2)}) copy-start(f32[20,20,384]{2,1,0:T(8,128)} %field.1) | copy-start | bytes 1843204
  3.5 7.6 %collective-permute-start = (f32[400,128]{1,0:T(8,128)S(1)}, f32[400,128]{1,0:T(8,128)S(1)}, u32[]{:S(2)}, u32[]{:S(2)}) collective-permute-start(f32[400,128]{1,0:T(8,128)S(1)} %get-tuple-element.6.refs_1_), channel_id=1, source_target_pairs={{0,32},{32,0},{1,33},{33,1},{2,34},{34,2},{3,35},{35,3},{4,36},{36... | collective-permute-start | bytes 614408 | tf_op jit(solution)/shard_map/ppermute | solution.py:231
  7.3 8.6 %collective-permute-start.2 = (f32[400,128]{1,0:T(8,128)S(1)}, f32[400,128]{1,0:T(8,128)S(1)}, u32[]{:S(2)}, u32[]{:S(2)}) collective-permute-start(f32[400,128]{1,0:T(8,128)S(1)} %get-tuple-element.7.refs_4_), channel_id=1, source_target_pairs={{0,32},{32,0},{1,33},{33,1},{2,34},{34,2},{3,35},{35,3},{4,36},{36... | collective-permute-start | bytes 614408 | tf_op jit(solution)/shard_map/ppermute | solution.py:231
  11.1 8.3 %collective-permute-start.1 = (f32[400,128]{1,0:T(8,128)S(1)}, f32[400,128]{1,0:T(8,128)S(1)}, u32[]{:S(2)}, u32[]{:S(2)}) collective-permute-start(f32[400,128]{1,0:T(8,128)S(1)} %collective-permute-done.refs_0_), channel_id=1, source_target_pairs={{0,64},{64,128},{128,192},{96,32},{160,96},{224,160},{1,65},{65,12... | collective-permute-start | bytes 614408 | tf_op jit(solution)/shard_map/ppermute | solution.py:234
  15.9 8.0 %collective-permute-start.3 = (f32[400,128]{1,0:T(8,128)S(1)}, f32[400,128]{1,0:T(8,128)S(1)}, u32[]{:S(2)}, u32[]{:S(2)}) collective-permute-start(f32[400,128]{1,0:T(8,128)S(1)} %collective-permute-done.2.refs_3_), channel_id=1, source_target_pairs={{0,64},{64,128},{128,192},{96,32},{160,96},{224,160},{1,65},{65,12... | collective-permute-start | bytes 614408 | tf_op jit(solution)/shard_map/ppermute | solution.py:234
  23.9 0.7 copy-start.2
  25.8 3.5 %collective-permute-start.4 = (f32[2,400,128]{2,1,0:T(8,128)S(1)}, f32[2,400,128]{2,1,0:T(8,128)S(1)}, u32[]{:S(2)}, u32[]{:S(2)}) collective-permute-start(f32[2,400,128]{2,1,0:T(8,128)S(1)} %lat.1.own), channel_id=1, source_target_pairs={{0,1},{1,0},{2,3},{3,2},{4,5},{5,4},{6,7},{7,6},{8,9},{9,8},{10,11... | collective-permute-start | bytes 1228808 | tf_op jit(solution)/shard_map/ppermute | solution.py:224
  27.6 7.4 %collective-permute-start.5 = (f32[2,400,128]{2,1,0:T(8,128)S(1)}, f32[2,400,128]{2,1,0:T(8,128)S(1)}, u32[]{:S(2)}, u32[]{:S(2)}) collective-permute-start(f32[2,400,128]{2,1,0:T(8,128)S(1)} %lat.1.own), channel_id=1, source_target_pairs={{1,2},{3,4},{5,6},{7,8},{9,10},{11,12},{13,14},{15,16},{17,18},{19... | collective-permute-start | bytes 1228808 | tf_op jit(solution)/shard_map/ppermute | solution.py:226
  34.9 0.7 copy-start.3
  37.6 6.3 %collective-permute-start.6 = (f32[128,256]{1,0:T(8,128)S(1)}, f32[128,256]{1,0:T(8,128)S(1)}, u32[]{:S(2)}, u32[]{:S(2)}) collective-permute-start(f32[128,256]{1,0:T(8,128)S(1)} %constant_dynamic-slice_fusion), channel_id=1, source_target_pairs={{0,1},{1,0},{2,3},{3,2},{4,5},{5,4},{6,7},{7,6},{8,9},{9,8},{10,11... | collective-permute-start | bytes 393224 | tf_op jit(solution)/shard_map/ppermute | solution.py:32
  79.7 5.2 %collective-permute-start.7 = (f32[128,256]{1,0:T(8,128)S(1)}, f32[128,256]{1,0:T(8,128)S(1)}, u32[]{:S(2)}, u32[]{:S(2)}) collective-permute-start(f32[128,256]{1,0:T(8,128)S(1)} %bitcast.13), channel_id=1, source_target_pairs={{0,1},{1,0},{2,3},{3,2},{4,5},{5,4},{6,7},{7,6},{8,9},{9,8},{10,11... | collective-permute-start | bytes 393224 | tf_op jit(solution)/shard_map/ppermute | solution.py:37

commit v6 on v4

--- a/solution.py
+++ b/solution.py
@@ -118,7 +118,7 @@
     merged[:TILE, TILE:] = r12 * (1.0 / scale)
     merged[TILE:, :TILE] = jnp.zeros((TILE, TILE), jnp.float32)
     merged[TILE:, TILE:] = r22 * (1.0 / scale)
-    first, second = (matrix[:, :TILE], matrix[:, TILE:])
+    first, second = (matrix[0], matrix[1])
     left = product(first, w11 * scale, COLS)
     right = product(first, w21 * scale, COLS) + product(second, w22 * scale, COLS)
     lines, side, _ = basis.shape
@@ -154,68 +154,95 @@
     out[pl.ds(line, side, stride=out.shape[0] // side), :] = value
 
 
-def filter_kernel(taps, field, first, second, padded):
+def ordered(first, kernel, side):
+    pair = 2 * side
+    plain = smoother(kernel[...], side)
+    lead, middle, trail = (plain[:, at : at + pair] for at in (0, pair, 2 * pair))
+    swapped = jnp.concatenate([trail, middle, lead], axis=1)
+    return jnp.where(first == 1, swapped, plain)
+
+
+def bands_kernel(side, low, weights, lat_kernel, lon_kernel, lat_band, lon_band, lat_weighted):
+    lat_band[...] = ordered(low[0], lat_kernel, side)
+    lon_band[...] = ordered(low[1], lon_kernel, side)
+    row = lax.broadcasted_iota(jnp.int32, (2 * side, 1), 0)
+    weight = jnp.zeros((2 * side, 1), jnp.float32)
+    for line in range(side):
+        weight = jnp.where((row == line) | (row == side + line), weights[line], weight)
+    lat_weighted[...] = lat_band[...] * weight
+
+
+def filter_kernel(lines, taps, field, first, second, staged, padded, arrived):
     rows, cols, hours = field.shape
-    steps = 2 * TILE
+    stride = padded.shape[1]
+    parts = [pl.ds(row, lines) for row in range(0, rows, lines)]
+    copies = [
+        pltpu.make_async_copy(field.at[part], staged.at[part], arrived.at[at])
+        for at, part in enumerate(parts)
+    ]
+    for copy in copies:
+        copy.start()
+    padded[:, cols:, :] = jnp.zeros((rows, stride - cols, hours), jnp.float32)
     count = taps.shape[1]
     lane = lax.broadcasted_iota(jnp.int32, (1, count), 1)
     full = taps[...] + jnp.where(lane == TH, 1.0, 0.0)
     full = jnp.concatenate([full, jnp.zeros((1, hours - count), jnp.float32)], axis=1)
-    skew = pltpu.roll(jnp.broadcast_to(full, (steps, hours)), 0, 1, stride=1, stride_axis=0)
-    padded[...] = jnp.zeros_like(padded)
-    padded[:, :cols, :] = field[...]
-    stride = padded.shape[1]
-    result = product(padded[...].reshape(rows * stride, hours), skew, COLS)
-    for row in range(rows):
-        line = slice(row * stride, row * stride + cols)
-        turned(first, row, cols, result[line, :TILE])
-        turned(second, row, cols, result[line, TILE:])
-
-
-def lat_kernel_body(side, low, kernel, near, own, far, out):
+    skew = pltpu.roll(jnp.broadcast_to(full, (2 * TILE, hours)), 0, 1, stride=1, stride_axis=0)
+    for at, copy in enumerate(copies):
+        copy.wait()
+        part = slice(at * lines, (at + 1) * lines)
+        padded[part, :cols, :] = staged[part]
+        part = padded[part].reshape(lines * stride, hours)
+        result = product(part, skew, COLS)
+        for line in range(lines):
+            row = at * lines + line
+            value = result[line * stride : line * stride + cols]
+            turned(first, row, cols, value[:, :TILE])
+            second[row * cols : (row + 1) * cols, :] = value[:, TILE:]
+
+
+def smooth_kernel(side, band, near, own, far, out):
     pair = 2 * side
-    plain = smoother(kernel[...], side)
-    lead, middle, trail = (plain[:, at : at + pair] for at in (0, pair, 2 * pair))
-    swapped = jnp.concatenate([trail, middle, lead], axis=1)
-    band = jnp.where(low[0] == 1, swapped, plain)
-    for first in range(0, own.shape[0], pair):
-        result = product(band, stacked(near, own, far, first, pair), PLAIN)
+    for first in range(0, out.shape[0], pair):
+        result = product(band[...], stacked(near, own, far, first, pair), PLAIN)
         for line in range(2):
             turned(out, first // side + line, side, result[line * side : (line + 1) * side])
 
 
-def lon_kernel_body(side, weights, kernel, *refs):
+def last_kernel(side, weights, lon_band, lat_band, *refs):
     parts, (out, gram) = (refs[:-2], refs[-2:])
-    band = smoother(kernel[...], side)
     pair = 2 * side
     row = lax.broadcasted_iota(jnp.int32, (pair, 1), 0)
-    for first in range(0, out.shape[0], pair):
+    for first in range(0, out.shape[1], pair):
         line = first // side
         weight = jnp.where(row < side, weights[line], weights[line + 1])
-        cells = [stacked(*parts[at : at + 3], first, pair) for at in (0, 3)]
-        result = product(band, jnp.concatenate(cells, axis=1), PLAIN)
-        out[first : first + pair, :] = result * weight
-    gram[...] = product(out[...], out[...], ROWS)
-
-
-def called(kernel, name, shapes, scratch, scalars, *args):
-    spaces = [pltpu.SMEM] * scalars + [pltpu.VMEM] * (len(args) - scalars)
+        result = product(lon_band[...], stacked(*parts[:3], first, pair), PLAIN)
+        out[0, first : first + pair, :] = result * weight
+        result = product(lat_band[...], stacked(*parts[3:], first, pair), PLAIN)
+        for at in range(2):
+            turned(out.at[1], line + at, side, result[at * side : (at + 1) * side])
+    both = jnp.concatenate([out[0], out[1]], axis=1)
+    gram[...] = product(both, both, ROWS)
+
+
+def called(kernel, name, shapes, spaces, scratch, *args, mib=24):
+    spaces = list(spaces) + [pltpu.VMEM] * (len(args) - len(spaces))
     return pl.pallas_call(
         kernel,
         out_shape=[jax.ShapeDtypeStruct(shape, jnp.float32) for shape in shapes],
         in_specs=[pl.BlockSpec(memory_space=space) for space in spaces],
         out_specs=[pl.BlockSpec(memory_space=pltpu.VMEM)] * len(shapes),
         scratch_shapes=scratch,
-        compiler_params=pltpu.CompilerParams(vmem_limit_bytes=24 * 1024 * 1024),
+        compiler_params=pltpu.CompilerParams(vmem_limit_bytes=mib * 1024 * 1024),
         name=name,
     )(*args)
 
 
-def neighbours(value, axes, wrap):
-    peers = lax.axis_size(axes)
-    up = [(i, (i + 1) % peers) for i in range(peers if wrap else peers - 1)]
-    down = [(j, i) for i, j in up]
-    return lax.ppermute(value, axes, up), lax.ppermute(value, axes, down)
+def around(value):
+    peers = lax.axis_size(LON)
+    near = lax.ppermute(value, "core", [(0, 1), (1, 0)])
+    across = [(i, (i + 1) % peers) for i in range(1, peers, 2)]
+    return near, lax.ppermute(value, LON, across + [(j, i) for i, j in across])
 
 
 def passed_on(value):
@@ -237,43 +264,65 @@
     globrow = (lat_place * rows_lat + jnp.arange(rows_lat, dtype=jnp.int32)).astype(jnp.float32)
     latitude = jnp.pi * (globrow + 0.5) / total_lat - jnp.pi / 2
     weights = jnp.sqrt(jnp.cos(latitude))
-    flat = (local, steps_out)
     half = (local, TILE)
-    filtered = called(
-        filter_kernel,
+    lines = 4
+    first, second = called(
+        functools.partial(filter_kernel, lines),
         "filter",
         [half, half],
-        [pltpu.VMEM((rows_lat, tall, length_in), jnp.float32)],
-        0,
+        [pltpu.VMEM, pltpu.HBM],
+        [
+            pltpu.VMEM((rows_lat, rows_lon, length_in), jnp.float32),
+            pltpu.VMEM((rows_lat, tall, length_in), jnp.float32),
+            pltpu.SemaphoreType.DMA((rows_lat // lines,)),
+        ],
         time_taps[None],
         field,
-    )
-    low = (lax.axis_index("yh") == 0).astype(jnp.int32)[None]
-    parts = []
-    for own in filtered:
-        near, far = passed_on(own)
-        (lat_done,) = called(
-            functools.partial(lat_kernel_body, SH), "lat", [half], [], 1, low, lat_kernel[None], near, own, far
-        )
-        before, after = neighbours(lat_done, LON, True)
-        parts += [before, lat_done, after]
+        mib=56,
+    )
+    low = jnp.stack([lax.axis_index("yh") == 0, lax.axis_index("core") == 0]).astype(jnp.int32)
+    bands = [(2 * SH, 6 * SH)] * 3
+    lat_band, lon_band, lat_weighted = called(
+        functools.partial(bands_kernel, SH),
+        "bands",
+        bands,
+        [pltpu.SMEM] * 2,
+        [],
+        low,
+        weights,
+        lat_kernel[None],
+        lon_kernel[None],
+    )
+    smooth = functools.partial(smooth_kernel, SH)
+    near, far = passed_on(first)
+    beside, beyond = around(second)
+    (second,) = called(smooth, "lon", [half], [], [], lon_band, beside, second, beyond)
+    (first,) = called(smooth, "lat", [half], [], [], lat_band, near, first, far)
+    near, far = passed_on(second)
+    beside, beyond = around(first)
     matrix, local_gram = called(
-        functools.partial(lon_kernel_body, SH),
-        "lon",
-        [flat, (steps_out, steps_out)],
+        functools.partial(last_kernel, SH),
+        "last",
+        [(2,) + half, (steps_out, steps_out)],
+        [pltpu.SMEM],
         [],
-        1,
         weights,
-        lon_kernel[None],
-        *parts,
+        lon_band,
+        lat_weighted,
+        beside,
+        first,
+        beyond,
+        near,
+        second,
+        far,
     )
     gram = summed(local_gram)
     basis, merged = called(
         functools.partial(factor_kernel, cells),
         "factor",
         [(rows_lat, rows_lon, steps_out), (steps_out, steps_out)],
+        [],
         [pltpu.VMEM((TILE, 2 * TILE), jnp.float32)],
-        0,
         gram,
         matrix,
     )

time: 93.9 us -> 94.2 us (level)
  Pallas kernels: 15.9 us -> 21.6 us
  blocking collectives: 37.8 us -> 33.1 us
    pallas_call x5 -> x6, Pallas kernels: 15.9 us -> 21.6 us  [called(): pl.pallas_call(kernel, out_shape=[jax.ShapeDtypeStruct(shape, jnp.float32...]
    all_to_all x2, blocking collectives: 24 us -> 19.7 us  [shared(): return lax.all_to_all(copies, axes, 0, 0)]
    ppermute x4, waiting for transfers between devices: 4.17 us -> 6.53 us  [the longest x2 5.45 us: around(): lax.ppermute(value, LON, across + [(j, i) for i, j in across])]
    ppermute x2, waiting for transfers between devices: 4.58 us -> 2.88 us  [passed_on(): near = lax.ppermute(value, 'yh', [(0, 1), (1, 0)])]
    ppermute x4, starting transfers between devices: 7.32 us -> 8.65 us  [the longest x2 8.65 us: around(): near = lax.ppermute(value, 'core', [(0, 1), (1, 0)])]
    ppermute x1, starting transfers between devices: 3.05 us -> 2 us  [summed(): kept = kept + lax.ppermute(given, 'core', swap)]
where the time goes in v6:
time: 94.2 us; the launch traced here: 93.9 us
  blocking collectives  33.1 us (35%)
  starting transfers between devices  25.2 us (27%)
  Pallas kernels  21.6 us (23%)
  waiting for transfers between devices  11.4 us (12%)
  local copies, waits for them, and re-layouts  1.64 us (2%)
    pallas_call x6, Pallas kernels, called(): pl.pallas_call(kernel, out_shape=[jax.ShapeDtypeStruct(shape, jnp.float32...  21.6 us
    all_to_all x2, blocking collectives, shared(): return lax.all_to_all(copies, axes, 0, 0)  19.7 us
    all_to_all x1, blocking collectives, summed(): lax.all_to_all(kept.reshape(peers, half // peers, cols), PLANE, 0, 0)  13.4 us
    ppermute x2, starting transfers between devices, around(): near = lax.ppermute(value, 'core', [(0, 1), (1, 0)])  8.65 us
    ppermute x2, starting transfers between devices, passed_on(): return (near, lax.ppermute(near, LAT, up + down))  6.45 us
    ppermute x2, waiting for transfers between devices, around(): lax.ppermute(value, LON, across + [(j, i) for i, j in across])  5.45 us
    ppermute x1, starting transfers between devices, summed(): given = lax.ppermute(kept, 'core', swap)  4.08 us
    ppermute x2, starting transfers between devices, passed_on(): near = lax.ppermute(value, 'yh', [(0, 1), (1, 0)])  4.07 us
  transfers between devices with their start and end apart: 10, of which 6 were waited for; matrix products, arithmetic and copies ran while one was open for 0% of the time, Pallas kernels for 2%

profile of v6, /device:TPU:1, one launch (start us, length us, event | category | flops | bytes accessed | tf_op | source)
XLA Modules:
  0.0 93.9 jit_solution(16616940865659026658)
XLA Ops:
  0.6 5.9 %filter.1 = (f32[400,128]{1,0:T(8,128)}, f32[400,128]{1,0:T(8,128)}) custom-call(f32[1,129]{1,0:T(1,128)} %bitcast.13, f32[20,20,384]{2,1,0:T(8,128)} %field.1), custom_call_target="tpu_custom_call" | custom-call | tf_op jit(solution)/shard_map/filter/pallas_call | solution.py:230
  6.5 3.3 %collective-permute-start.4 = (f32[400,128]{1,0:T(8,128)}, f32[400,128]{1,0:T(8,128)S(1)}, u32[]{:S(2)}, u32[]{:S(2)}) collective-permute-start(f32[400,128]{1,0:T(8,128)} %get-tuple-element.13.own), channel_id=1, source_target_pairs={{0,1},{1,0},{2,3},{3,2},{4,5},{5,4},{6,7},{7,6},{8,9},{9,8},{10,11... | collective-permute-start | bytes 614408 | tf_op jit(solution)/shard_map/ppermute | solution.py:243
  9.8 0.0 collective-permute-start.5
  9.8 2.8 %collective-permute-start = (f32[400,128]{1,0:T(8,128)}, f32[400,128]{1,0:T(8,128)S(1)}, u32[]{:S(2)}, u32[]{:S(2)}) collective-permute-start(f32[400,128]{1,0:T(8,128)} %get-tuple-element.12.own), channel_id=1, source_target_pairs={{0,32},{32,0},{1,33},{33,1},{2,34},{34,2},{3,35},{35,3},{4,36},{36... | collective-permute-start | bytes 614408 | tf_op jit(solution)/shard_map/ppermute | solution.py:250
  12.7 0.1 add_convert_fusion.low
  12.8 0.7 copy-done.2
  13.4 0.0 copy-done.3
  13.4 0.7 bands.1
  14.2 0.0 collective-permute-done.4.near
  14.2 1.1 %collective-permute-done.5.far = f32[400,128]{1,0:T(8,128)S(1)} collective-permute-done((f32[400,128]{1,0:T(8,128)}, f32[400,128]{1,0:T(8,128)S(1)}, u32[]{:S(2)}, u32[]{:S(2)}) %collective-permute-start.5) | collective-permute-done | bytes 204832 | tf_op jit(solution)/shard_map/ppermute | solution.py:245
  15.2 0.9 copy-done.1
  16.2 0.6 lon.1.refs_4_
  16.8 1.3 %collective-permute-start.6 = (f32[400,128]{1,0:T(8,128)S(1)}, f32[400,128]{1,0:T(8,128)S(1)}, u32[]{:S(2)}, u32[]{:S(2)}) collective-permute-start(f32[400,128]{1,0:T(8,128)S(1)} %lon.1.refs_4_), channel_id=1, source_target_pairs={{0,32},{32,0},{1,33},{33,1},{2,34},{34,2},{3,35},{35,3},{4,36},{36... | collective-permute-start | bytes 614408 | tf_op jit(solution)/shard_map/ppermute | solution.py:250
  18.1 0.0 collective-permute-done.near
  18.1 3.1 %collective-permute-start.1 = (f32[400,128]{1,0:T(8,128)S(1)}, f32[400,128]{1,0:T(8,128)S(1)}, u32[]{:S(2)}, u32[]{:S(2)}) collective-permute-start(f32[400,128]{1,0:T(8,128)S(1)} %collective-permute-done.near), channel_id=1, source_target_pairs={{0,64},{64,128},{128,192},{96,32},{160,96},{224,160},{1,65},{65,12... | collective-permute-start | bytes 614408 | tf_op jit(solution)/shard_map/ppermute | solution.py:253
  21.2 2.9 %collective-permute-done.6.refs_3_ = f32[400,128]{1,0:T(8,128)S(1)} collective-permute-done((f32[400,128]{1,0:T(8,128)S(1)}, f32[400,128]{1,0:T(8,128)S(1)}, u32[]{:S(2)}, u32[]{:S(2)}) %collective-permute-start.6) | collective-permute-done | bytes 204832 | tf_op jit(solution)/shard_map/ppermute | solution.py:250
  24.1 3.3 %collective-permute-start.7 = (f32[400,128]{1,0:T(8,128)S(1)}, f32[400,128]{1,0:T(8,128)S(1)}, u32[]{:S(2)}, u32[]{:S(2)}) collective-permute-start(f32[400,128]{1,0:T(8,128)S(1)} %collective-permute-done.6.refs_3_), channel_id=1, source_target_pairs={{0,64},{64,128},{128,192},{96,32},{160,96},{224,160},{1,65},{65,12... | collective-permute-start | bytes 614408 | tf_op jit(solution)/shard_map/ppermute | solution.py:253
  27.4 0.6 lat.1.refs_1_
  28.1 5.3 %collective-permute-start.2 = (f32[400,128]{1,0:T(8,128)S(1)}, f32[400,128]{1,0:T(8,128)S(1)}, u32[]{:S(2)}, u32[]{:S(2)}) collective-permute-start(f32[400,128]{1,0:T(8,128)S(1)} %lat.1.refs_1_), channel_id=1, source_target_pairs={{0,1},{1,0},{2,3},{3,2},{4,5},{5,4},{6,7},{7,6},{8,9},{9,8},{10,11... | collective-permute-start | bytes 614408 | tf_op jit(solution)/shard_map/ppermute | solution.py:243
  33.4 0.0 collective-permute-start.3
  33.4 0.0 collective-permute-done.7.refs_5_
  33.4 1.1 %collective-permute-done.2.refs_0_ = f32[400,128]{1,0:T(8,128)S(1)} collective-permute-done((f32[400,128]{1,0:T(8,128)S(1)}, f32[400,128]{1,0:T(8,128)S(1)}, u32[]{:S(2)}, u32[]{:S(2)}) %collective-permute-start.2) | collective-permute-done | bytes 204832 | tf_op jit(solution)/shard_map/ppermute | solution.py:243
  34.5 4.4 %collective-permute-done.3.refs_2_ = f32[400,128]{1,0:T(8,128)S(1)} collective-permute-done((f32[400,128]{1,0:T(8,128)S(1)}, f32[400,128]{1,0:T(8,128)S(1)}, u32[]{:S(2)}, u32[]{:S(2)}) %collective-permute-start.3) | collective-permute-done | bytes 204832 | tf_op jit(solution)/shard_map/ppermute | solution.py:245
  38.9 2.3 %last.1 = (f32[2,400,128]{2,1,0:T(8,128)S(1)}, f32[256,256]{1,0:T(8,128)S(1)}) custom-call(f32[20]{0:T(128)S(1)} %cosine_sqrt_fusion.weights, f32[40,120]{1,0:T(8,128)S(1)} %get-tuple-element.9.band.lon_band, f32[40,120]{1,0:T(8,128)S(1)} %get-tuple-element.10.lat_band, f32[400,128]{1,0:T(8,128)S(1)} %collective-permute-done.2.refs_0_, ...), custom_call_target="tpu_custom_call" | custom-call | tf_op jit(solution)/shard_map/last/pallas_call | solution.py:230
  41.2 2.0 %collective-permute-start.8 = (f32[128,256]{1,0:T(8,128)S(1)}, f32[128,256]{1,0:T(8,128)S(1)}, u32[]{:S(2)}, u32[]{:S(2)}) collective-permute-start(f32[128,256]{1,0:T(8,128)S(1)} %constant_dynamic-slice_fusion), channel_id=1, source_target_pairs={{0,1},{1,0},{2,3},{3,2},{4,5},{5,4},{6,7},{7,6},{8,9},{9,8},{10,11... | collective-permute-start | bytes 393224 | tf_op jit(solution)/shard_map/ppermute | solution.py:32
  43.2 1.0 %collective-permute-done.8 = f32[128,256]{1,0:T(8,128)S(1)} collective-permute-done((f32[128,256]{1,0:T(8,128)S(1)}, f32[128,256]{1,0:T(8,128)S(1)}, u32[]{:S(2)}, u32[]{:S(2)}) %collective-permute-start.8) | collective-permute-done | bytes 131104 | tf_op jit(solution)/shard_map/ppermute | solution.py:32
  44.2 13.4 %all_to_all.15 = f32[16,8,256]{2,1,0:T(8,128)S(1)} all-to-all(f32[16,8,256]{2,1,0:T(8,128)S(1)} %add_bitcast_fusion), channel_id=1, replica_groups=mesh['x'=4,'yh'=2,'yl'=2,'z'=8,'core'=2] {'x','yh','yl'}, dimensions={0} | all-to-all | bytes 262144 | tf_op jit(solution)/shard_map/all_to_all | solution.py:34
  57.6 9.7 %all_to_all.16 = f32[8,8,256]{2,1,0:T(8,128)S(1)} all-to-all(f32[8,8,256]{2,1,0:T(8,128)S(1)} %broadcast_in_dim.24), channel_id=1, replica_groups=mesh['x'=4,'yh'=2,'yl'=2,'z'=8,'core'=2] {'z'}, dimensions={0} | all-to-all | bytes 131072 | tf_op jit(solution)/shard_map/all_to_all | solution.py:22
  67.4 10.0 %all_to_all.17 = f32[16,8,256]{2,1,0:T(8,128)S(1)} all-to-all(f32[16,8,256]{2,1,0:T(8,128)S(1)} %broadcast_in_dim.25), channel_id=1, replica_groups=mesh['x'=4,'yh'=2,'yl'=2,'z'=8,'core'=2] {'x','yh','yl'}, dimensions={0} | all-to-all | bytes 262144 | tf_op jit(solution)/shard_map/all_to_all | solution.py:22
  77.4 4.1 %collective-permute-start.9 = (f32[128,256]{1,0:T(8,128)S(1)}, f32[128,256]{1,0:T(8,128)S(1)}, u32[]{:S(2)}, u32[]{:S(2)}) collective-permute-start(f32[128,256]{1,0:T(8,128)S(1)} %bitcast.12), channel_id=1, source_target_pairs={{0,1},{1,0},{2,3},{3,2},{4,5},{5,4},{6,7},{7,6},{8,9},{9,8},{10,11... | collective-permute-start | bytes 393224 | tf_op jit(solution)/shard_map/ppermute | solution.py:37
  81.4 1.0 %collective-permute-done.9 = f32[128,256]{1,0:T(8,128)S(1)} collective-permute-done((f32[128,256]{1,0:T(8,128)S(1)}, f32[128,256]{1,0:T(8,128)S(1)}, u32[]{:S(2)}, u32[]{:S(2)}) %collective-permute-start.9) | collective-permute-done | bytes 131104 | tf_op jit(solution)/shard_map/ppermute | solution.py:37
  82.5 11.4 %factor.1 = (f32[20,20,256]{2,1,0:T(8,128)}, f32[256,256]{1,0:T(8,128)}) custom-call(f32[256,256]{1,0:T(8,128)S(1)} %pad_maximum_fusion.gram, f32[2,400,128]{2,1,0:T(8,128)S(1)} %get-tuple-element.15.matrix), custom_call_target="tpu_custom_call" | custom-call | tf_op jit(solution)/shard_map/factor/pallas_call | solution.py:230
  (15 shorter events, 0.2 us)
Async XLA Ops:
  6.5 7.7 %collective-permute-start.4 = (f32[400,128]{1,0:T(8,128)}, f32[400,128]{1,0:T(8,128)S(1)}, u32[]{:S(2)}, u32[]{:S(2)}) collective-permute-start(f32[400,128]{1,0:T(8,128)} %get-tuple-element.13.own), channel_id=1, source_target_pairs={{0,1},{1,0},{2,3},{3,2},{4,5},{5,4},{6,7},{7,6},{8,9},{9,8},{10,11... | collective-permute-start | bytes 614408 | tf_op jit(solution)/shard_map/ppermute | solution.py:243
  9.8 5.4 %collective-permute-start.5 = (f32[400,128]{1,0:T(8,128)}, f32[400,128]{1,0:T(8,128)S(1)}, u32[]{:S(2)}, u32[]{:S(2)}) collective-permute-start(f32[400,128]{1,0:T(8,128)} %get-tuple-element.13.own), channel_id=1, source_target_pairs={{1,2},{3,4},{5,6},{7,8},{9,10},{11,12},{13,14},{15,16},{17,18},{19... | collective-permute-start | bytes 614408 | tf_op jit(solution)/shard_map/ppermute | solution.py:245
  9.8 8.2 %collective-permute-start = (f32[400,128]{1,0:T(8,128)}, f32[400,128]{1,0:T(8,128)S(1)}, u32[]{:S(2)}, u32[]{:S(2)}) collective-permute-start(f32[400,128]{1,0:T(8,128)} %get-tuple-element.12.own), channel_id=1, source_target_pairs={{0,32},{32,0},{1,33},{33,1},{2,34},{34,2},{3,35},{35,3},{4,36},{36... | collective-permute-start | bytes 614408 | tf_op jit(solution)/shard_map/ppermute | solution.py:250
  12.8 0.7 copy-start.2
  12.8 0.7 copy-start.3
  15.2 0.9 copy-start.1
  16.2 11.3 %copy-start = (f32[400,128]{1,0:T(8,128)S(1)}, f32[400,128]{1,0:T(8,128)}, u32[]{:S(2)}) copy-start(f32[400,128]{1,0:T(8,128)} %get-tuple-element.12.own) | copy-start | bytes 614404
  16.8 7.3 %collective-permute-start.6 = (f32[400,128]{1,0:T(8,128)S(1)}, f32[400,128]{1,0:T(8,128)S(1)}, u32[]{:S(2)}, u32[]{:S(2)}) collective-permute-start(f32[400,128]{1,0:T(8,128)S(1)} %lon.1.refs_4_), channel_id=1, source_target_pairs={{0,32},{32,0},{1,33},{33,1},{2,34},{34,2},{3,35},{35,3},{4,36},{36... | collective-permute-start | bytes 614408 | tf_op jit(solution)/shard_map/ppermute | solution.py:250
  18.1 9.3 %collective-permute-start.1 = (f32[400,128]{1,0:T(8,128)S(1)}, f32[400,128]{1,0:T(8,128)S(1)}, u32[]{:S(2)}, u32[]{:S(2)}) collective-permute-start(f32[400,128]{1,0:T(8,128)S(1)} %collective-permute-done.near), channel_id=1, source_target_pairs={{0,64},{64,128},{128,192},{96,32},{160,96},{224,160},{1,65},{65,12... | collective-permute-start | bytes 614408 | tf_op jit(solution)/shard_map/ppermute | solution.py:253
  24.1 9.3 %collective-permute-start.7 = (f32[400,128]{1,0:T(8,128)S(1)}, f32[400,128]{1,0:T(8,128)S(1)}, u32[]{:S(2)}, u32[]{:S(2)}) collective-permute-start(f32[400,128]{1,0:T(8,128)S(1)} %collective-permute-done.6.refs_3_), channel_id=1, source_target_pairs={{0,64},{64,128},{128,192},{96,32},{160,96},{224,160},{1,65},{65,12... | collective-permute-start | bytes 614408 | tf_op jit(solution)/shard_map/ppermute | solution.py:253
  28.1 6.4 %collective-permute-start.2 = (f32[400,128]{1,0:T(8,128)S(1)}, f32[400,128]{1,0:T(8,128)S(1)}, u32[]{:S(2)}, u32[]{:S(2)}) collective-permute-start(f32[400,128]{1,0:T(8,128)S(1)} %lat.1.refs_1_), channel_id=1, source_target_pairs={{0,1},{1,0},{2,3},{3,2},{4,5},{5,4},{6,7},{7,6},{8,9},{9,8},{10,11... | collective-permute-start | bytes 614408 | tf_op jit(solution)/shard_map/ppermute | solution.py:243
  33.4 5.5 %collective-permute-start.3 = (f32[400,128]{1,0:T(8,128)S(1)}, f32[400,128]{1,0:T(8,128)S(1)}, u32[]{:S(2)}, u32[]{:S(2)}) collective-permute-start(f32[400,128]{1,0:T(8,128)S(1)} %lat.1.refs_1_), channel_id=1, source_target_pairs={{1,2},{3,4},{5,6},{7,8},{9,10},{11,12},{13,14},{15,16},{17,18},{19... | collective-permute-start | bytes 614408 | tf_op jit(solution)/shard_map/ppermute | solution.py:245
  41.2 3.0 %collective-permute-start.8 = (f32[128,256]{1,0:T(8,128)S(1)}, f32[128,256]{1,0:T(8,128)S(1)}, u32[]{:S(2)}, u32[]{:S(2)}) collective-permute-start(f32[128,256]{1,0:T(8,128)S(1)} %constant_dynamic-slice_fusion), channel_id=1, source_target_pairs={{0,1},{1,0},{2,3},{3,2},{4,5},{5,4},{6,7},{7,6},{8,9},{9,8},{10,11... | collective-permute-start | bytes 393224 | tf_op jit(solution)/shard_map/ppermute | solution.py:32
  77.4 5.1 %collective-permute-start.9 = (f32[128,256]{1,0:T(8,128)S(1)}, f32[128,256]{1,0:T(8,128)S(1)}, u32[]{:S(2)}, u32[]{:S(2)}) collective-permute-start(f32[128,256]{1,0:T(8,128)S(1)} %bitcast.12), channel_id=1, source_target_pairs={{0,1},{1,0},{2,3},{3,2},{4,5},{5,4},{6,7},{7,6},{8,9},{9,8},{10,11... | collective-permute-start | bytes 393224 | tf_op jit(solution)/shard_map/ppermute | solution.py:37

commit v7 on v6

--- a/solution.py
+++ b/solution.py
@@ -162,43 +162,28 @@
     return jnp.where(first == 1, swapped, plain)
 
 
-def bands_kernel(side, low, weights, lat_kernel, lon_kernel, lat_band, lon_band, lat_weighted):
-    lat_band[...] = ordered(low[0], lat_kernel, side)
-    lon_band[...] = ordered(low[1], lon_kernel, side)
-    row = lax.broadcasted_iota(jnp.int32, (2 * side, 1), 0)
-    weight = jnp.zeros((2 * side, 1), jnp.float32)
-    for line in range(side):
-        weight = jnp.where((row == line) | (row == side + line), weights[line], weight)
-    lat_weighted[...] = lat_band[...] * weight
-
-
-def filter_kernel(lines, taps, field, first, second, staged, padded, arrived):
+def filter_kernel(low, weights, taps, lat_kernel, lon_kernel, field, first, second, lat_band, lon_band, lat_weighted, padded):
     rows, cols, hours = field.shape
     stride = padded.shape[1]
-    parts = [pl.ds(row, lines) for row in range(0, rows, lines)]
-    copies = [
-        pltpu.make_async_copy(field.at[part], staged.at[part], arrived.at[at])
-        for at, part in enumerate(parts)
-    ]
-    for copy in copies:
-        copy.start()
-    padded[:, cols:, :] = jnp.zeros((rows, stride - cols, hours), jnp.float32)
     count = taps.shape[1]
     lane = lax.broadcasted_iota(jnp.int32, (1, count), 1)
     full = taps[...] + jnp.where(lane == TH, 1.0, 0.0)
     full = jnp.concatenate([full, jnp.zeros((1, hours - count), jnp.float32)], axis=1)
     skew = pltpu.roll(jnp.broadcast_to(full, (2 * TILE, hours)), 0, 1, stride=1, stride_axis=0)
-    for at, copy in enumerate(copies):
-        copy.wait()
-        part = slice(at * lines, (at + 1) * lines)
-        padded[part, :cols, :] = staged[part]
-        part = padded[part].reshape(lines * stride, hours)
-        result = product(part, skew, COLS)
-        for line in range(lines):
-            row = at * lines + line
-            value = result[line * stride : line * stride + cols]
-            turned(first, row, cols, value[:, :TILE])
-            second[row * cols : (row + 1) * cols, :] = value[:, TILE:]
+    padded[:, cols:, :] = jnp.zeros((rows, stride - cols, hours), jnp.float32)
+    padded[:, :cols, :] = field[...]
+    result = product(padded[...].reshape(rows * stride, hours), skew, COLS)
+    for row in range(rows):
+        value = result[row * stride : row * stride + cols]
+        turned(first, row, cols, value[:, :TILE])
+        second[row * cols : (row + 1) * cols, :] = value[:, TILE:]
+    lat_band[...] = ordered(low[0], lat_kernel, SH)
+    lon_band[...] = ordered(low[1], lon_kernel, SH)
+    row = lax.broadcasted_iota(jnp.int32, (2 * SH, 1), 0)
+    weight = jnp.zeros((2 * SH, 1), jnp.float32)
+    for line in range(SH):
+        weight = jnp.where((row == line) | (row == SH + line), weights[line], weight)
+    lat_weighted[...] = lat_band[...] * weight
 
 
 def smooth_kernel(side, band, near, own, far, out):
@@ -225,7 +210,7 @@
     gram[...] = product(both, both, ROWS)
 
 
-def called(kernel, name, shapes, spaces, scratch, *args, mib=24):
+def called(kernel, name, shapes, spaces, scratch, *args):
     spaces = list(spaces) + [pltpu.VMEM] * (len(args) - len(spaces))
     return pl.pallas_call(
         kernel,
@@ -233,7 +218,7 @@
         in_specs=[pl.BlockSpec(memory_space=space) for space in spaces],
         out_specs=[pl.BlockSpec(memory_space=pltpu.VMEM)] * len(shapes),
         scratch_shapes=scratch,
-        compiler_params=pltpu.CompilerParams(vmem_limit_bytes=mib * 1024 * 1024),
+        compiler_params=pltpu.CompilerParams(vmem_limit_bytes=24 * 1024 * 1024),
         name=name,
     )(*args)
 
@@ -265,33 +250,19 @@
     latitude = jnp.pi * (globrow + 0.5) / total_lat - jnp.pi / 2
     weights = jnp.sqrt(jnp.cos(latitude))
     half = (local, TILE)
-    lines = 4
-    first, second = called(
-        functools.partial(filter_kernel, lines),
+    low = jnp.stack([lax.axis_index("yh") == 0, lax.axis_index("core") == 0]).astype(jnp.int32)
+    first, second, lat_band, lon_band, lat_weighted = called(
+        filter_kernel,
         "filter",
-        [half, half],
-        [pltpu.VMEM, pltpu.HBM],
-        [
-            pltpu.VMEM((rows_lat, rows_lon, length_in), jnp.float32),
-            pltpu.VMEM((rows_lat, tall, length_in), jnp.float32),
-            pltpu.SemaphoreType.DMA((rows_lat // lines,)),
-        ],
-        time_taps[None],
-        field,
-        mib=56,
-    )
-    low = jnp.stack([lax.axis_index("yh") == 0, lax.axis_index("core") == 0]).astype(jnp.int32)
-    bands = [(2 * SH, 6 * SH)] * 3
-    lat_band, lon_band, lat_weighted = called(
-        functools.partial(bands_kernel, SH),
-        "bands",
-        bands,
+        [half, half] + [(2 * SH, 6 * SH)] * 3,
         [pltpu.SMEM] * 2,
-        [],
+        [pltpu.VMEM((rows_lat, tall, length_in), jnp.float32)],
         low,
         weights,
+        time_taps[None],
         lat_kernel[None],
         lon_kernel[None],
+        field,
     )
     smooth = functools.partial(smooth_kernel, SH)
     near, far = passed_on(first)

time: 94.2 us -> 91.1 us (0.967)
  Pallas kernels: 21.6 us -> 16.6 us
  waiting for transfers between devices: 11.4 us -> 14 us
    pallas_call x6 -> x5, Pallas kernels: 21.6 us -> 16.6 us  [called(): pl.pallas_call(kernel, out_shape=[jax.ShapeDtypeStruct(shape, jnp.float32...]
    ppermute x2, waiting for transfers between devices: 5.45 us -> 6.77 us  [around(): lax.ppermute(value, LON, across + [(j, i) for i, j in across])]
    all_to_all x1, blocking collectives: 13.4 us -> 12.1 us  [summed(): lax.all_to_all(kept.reshape(peers, half // peers, cols), PLANE, 0, 0)]
    ppermute x2, waiting for transfers between devices: 2.88 us -> 4.17 us  [passed_on(): near = lax.ppermute(value, 'yh', [(0, 1), (1, 0)])]
  transfers between devices with their start and end apart: 10 -> 10, of which waited for: 6 -> 7; matrix products, arithmetic and copies ran while one was open for 0% -> 0% of each run, Pallas kernels for 2% -> 1%
where the time goes in v7:
time: 91.1 us; the launch traced here: 90.8 us
  blocking collectives  32.4 us (36%)
  starting transfers between devices  25 us (27%)
  Pallas kernels  16.6 us (18%)
  waiting for transfers between devices  14 us (15%)
  local copies, waits for them, and re-layouts  1.85 us (2%)
    all_to_all x2, blocking collectives, shared(): return lax.all_to_all(copies, axes, 0, 0)  20.3 us
    pallas_call x5, Pallas kernels, called(): pl.pallas_call(kernel, out_shape=[jax.ShapeDtypeStruct(shape, jnp.float32...  16.6 us
    all_to_all x1, blocking collectives, summed(): lax.all_to_all(kept.reshape(peers, half // peers, cols), PLANE, 0, 0)  12.1 us
    ppermute x2, starting transfers between devices, around(): near = lax.ppermute(value, 'core', [(0, 1), (1, 0)])  8.66 us
    ppermute x2, waiting for transfers between devices, around(): lax.ppermute(value, LON, across + [(j, i) for i, j in across])  6.77 us
    ppermute x2, starting transfers between devices, passed_on(): return (near, lax.ppermute(near, LAT, up + down))  6.06 us
    ppermute x1, starting transfers between devices, summed(): given = lax.ppermute(kept, 'core', swap)  4.26 us
    ppermute x2, waiting for transfers between devices, passed_on(): near = lax.ppermute(value, 'yh', [(0, 1), (1, 0)])  4.17 us
  transfers between devices with their start and end apart: 10, of which 7 were waited for; matrix products, arithmetic and copies ran while one was open for 0% of the time, Pallas kernels for 1%

profile of v7, /device:TPU:1, one launch (start us, length us, event | category | flops | bytes accessed | tf_op | source)
XLA Modules:
  0.0 90.8 jit_solution(2868635507786019683)
XLA Ops:
  0.7 0.1 add_convert_fusion.low
  0.8 0.7 copy-done.3
  1.4 0.0 copy-done.1
  1.5 1.1 %copy-done = f32[20,20,384]{2,1,0:T(8,128)S(1)} copy-done((f32[20,20,384]{2,1,0:T(8,128)S(1)}, f32[20,20,384]{2,1,0:T(8,128)}, u32[]{:S(2)}) %copy-start) | copy-done | bytes 614424
  2.6 1.6 %filter.1 = (f32[400,128]{1,0:T(8,128)S(1)}, f32[400,128]{1,0:T(8,128)S(1)}, f32[40,120]{1,0:T(8,128)S(1)}, f32[40,120]{1,0:T(8,128)S(1)}, f32[40,120]{1,0:T(8,128)S(1)}) custom-call(s32[2]{0:T(128)S(1)} %add_convert_fusion.low, f32[20]{0:T(128)S(1)} %cosine_sqrt_fusion.weights, f32[1,129]{1,0:T(1,128)S(1)} %bitcast.10, f32[1,41]{1,0:T(1,128)S(1)} %bitcast.11, ...), custom_call_target="tpu_custom_call" | custom-call | tf_op jit(solution)/shard_map/filter/pallas_call | solution.py:215
  4.2 3.3 %collective-permute-start.4 = (f32[400,128]{1,0:T(8,128)S(1)}, f32[400,128]{1,0:T(8,128)S(1)}, u32[]{:S(2)}, u32[]{:S(2)}) collective-permute-start(f32[400,128]{1,0:T(8,128)S(1)} %get-tuple-element.13.own), channel_id=1, source_target_pairs={{0,1},{1,0},{2,3},{3,2},{4,5},{5,4},{6,7},{7,6},{8,9},{9,8},{10,11... | collective-permute-start | bytes 614408 | tf_op jit(solution)/shard_map/ppermute | solution.py:228
  7.5 0.0 collective-permute-start.5
  7.5 2.8 %collective-permute-start = (f32[400,128]{1,0:T(8,128)S(1)}, f32[400,128]{1,0:T(8,128)S(1)}, u32[]{:S(2)}, u32[]{:S(2)}) collective-permute-start(f32[400,128]{1,0:T(8,128)S(1)} %get-tuple-element.12.own), channel_id=1, source_target_pairs={{0,32},{32,0},{1,33},{33,1},{2,34},{34,2},{3,35},{35,3},{4,36},{36... | collective-permute-start | bytes 614408 | tf_op jit(solution)/shard_map/ppermute | solution.py:235
  10.3 0.0 collective-permute-done.4.near
  10.3 2.4 %collective-permute-done.5.far = f32[400,128]{1,0:T(8,128)S(1)} collective-permute-done((f32[400,128]{1,0:T(8,128)S(1)}, f32[400,128]{1,0:T(8,128)S(1)}, u32[]{:S(2)}, u32[]{:S(2)}) %collective-permute-start.5) | collective-permute-done | bytes 204832 | tf_op jit(solution)/shard_map/ppermute | solution.py:230
  12.7 0.6 lon.1.refs_4_
  13.3 1.3 %collective-permute-start.6 = (f32[400,128]{1,0:T(8,128)S(1)}, f32[400,128]{1,0:T(8,128)S(1)}, u32[]{:S(2)}, u32[]{:S(2)}) collective-permute-start(f32[400,128]{1,0:T(8,128)S(1)} %lon.1.refs_4_), channel_id=1, source_target_pairs={{0,32},{32,0},{1,33},{33,1},{2,34},{34,2},{3,35},{35,3},{4,36},{36... | collective-permute-start | bytes 614408 | tf_op jit(solution)/shard_map/ppermute | solution.py:235
  14.6 0.6 collective-permute-done.near
  15.2 3.1 %collective-permute-start.1 = (f32[400,128]{1,0:T(8,128)S(1)}, f32[400,128]{1,0:T(8,128)S(1)}, u32[]{:S(2)}, u32[]{:S(2)}) collective-permute-start(f32[400,128]{1,0:T(8,128)S(1)} %collective-permute-done.near), channel_id=1, source_target_pairs={{0,64},{64,128},{128,192},{96,32},{160,96},{224,160},{1,65},{65,12... | collective-permute-start | bytes 614408 | tf_op jit(solution)/shard_map/ppermute | solution.py:238
  18.3 3.6 %collective-permute-done.6.refs_3_ = f32[400,128]{1,0:T(8,128)S(1)} collective-permute-done((f32[400,128]{1,0:T(8,128)S(1)}, f32[400,128]{1,0:T(8,128)S(1)}, u32[]{:S(2)}, u32[]{:S(2)}) %collective-permute-start.6) | collective-permute-done | bytes 204832 | tf_op jit(solution)/shard_map/ppermute | solution.py:235
  21.9 2.9 %collective-permute-start.7 = (f32[400,128]{1,0:T(8,128)S(1)}, f32[400,128]{1,0:T(8,128)S(1)}, u32[]{:S(2)}, u32[]{:S(2)}) collective-permute-start(f32[400,128]{1,0:T(8,128)S(1)} %collective-permute-done.6.refs_3_), channel_id=1, source_target_pairs={{0,64},{64,128},{128,192},{96,32},{160,96},{224,160},{1,65},{65,12... | collective-permute-start | bytes 614408 | tf_op jit(solution)/shard_map/ppermute | solution.py:238
  24.8 0.0 collective-permute-done.1.far
  24.9 0.6 lat.1.refs_1_
  25.5 5.3 %collective-permute-start.2 = (f32[400,128]{1,0:T(8,128)S(1)}, f32[400,128]{1,0:T(8,128)S(1)}, u32[]{:S(2)}, u32[]{:S(2)}) collective-permute-start(f32[400,128]{1,0:T(8,128)S(1)} %lat.1.refs_1_), channel_id=1, source_target_pairs={{0,1},{1,0},{2,3},{3,2},{4,5},{5,4},{6,7},{7,6},{8,9},{9,8},{10,11... | collective-permute-start | bytes 614408 | tf_op jit(solution)/shard_map/ppermute | solution.py:228
  30.8 0.0 collective-permute-start.3
  30.8 0.0 collective-permute-done.7.refs_5_
  30.8 1.1 %collective-permute-done.2.refs_0_ = f32[400,128]{1,0:T(8,128)S(1)} collective-permute-done((f32[400,128]{1,0:T(8,128)S(1)}, f32[400,128]{1,0:T(8,128)S(1)}, u32[]{:S(2)}, u32[]{:S(2)}) %collective-permute-start.2) | collective-permute-done | bytes 204832 | tf_op jit(solution)/shard_map/ppermute | solution.py:228
  31.9 4.4 %collective-permute-done.3.refs_2_ = f32[400,128]{1,0:T(8,128)S(1)} collective-permute-done((f32[400,128]{1,0:T(8,128)S(1)}, f32[400,128]{1,0:T(8,128)S(1)}, u32[]{:S(2)}, u32[]{:S(2)}) %collective-permute-start.3) | collective-permute-done | bytes 204832 | tf_op jit(solution)/shard_map/ppermute | solution.py:230
  36.3 2.3 %last.1 = (f32[2,400,128]{2,1,0:T(8,128)S(1)}, f32[256,256]{1,0:T(8,128)S(1)}) custom-call(f32[20]{0:T(128)S(1)} %cosine_sqrt_fusion.weights, f32[40,120]{1,0:T(8,128)S(1)} %get-tuple-element.9.band.lon_band, f32[40,120]{1,0:T(8,128)S(1)} %get-tuple-element.10.lat_band, f32[400,128]{1,0:T(8,128)S(1)} %collective-permute-done.2.refs_0_, ...), custom_call_target="tpu_custom_call" | custom-call | tf_op jit(solution)/shard_map/last/pallas_call | solution.py:215
  38.6 2.0 %collective-permute-start.8 = (f32[128,256]{1,0:T(8,128)S(1)}, f32[128,256]{1,0:T(8,128)S(1)}, u32[]{:S(2)}, u32[]{:S(2)}) collective-permute-start(f32[128,256]{1,0:T(8,128)S(1)} %constant_dynamic-slice_fusion), channel_id=1, source_target_pairs={{0,1},{1,0},{2,3},{3,2},{4,5},{5,4},{6,7},{7,6},{8,9},{9,8},{10,11... | collective-permute-start | bytes 393224 | tf_op jit(solution)/shard_map/ppermute | solution.py:32
  40.6 1.0 %collective-permute-done.8 = f32[128,256]{1,0:T(8,128)S(1)} collective-permute-done((f32[128,256]{1,0:T(8,128)S(1)}, f32[128,256]{1,0:T(8,128)S(1)}, u32[]{:S(2)}, u32[]{:S(2)}) %collective-permute-start.8) | collective-permute-done | bytes 131104 | tf_op jit(solution)/shard_map/ppermute | solution.py:32
  41.6 12.1 %all_to_all.15 = f32[16,8,256]{2,1,0:T(8,128)S(1)} all-to-all(f32[16,8,256]{2,1,0:T(8,128)S(1)} %add_bitcast_fusion), channel_id=1, replica_groups=mesh['x'=4,'yh'=2,'yl'=2,'z'=8,'core'=2] {'x','yh','yl'}, dimensions={0} | all-to-all | bytes 262144 | tf_op jit(solution)/shard_map/all_to_all | solution.py:34
  53.7 10.1 %all_to_all.16 = f32[8,8,256]{2,1,0:T(8,128)S(1)} all-to-all(f32[8,8,256]{2,1,0:T(8,128)S(1)} %broadcast_in_dim.24), channel_id=1, replica_groups=mesh['x'=4,'yh'=2,'yl'=2,'z'=8,'core'=2] {'z'}, dimensions={0} | all-to-all | bytes 131072 | tf_op jit(solution)/shard_map/all_to_all | solution.py:22
  63.9 10.2 %all_to_all.17 = f32[16,8,256]{2,1,0:T(8,128)S(1)} all-to-all(f32[16,8,256]{2,1,0:T(8,128)S(1)} %broadcast_in_dim.25), channel_id=1, replica_groups=mesh['x'=4,'yh'=2,'yl'=2,'z'=8,'core'=2] {'x','yh','yl'}, dimensions={0} | all-to-all | bytes 262144 | tf_op jit(solution)/shard_map/all_to_all | solution.py:22
  74.1 4.3 %collective-permute-start.9 = (f32[128,256]{1,0:T(8,128)S(1)}, f32[128,256]{1,0:T(8,128)S(1)}, u32[]{:S(2)}, u32[]{:S(2)}) collective-permute-start(f32[128,256]{1,0:T(8,128)S(1)} %bitcast.13), channel_id=1, source_target_pairs={{0,1},{1,0},{2,3},{3,2},{4,5},{5,4},{6,7},{7,6},{8,9},{9,8},{10,11... | collective-permute-start | bytes 393224 | tf_op jit(solution)/shard_map/ppermute | solution.py:37
  78.3 1.0 %collective-permute-done.9 = f32[128,256]{1,0:T(8,128)S(1)} collective-permute-done((f32[128,256]{1,0:T(8,128)S(1)}, f32[128,256]{1,0:T(8,128)S(1)}, u32[]{:S(2)}, u32[]{:S(2)}) %collective-permute-start.9) | collective-permute-done | bytes 131104 | tf_op jit(solution)/shard_map/ppermute | solution.py:37
  79.4 11.4 %factor.1 = (f32[20,20,256]{2,1,0:T(8,128)}, f32[256,256]{1,0:T(8,128)}) custom-call(f32[256,256]{1,0:T(8,128)S(1)} %pad_maximum_fusion.gram, f32[2,400,128]{2,1,0:T(8,128)S(1)} %get-tuple-element.15.matrix), custom_call_target="tpu_custom_call" | custom-call | tf_op jit(solution)/shard_map/factor/pallas_call | solution.py:215
  (14 shorter events, 0.2 us)
Async XLA Ops:
  0.8 0.7 copy-start.3
  0.8 0.7 copy-start.1
  0.8 0.7 copy-start.2
  1.5 1.1 %copy-start = (f32[20,20,384]{2,1,0:T(8,128)S(1)}, f32[20,20,384]{2,1,0:T(8,128)}, u32[]{:S(2)}) copy-start(f32[20,20,384]{2,1,0:T(8,128)} %field.1) | copy-start | bytes 1843204
  4.2 6.1 %collective-permute-start.4 = (f32[400,128]{1,0:T(8,128)S(1)}, f32[400,128]{1,0:T(8,128)S(1)}, u32[]{:S(2)}, u32[]{:S(2)}) collective-permute-start(f32[400,128]{1,0:T(8,128)S(1)} %get-tuple-element.13.own), channel_id=1, source_target_pairs={{0,1},{1,0},{2,3},{3,2},{4,5},{5,4},{6,7},{7,6},{8,9},{9,8},{10,11... | collective-permute-start | bytes 614408 | tf_op jit(solution)/shard_map/ppermute | solution.py:228
  7.5 5.2 %collective-permute-start.5 = (f32[400,128]{1,0:T(8,128)S(1)}, f32[400,128]{1,0:T(8,128)S(1)}, u32[]{:S(2)}, u32[]{:S(2)}) collective-permute-start(f32[400,128]{1,0:T(8,128)S(1)} %get-tuple-element.13.own), channel_id=1, source_target_pairs={{1,2},{3,4},{5,6},{7,8},{9,10},{11,12},{13,14},{15,16},{17,18},{19... | collective-permute-start | bytes 614408 | tf_op jit(solution)/shard_map/ppermute | solution.py:230
  7.5 7.7 %collective-permute-start = (f32[400,128]{1,0:T(8,128)S(1)}, f32[400,128]{1,0:T(8,128)S(1)}, u32[]{:S(2)}, u32[]{:S(2)}) collective-permute-start(f32[400,128]{1,0:T(8,128)S(1)} %get-tuple-element.12.own), channel_id=1, source_target_pairs={{0,32},{32,0},{1,33},{33,1},{2,34},{34,2},{3,35},{35,3},{4,36},{36... | collective-permute-start | bytes 614408 | tf_op jit(solution)/shard_map/ppermute | solution.py:235
  13.3 8.6 %collective-permute-start.6 = (f32[400,128]{1,0:T(8,128)S(1)}, f32[400,128]{1,0:T(8,128)S(1)}, u32[]{:S(2)}, u32[]{:S(2)}) collective-permute-start(f32[400,128]{1,0:T(8,128)S(1)} %lon.1.refs_4_), channel_id=1, source_target_pairs={{0,32},{32,0},{1,33},{33,1},{2,34},{34,2},{3,35},{35,3},{4,36},{36... | collective-permute-start | bytes 614408 | tf_op jit(solution)/shard_map/ppermute | solution.py:235
  15.2 9.6 %collective-permute-start.1 = (f32[400,128]{1,0:T(8,128)S(1)}, f32[400,128]{1,0:T(8,128)S(1)}, u32[]{:S(2)}, u32[]{:S(2)}) collective-permute-start(f32[400,128]{1,0:T(8,128)S(1)} %collective-permute-done.near), channel_id=1, source_target_pairs={{0,64},{64,128},{128,192},{96,32},{160,96},{224,160},{1,65},{65,12... | collective-permute-start | bytes 614408 | tf_op jit(solution)/shard_map/ppermute | solution.py:238
  21.9 8.9 %collective-permute-start.7 = (f32[400,128]{1,0:T(8,128)S(1)}, f32[400,128]{1,0:T(8,128)S(1)}, u32[]{:S(2)}, u32[]{:S(2)}) collective-permute-start(f32[400,128]{1,0:T(8,128)S(1)} %collective-permute-done.6.refs_3_), channel_id=1, source_target_pairs={{0,64},{64,128},{128,192},{96,32},{160,96},{224,160},{1,65},{65,12... | collective-permute-start | bytes 614408 | tf_op jit(solution)/shard_map/ppermute | solution.py:238
  25.5 6.4 %collective-permute-start.2 = (f32[400,128]{1,0:T(8,128)S(1)}, f32[400,128]{1,0:T(8,128)S(1)}, u32[]{:S(2)}, u32[]{:S(2)}) collective-permute-start(f32[400,128]{1,0:T(8,128)S(1)} %lat.1.refs_1_), channel_id=1, source_target_pairs={{0,1},{1,0},{2,3},{3,2},{4,5},{5,4},{6,7},{7,6},{8,9},{9,8},{10,11... | collective-permute-start | bytes 614408 | tf_op jit(solution)/shard_map/ppermute | solution.py:228
  30.8 5.5 %collective-permute-start.3 = (f32[400,128]{1,0:T(8,128)S(1)}, f32[400,128]{1,0:T(8,128)S(1)}, u32[]{:S(2)}, u32[]{:S(2)}) collective-permute-start(f32[400,128]{1,0:T(8,128)S(1)} %lat.1.refs_1_), channel_id=1, source_target_pairs={{1,2},{3,4},{5,6},{7,8},{9,10},{11,12},{13,14},{15,16},{17,18},{19... | collective-permute-start | bytes 614408 | tf_op jit(solution)/shard_map/ppermute | solution.py:230
  38.6 3.0 %collective-permute-start.8 = (f32[128,256]{1,0:T(8,128)S(1)}, f32[128,256]{1,0:T(8,128)S(1)}, u32[]{:S(2)}, u32[]{:S(2)}) collective-permute-start(f32[128,256]{1,0:T(8,128)S(1)} %constant_dynamic-slice_fusion), channel_id=1, source_target_pairs={{0,1},{1,0},{2,3},{3,2},{4,5},{5,4},{6,7},{7,6},{8,9},{9,8},{10,11... | collective-permute-start | bytes 393224 | tf_op jit(solution)/shard_map/ppermute | solution.py:32
  74.1 5.2 %collective-permute-start.9 = (f32[128,256]{1,0:T(8,128)S(1)}, f32[128,256]{1,0:T(8,128)S(1)}, u32[]{:S(2)}, u32[]{:S(2)}) collective-permute-start(f32[128,256]{1,0:T(8,128)S(1)} %bitcast.13), channel_id=1, source_target_pairs={{0,1},{1,0},{2,3},{3,2},{4,5},{5,4},{6,7},{7,6},{8,9},{9,8},{10,11... | collective-permute-start | bytes 393224 | tf_op jit(solution)/shard_map/ppermute | solution.py:37

commit v8 on v7

--- a/solution.py
+++ b/solution.py
@@ -13,7 +13,7 @@
 LON = ("yl", "z", "core")
 
 
-PLANE = ("x", "yh", "yl")
+PLANE = ("x", "yh", "yl", "core")
 
 
 def shared(value, axes):
@@ -23,25 +23,15 @@
 
 
 def summed(value):
-    swap = [(0, 1), (1, 0)]
-    core = lax.axis_index("core")
-    rows, cols = value.shape
-    half = rows // 2
-    kept = lax.dynamic_slice_in_dim(value, core * half, half, 0)
-    given = lax.dynamic_slice_in_dim(value, (1 - core) * half, half, 0)
-    kept = kept + lax.ppermute(given, "core", swap)
     peers = lax.axis_size(PLANE)
-    pieces = lax.all_to_all(kept.reshape(peers, half // peers, cols), PLANE, 0, 0)
+    pieces = lax.all_to_all(value.reshape(peers, 1, value.size // peers), PLANE, 0, 0)
     piece = shared(pieces.sum(axis=0), ("z",)).sum(axis=0)
-    kept = shared(piece, PLANE).reshape(half, cols)
-    given = lax.ppermute(kept, "core", swap)
-    top = jnp.where(core == 0, kept, given)
-    bottom = jnp.where(core == 0, given, kept)
-    return jnp.concatenate([top, bottom], axis=0)
+    return shared(piece, PLANE).reshape(value.shape)
 
 
 TILE = 128
 STEP = 8
+PACK = TILE // 2
 
 def product(left, right, over):
     return lax.dot_general(
@@ -110,9 +100,11 @@
         lower = jnp.where(row >= col, work[:, TILE:], 0.0)
         return upper, lower
 
-    r11, w11 = solve(gram[:TILE, :TILE])
-    r12 = product(w11, gram[:TILE, TILE:], PLAIN)
-    r22, w22 = solve(gram[TILE:, TILE:] - product(r12, r12, ROWS))
+    blocks = [gram[at * PACK : (at + 1) * PACK, :] for at in range(5)]
+    r11, w11 = solve(mirrored(blocks[0], blocks[4]))
+    r12 = product(w11, jnp.concatenate(blocks[1:3], axis=0), PLAIN)
+    a22 = mirrored(blocks[3], pltpu.roll(blocks[4], PACK, 1))
+    r22, w22 = solve(a22 - product(r12, r12, ROWS))
     w21 = -product(w22, product(r12, w11, ROWS), PLAIN)
     merged[:TILE, :TILE] = r11 * (1.0 / scale)
     merged[:TILE, TILE:] = r12 * (1.0 / scale)
@@ -162,21 +154,33 @@
     return jnp.where(first == 1, swapped, plain)
 
 
-def filter_kernel(low, weights, taps, lat_kernel, lon_kernel, field, first, second, lat_band, lon_band, lat_weighted, padded):
-    rows, cols, hours = field.shape
-    stride = padded.shape[1]
+def filtered(taps, field, padded, start):
+    rows, cols, hours = padded.shape
+    side = field.shape[1]
     count = taps.shape[1]
     lane = lax.broadcasted_iota(jnp.int32, (1, count), 1)
     full = taps[...] + jnp.where(lane == TH, 1.0, 0.0)
     full = jnp.concatenate([full, jnp.zeros((1, hours - count), jnp.float32)], axis=1)
-    skew = pltpu.roll(jnp.broadcast_to(full, (2 * TILE, hours)), 0, 1, stride=1, stride_axis=0)
-    padded[:, cols:, :] = jnp.zeros((rows, stride - cols, hours), jnp.float32)
-    padded[:, :cols, :] = field[...]
-    result = product(padded[...].reshape(rows * stride, hours), skew, COLS)
+    skew = pltpu.roll(jnp.broadcast_to(full, (TILE, hours)), 0, 1, stride=1, stride_axis=0)
+    padded[:, side:, :] = jnp.zeros((rows, cols - side, hours), jnp.float32)
+    padded[:, :side, :] = field[:, :, start : start + hours]
+    return product(padded[...].reshape(rows * cols, hours), skew, COLS)
+
+
+def early_kernel(taps, field, out, padded):
+    rows, side, _ = field.shape
+    result = filtered(taps, field, padded, 0)
     for row in range(rows):
-        value = result[row * stride : row * stride + cols]
-        turned(first, row, cols, value[:, :TILE])
-        second[row * cols : (row + 1) * cols, :] = value[:, TILE:]
+        at = row * padded.shape[1]
+        turned(out, row, side, result[at : at + side])
+
+
+def late_kernel(low, weights, taps, lat_kernel, lon_kernel, field, out, lat_band, lon_band, lat_weighted, padded):
+    rows, side, _ = field.shape
+    result = filtered(taps, field, padded, TILE)
+    for row in range(rows):
+        at = row * padded.shape[1]
+        out[row * side : (row + 1) * side, :] = result[at : at + side]
     lat_band[...] = ordered(low[0], lat_kernel, SH)
     lon_band[...] = ordered(low[1], lon_kernel, SH)
     row = lax.broadcasted_iota(jnp.int32, (2 * SH, 1), 0)
@@ -192,6 +196,18 @@
         result = product(band[...], stacked(near, own, far, first, pair), PLAIN)
         for line in range(2):
             turned(out, first // side + line, side, result[line * side : (line + 1) * side])
+
+
+def packed_corner(first, second):
+    lane = lax.broadcasted_iota(jnp.int32, (PACK, TILE), 1)
+    return jnp.where(lane < PACK, pltpu.roll(second[PACK:], PACK, 1), first[PACK:])
+
+
+def mirrored(top, corner):
+    row = lax.broadcasted_iota(jnp.int32, (TILE, TILE), 0)
+    lane = lax.broadcasted_iota(jnp.int32, (TILE, TILE), 1)
+    upper = jnp.concatenate([top, corner], axis=0)
+    return jnp.where((row >= PACK) & (lane < PACK), upper.T, upper)
 
 
 def last_kernel(side, weights, lon_band, lat_band, *refs):
@@ -206,8 +222,13 @@
         result = product(lat_band[...], stacked(*parts[3:], first, pair), PLAIN)
         for at in range(2):
             turned(out.at[1], line + at, side, result[at * side : (at + 1) * side])
-    both = jnp.concatenate([out[0], out[1]], axis=1)
-    gram[...] = product(both, both, ROWS)
+    early, late = (out[0], out[1])
+    first = product(early, early, ROWS)
+    cross = product(early, late, ROWS)
+    second = product(late, late, ROWS)
+    packed = packed_corner(first, second)
+    for at, block in enumerate((first[:PACK], cross[:PACK], cross[PACK:], second[:PACK], packed)):
+        gram[at * PACK : (at + 1) * PACK, :] = block
 
 
 def called(kernel, name, shapes, spaces, scratch, *args):
@@ -251,12 +272,14 @@
     weights = jnp.sqrt(jnp.cos(latitude))
     half = (local, TILE)
     low = jnp.stack([lax.axis_index("yh") == 0, lax.axis_index("core") == 0]).astype(jnp.int32)
-    first, second, lat_band, lon_band, lat_weighted = called(
-        filter_kernel,
-        "filter",
-        [half, half] + [(2 * SH, 6 * SH)] * 3,
+    padded = [pltpu.VMEM((rows_lat, tall, 2 * TILE), jnp.float32)]
+    (first,) = called(early_kernel, "early", [half], [], padded, time_taps[None], field)
+    second, lat_band, lon_band, lat_weighted = called(
+        late_kernel,
+        "late",
+        [half] + [(2 * SH, 6 * SH)] * 3,
         [pltpu.SMEM] * 2,
-        [pltpu.VMEM((rows_lat, tall, length_in), jnp.float32)],
+        padded,
         low,
         weights,
         time_taps[None],
@@ -274,7 +297,7 @@
     matrix, local_gram = called(
         functools.partial(last_kernel, SH),
         "last",
-        [(2,) + half, (steps_out, steps_out)],
+        [(2,) + half, (5 * PACK, TILE)],
         [pltpu.SMEM],
         [],
         weights,

time: 91.1 us -> 88.8 us (0.975)
  blocking collectives: 32.4 us -> 41.2 us
  starting transfers between devices: 25 us -> 17.9 us
  waiting for transfers between devices: 14 us -> 8.8 us
    ppermute x2, waiting for transfers between devices: 0.01 us -> 6.91 us  [passed_on(): return (near, lax.ppermute(near, LAT, up + down))]
    ppermute x2, waiting for transfers between devices: 6.77 us -> 0.01 us  [around(): lax.ppermute(value, LON, across + [(j, i) for i, j in across])]
    ppermute x2 -> x0, starting transfers between devices: 6.26 us -> none  [the longest x1 4.26 us: summed(): given = lax.ppermute(kept, 'core', swap)]
    all_to_all x1, blocking collectives: 12.1 us -> 16.9 us  [summed(): lax.all_to_all(value.reshape(peers, 1, value.size // peers), PLANE, 0, 0)]
    all_to_all x2, blocking collectives: 20.3 us -> 24.3 us  [shared(): return lax.all_to_all(copies, axes, 0, 0)]
    ppermute x2, starting transfers between devices: 8.66 us -> 5.15 us  [around(): near = lax.ppermute(value, 'core', [(0, 1), (1, 0)])]
    ppermute x2, starting transfers between devices: 0.01 us -> 2.66 us  [around(): lax.ppermute(value, LON, across + [(j, i) for i, j in across])]
    ppermute x2, waiting for transfers between devices: 4.17 us -> 1.87 us  [passed_on(): near = lax.ppermute(value, 'yh', [(0, 1), (1, 0)])]
  transfers between devices with their start and end apart: 10 -> 8, of which waited for: 7 -> 3; matrix products, arithmetic and copies ran while one was open for 0% -> 0% of each run, Pallas kernels for 1% -> 3%
where the time goes in v8:
time: 88.8 us; the launch traced here: 88.4 us
  blocking collectives  41.2 us (46%)
  starting transfers between devices  17.9 us (20%)
  Pallas kernels  16.9 us (19%)
  waiting for transfers between devices  8.8 us (10%)
  local copies, waits for them, and re-layouts  2.57 us (3%)
    all_to_all x2, blocking collectives, shared(): return lax.all_to_all(copies, axes, 0, 0)  24.3 us
    all_to_all x1, blocking collectives, summed(): lax.all_to_all(value.reshape(peers, 1, value.size // peers), PLANE, 0, 0)  16.9 us
    pallas_call x6, Pallas kernels, called(): pl.pallas_call(kernel, out_shape=[jax.ShapeDtypeStruct(shape, jnp.float32...  16.9 us
    ppermute x2, waiting for transfers between devices, passed_on(): return (near, lax.ppermute(near, LAT, up + down))  6.91 us
    ppermute x2, starting transfers between devices, passed_on(): return (near, lax.ppermute(near, LAT, up + down))  6.21 us
    ppermute x2, starting transfers between devices, around(): near = lax.ppermute(value, 'core', [(0, 1), (1, 0)])  5.15 us
    ppermute x2, starting transfers between devices, passed_on(): near = lax.ppermute(value, 'yh', [(0, 1), (1, 0)])  3.92 us
    ppermute x2, starting transfers between devices, around(): lax.ppermute(value, LON, across + [(j, i) for i, j in across])  2.66 us
  transfers between devices with their start and end apart: 8, of which 3 were waited for; matrix products, arithmetic and copies ran while one was open for 0% of the time, Pallas kernels for 3%

profile of v8, /device:TPU:1, one launch (start us, length us, event | category | flops | bytes accessed | tf_op | source)
XLA Modules:
  0.0 88.4 jit_solution(13291285499824359308)
XLA Ops:
  0.6 0.7 copy-done.2
  1.3 1.1 %copy-done = f32[20,20,384]{2,1,0:T(8,128)S(1)} copy-done((f32[20,20,384]{2,1,0:T(8,128)S(1)}, f32[20,20,384]{2,1,0:T(8,128)}, u32[]{:S(2)}) %copy-start) | copy-done | bytes 614424
  2.4 0.6 early.1.own
  3.1 3.8 %collective-permute-start = (f32[400,128]{1,0:T(8,128)S(1)}, f32[400,128]{1,0:T(8,128)S(1)}, u32[]{:S(2)}, u32[]{:S(2)}) collective-permute-start(f32[400,128]{1,0:T(8,128)S(1)} %early.1.own), channel_id=1, source_target_pairs={{0,32},{32,0},{1,33},{33,1},{2,34},{34,2},{3,35},{35,3},{4,36},{36... | collective-permute-start | bytes 614408 | tf_op jit(solution)/shard_map/ppermute | solution.py:256
  6.9 0.1 add_convert_fusion.low
  7.0 0.7 copy-done.3
  7.7 0.0 copy-done.4
  7.7 1.2 %late.1 = (f32[400,128]{1,0:T(8,128)S(1)}, f32[40,120]{1,0:T(8,128)S(1)}, f32[40,120]{1,0:T(8,128)S(1)}, f32[40,120]{1,0:T(8,128)S(1)}) custom-call(s32[2]{0:T(128)S(1)} %add_convert_fusion.low, f32[20]{0:T(128)S(1)} %cosine_sqrt_fusion.weights, f32[1,129]{1,0:T(1,128)S(1)} %bitcast.10, f32[1,41]{1,0:T(1,128)S(1)} %bitcast.11, f32[1,41]{1,0:T(1,128)S(1)} %bitcast.12, ...), custom_call_target="tpu_custom_call" | custom-call | tf_op jit(solution)/shard_map/late/pallas_call | solution.py:236
  8.9 2.6 %collective-permute-start.5 = (f32[400,128]{1,0:T(8,128)S(1)}, f32[400,128]{1,0:T(8,128)S(1)}, u32[]{:S(2)}, u32[]{:S(2)}) collective-permute-start(f32[400,128]{1,0:T(8,128)S(1)} %get-tuple-element.11.own), channel_id=1, source_target_pairs={{1,2},{3,4},{5,6},{7,8},{9,10},{11,12},{13,14},{15,16},{17,18},{19... | collective-permute-start | bytes 614408 | tf_op jit(solution)/shard_map/ppermute | solution.py:251
  11.4 3.6 %collective-permute-start.4 = (f32[400,128]{1,0:T(8,128)S(1)}, f32[400,128]{1,0:T(8,128)S(1)}, u32[]{:S(2)}, u32[]{:S(2)}) collective-permute-start(f32[400,128]{1,0:T(8,128)S(1)} %get-tuple-element.11.own), channel_id=1, source_target_pairs={{0,1},{1,0},{2,3},{3,2},{4,5},{5,4},{6,7},{7,6},{8,9},{9,8},{10,11... | collective-permute-start | bytes 614408 | tf_op jit(solution)/shard_map/ppermute | solution.py:249
  15.1 0.0 collective-permute-done.near
  15.1 3.1 %collective-permute-start.1 = (f32[400,128]{1,0:T(8,128)S(1)}, f32[400,128]{1,0:T(8,128)S(1)}, u32[]{:S(2)}, u32[]{:S(2)}) collective-permute-start(f32[400,128]{1,0:T(8,128)S(1)} %collective-permute-done.near), channel_id=1, source_target_pairs={{0,64},{64,128},{128,192},{96,32},{160,96},{224,160},{1,65},{65,12... | collective-permute-start | bytes 614408 | tf_op jit(solution)/shard_map/ppermute | solution.py:259
  18.2 0.0 collective-permute-done.5.far
  18.2 0.0 collective-permute-done.4.near
  18.2 0.6 lon.1.refs_4_
  18.8 0.1 collective-permute-start.6
  18.9 3.7 %collective-permute-done.1.far = f32[400,128]{1,0:T(8,128)S(1)} collective-permute-done((f32[400,128]{1,0:T(8,128)S(1)}, f32[400,128]{1,0:T(8,128)S(1)}, u32[]{:S(2)}, u32[]{:S(2)}) %collective-permute-start.1) | collective-permute-done | bytes 204832 | tf_op jit(solution)/shard_map/ppermute | solution.py:259
  22.7 0.6 lat.1.refs_1_
  23.3 0.1 collective-permute-start.3
  23.4 1.5 %collective-permute-start.2 = (f32[400,128]{1,0:T(8,128)S(1)}, f32[400,128]{1,0:T(8,128)S(1)}, u32[]{:S(2)}, u32[]{:S(2)}) collective-permute-start(f32[400,128]{1,0:T(8,128)S(1)} %lat.1.refs_1_), channel_id=1, source_target_pairs={{0,1},{1,0},{2,3},{3,2},{4,5},{5,4},{6,7},{7,6},{8,9},{9,8},{10,11... | collective-permute-start | bytes 614408 | tf_op jit(solution)/shard_map/ppermute | solution.py:249
  24.9 1.9 %collective-permute-done.6.refs_3_ = f32[400,128]{1,0:T(8,128)S(1)} collective-permute-done((f32[400,128]{1,0:T(8,128)S(1)}, f32[400,128]{1,0:T(8,128)S(1)}, u32[]{:S(2)}, u32[]{:S(2)}) %collective-permute-start.6) | collective-permute-done | bytes 204832 | tf_op jit(solution)/shard_map/ppermute | solution.py:256
  26.8 3.1 %collective-permute-start.7 = (f32[400,128]{1,0:T(8,128)S(1)}, f32[400,128]{1,0:T(8,128)S(1)}, u32[]{:S(2)}, u32[]{:S(2)}) collective-permute-start(f32[400,128]{1,0:T(8,128)S(1)} %collective-permute-done.6.refs_3_), channel_id=1, source_target_pairs={{0,64},{64,128},{128,192},{96,32},{160,96},{224,160},{1,65},{65,12... | collective-permute-start | bytes 614408 | tf_op jit(solution)/shard_map/ppermute | solution.py:259
  29.9 0.0 collective-permute-done.3.refs_2_
  29.9 0.0 collective-permute-done.2.refs_0_
  29.9 3.2 %collective-permute-done.7.refs_5_ = f32[400,128]{1,0:T(8,128)S(1)} collective-permute-done((f32[400,128]{1,0:T(8,128)S(1)}, f32[400,128]{1,0:T(8,128)S(1)}, u32[]{:S(2)}, u32[]{:S(2)}) %collective-permute-start.7) | collective-permute-done | bytes 204832 | tf_op jit(solution)/shard_map/ppermute | solution.py:259
  33.1 2.5 %last.1 = (f32[2,400,128]{2,1,0:T(8,128)S(1)}, f32[320,128]{1,0:T(8,128)S(1)}) custom-call(f32[20]{0:T(128)S(1)} %cosine_sqrt_fusion.weights, f32[40,120]{1,0:T(8,128)S(1)} %get-tuple-element.8.band.lon_band, f32[40,120]{1,0:T(8,128)S(1)} %get-tuple-element.9.lat_band, f32[400,128]{1,0:T(8,128)S(1)} %collective-permute-done.2.refs_0_, ...), custom_call_target="tpu_custom_call" | custom-call | tf_op jit(solution)/shard_map/last/pallas_call | solution.py:236
  35.6 16.9 %all_to_all.15 = f32[32,1,1280]{2,1,0:T(1,128)S(1)} all-to-all(f32[32,1,1280]{2,1,0:T(1,128)S(1)} %bitcast.8), channel_id=1, replica_groups=mesh['x'=4,'yh'=2,'yl'=2,'z'=8,'core'=2] {'x','yh','yl','core'}, dimensions={0} | all-to-all | bytes 327680 | tf_op jit(solution)/shard_map/all_to_all | solution.py:27
  52.5 0.1 reduce_sum.18
  52.7 11.4 %all_to_all.16 = f32[8,1,1280]{2,1,0:T(1,128)S(1)} all-to-all(f32[8,1,1280]{2,1,0:T(1,128)S(1)} %broadcast_in_dim.25), channel_id=1, replica_groups=mesh['x'=4,'yh'=2,'yl'=2,'z'=8,'core'=2] {'z'}, dimensions={0} | all-to-all | bytes 81920 | tf_op jit(solution)/shard_map/all_to_all | solution.py:22
  64.1 0.1 broadcast_in_dim.26
  64.2 13.0 %all_to_all.17 = f32[32,1,1280]{2,1,0:T(1,128)S(1)} all-to-all(f32[32,1,1280]{2,1,0:T(1,128)S(1)} %broadcast_in_dim.26), channel_id=1, replica_groups=mesh['x'=4,'yh'=2,'yl'=2,'z'=8,'core'=2] {'x','yh','yl','core'}, dimensions={0} | all-to-all | bytes 327680 | tf_op jit(solution)/shard_map/all_to_all | solution.py:22
  77.1 11.3 %factor.1 = (f32[20,20,256]{2,1,0:T(8,128)}, f32[256,256]{1,0:T(8,128)}) custom-call(f32[320,128]{1,0:T(8,128)S(1)} %bitcast.7, f32[2,400,128]{2,1,0:T(8,128)S(1)} %get-tuple-element.13.matrix), custom_call_target="tpu_custom_call" | custom-call | tf_op jit(solution)/shard_map/factor/pallas_call | solution.py:236
  (9 shorter events, 0.1 us)
Async XLA Ops:
  0.6 0.7 copy-start.2
  1.3 1.1 %copy-start = (f32[20,20,384]{2,1,0:T(8,128)S(1)}, f32[20,20,384]{2,1,0:T(8,128)}, u32[]{:S(2)}) copy-start(f32[20,20,384]{2,1,0:T(8,128)} %field.3) | copy-start | bytes 1843204
  2.4 4.6 %copy-start.1 = (f32[20,20,384]{2,1,0:T(8,128)S(1)}, f32[20,20,384]{2,1,0:T(8,128)}, u32[]{:S(2)}) copy-start(f32[20,20,384]{2,1,0:T(8,128)} %field.3) | copy-start | bytes 1843204
  3.1 12.0 %collective-permute-start = (f32[400,128]{1,0:T(8,128)S(1)}, f32[400,128]{1,0:T(8,128)S(1)}, u32[]{:S(2)}, u32[]{:S(2)}) collective-permute-start(f32[400,128]{1,0:T(8,128)S(1)} %early.1.own), channel_id=1, source_target_pairs={{0,32},{32,0},{1,33},{33,1},{2,34},{34,2},{3,35},{35,3},{4,36},{36... | collective-permute-start | bytes 614408 | tf_op jit(solution)/shard_map/ppermute | solution.py:256
  7.0 0.7 copy-start.3
  7.0 0.7 copy-start.4
  8.9 9.3 %collective-permute-start.5 = (f32[400,128]{1,0:T(8,128)S(1)}, f32[400,128]{1,0:T(8,128)S(1)}, u32[]{:S(2)}, u32[]{:S(2)}) collective-permute-start(f32[400,128]{1,0:T(8,128)S(1)} %get-tuple-element.11.own), channel_id=1, source_target_pairs={{1,2},{3,4},{5,6},{7,8},{9,10},{11,12},{13,14},{15,16},{17,18},{19... | collective-permute-start | bytes 614408 | tf_op jit(solution)/shard_map/ppermute | solution.py:251
  11.4 6.7 %collective-permute-start.4 = (f32[400,128]{1,0:T(8,128)S(1)}, f32[400,128]{1,0:T(8,128)S(1)}, u32[]{:S(2)}, u32[]{:S(2)}) collective-permute-start(f32[400,128]{1,0:T(8,128)S(1)} %get-tuple-element.11.own), channel_id=1, source_target_pairs={{0,1},{1,0},{2,3},{3,2},{4,5},{5,4},{6,7},{7,6},{8,9},{9,8},{10,11... | collective-permute-start | bytes 614408 | tf_op jit(solution)/shard_map/ppermute | solution.py:249
  15.1 7.6 %collective-permute-start.1 = (f32[400,128]{1,0:T(8,128)S(1)}, f32[400,128]{1,0:T(8,128)S(1)}, u32[]{:S(2)}, u32[]{:S(2)}) collective-permute-start(f32[400,128]{1,0:T(8,128)S(1)} %collective-permute-done.near), channel_id=1, source_target_pairs={{0,64},{64,128},{128,192},{96,32},{160,96},{224,160},{1,65},{65,12... | collective-permute-start | bytes 614408 | tf_op jit(solution)/shard_map/ppermute | solution.py:259
  18.8 8.0 %collective-permute-start.6 = (f32[400,128]{1,0:T(8,128)S(1)}, f32[400,128]{1,0:T(8,128)S(1)}, u32[]{:S(2)}, u32[]{:S(2)}) collective-permute-start(f32[400,128]{1,0:T(8,128)S(1)} %lon.1.refs_4_), channel_id=1, source_target_pairs={{0,32},{32,0},{1,33},{33,1},{2,34},{34,2},{3,35},{35,3},{4,36},{36... | collective-permute-start | bytes 614408 | tf_op jit(solution)/shard_map/ppermute | solution.py:256
  23.3 6.6 %collective-permute-start.3 = (f32[400,128]{1,0:T(8,128)S(1)}, f32[400,128]{1,0:T(8,128)S(1)}, u32[]{:S(2)}, u32[]{:S(2)}) collective-permute-start(f32[400,128]{1,0:T(8,128)S(1)} %lat.1.refs_1_), channel_id=1, source_target_pairs={{1,2},{3,4},{5,6},{7,8},{9,10},{11,12},{13,14},{15,16},{17,18},{19... | collective-permute-start | bytes 614408 | tf_op jit(solution)/shard_map/ppermute | solution.py:251
  23.4 6.5 %collective-permute-start.2 = (f32[400,128]{1,0:T(8,128)S(1)}, f32[400,128]{1,0:T(8,128)S(1)}, u32[]{:S(2)}, u32[]{:S(2)}) collective-permute-start(f32[400,128]{1,0:T(8,128)S(1)} %lat.1.refs_1_), channel_id=1, source_target_pairs={{0,1},{1,0},{2,3},{3,2},{4,5},{5,4},{6,7},{7,6},{8,9},{9,8},{10,11... | collective-permute-start | bytes 614408 | tf_op jit(solution)/shard_map/ppermute | solution.py:249
  26.8 6.3 %collective-permute-start.7 = (f32[400,128]{1,0:T(8,128)S(1)}, f32[400,128]{1,0:T(8,128)S(1)}, u32[]{:S(2)}, u32[]{:S(2)}) collective-permute-start(f32[400,128]{1,0:T(8,128)S(1)} %collective-permute-done.6.refs_3_), channel_id=1, source_target_pairs={{0,64},{64,128},{128,192},{96,32},{160,96},{224,160},{1,65},{65,12... | collective-permute-start | bytes 614408 | tf_op jit(solution)/shard_map/ppermute | solution.py:259

commit v9 on v8

--- a/solution.py
+++ b/solution.py
@@ -49,9 +49,8 @@
 
 def eliminate(work):
     for top in range(0, TILE, STEP):
-        own = work[top:top + STEP, :TILE]
-        cols = [wide(own[:, top + j:top + j + 1]) for j in range(STEP)]
-        left = {(i, j): wide(cols[j][i:i + 1, :]) for j in range(STEP) for i in range(j + 1)}
+        flat = [wide(work[top + i:top + i + 1, :TILE]) for i in range(STEP)]
+        left = {(i, j): wide(flat[i][:, top + j:top + j + 1]) for j in range(STEP) for i in range(j + 1)}
         rows = [[wide(work[top + i:top + i + 1, s:s + TILE]) for s in (0, TILE)] for i in range(STEP)]
         root, upper = [], {}
         for j in range(STEP):
@@ -75,8 +74,11 @@
                 factors[j] = factors[j] * root[j]
                 for i in range(j + 1, STEP):
                     factors[i] = factors[i] - upper[j, i] * factors[j]
-            for j in range(STEP):
-                parts = [value - factors[j] * done for value, done in zip(parts, rows[j])]
+            for half in range(2):
+                terms = [factors[j] * rows[j][half] for j in range(STEP)]
+                while len(terms) > 1:
+                    terms = [one + other for one, other in zip(terms[::2], terms[1::2])]
+                parts[half] = parts[half] - terms[0]
             for half in range(2):
                 work[below:below + STEP, half * TILE:(half + 1) * TILE] = parts[half]
 
@@ -103,20 +105,19 @@
     blocks = [gram[at * PACK : (at + 1) * PACK, :] for at in range(5)]
     r11, w11 = solve(mirrored(blocks[0], blocks[4]))
     r12 = product(w11, jnp.concatenate(blocks[1:3], axis=0), PLAIN)
-    a22 = mirrored(blocks[3], pltpu.roll(blocks[4], PACK, 1))
-    r22, w22 = solve(a22 - product(r12, r12, ROWS))
-    w21 = -product(w22, product(r12, w11, ROWS), PLAIN)
+    a22 = mirrored(blocks[3], pltpu.roll(blocks[4], PACK, 1)) - product(r12, r12, ROWS)
+    left = product(matrix[0], w11, COLS)
+    rest = matrix[1] - product(left, r12, PLAIN)
+    r22, w22 = solve(a22)
+    right = product(rest, w22 * scale, COLS)
     merged[:TILE, :TILE] = r11 * (1.0 / scale)
     merged[:TILE, TILE:] = r12 * (1.0 / scale)
     merged[TILE:, :TILE] = jnp.zeros((TILE, TILE), jnp.float32)
     merged[TILE:, TILE:] = r22 * (1.0 / scale)
-    first, second = (matrix[0], matrix[1])
-    left = product(first, w11 * scale, COLS)
-    right = product(first, w21 * scale, COLS) + product(second, w22 * scale, COLS)
     lines, side, _ = basis.shape
     for line in range(lines):
         part = slice(line * side, (line + 1) * side)
-        basis[line, :, :TILE] = left[part]
+        basis[line, :, :TILE] = left[part] * scale
         basis[line, :, TILE:] = right[part]
 
 

time: 88.8 us -> 85.5 us (0.963)
  Pallas kernels: 16.9 us -> 13.6 us
    pallas_call x6, Pallas kernels: 16.9 us -> 13.6 us  [called(): pl.pallas_call(kernel, out_shape=[jax.ShapeDtypeStruct(shape, jnp.float32...]
where the time goes in v9:
time: 85.5 us; the launch traced here: 85.2 us
  blocking collectives  41.2 us (48%)
  starting transfers between devices  17.9 us (21%)
  Pallas kernels  13.6 us (16%)
  waiting for transfers between devices  8.8 us (10%)
  local copies, waits for them, and re-layouts  2.57 us (3%)
    all_to_all x2, blocking collectives, shared(): return lax.all_to_all(copies, axes, 0, 0)  24.3 us
    all_to_all x1, blocking collectives, summed(): lax.all_to_all(value.reshape(peers, 1, value.size // peers), PLANE, 0, 0)  16.9 us
    pallas_call x6, Pallas kernels, called(): pl.pallas_call(kernel, out_shape=[jax.ShapeDtypeStruct(shape, jnp.float32...  13.6 us
    ppermute x2, waiting for transfers between devices, passed_on(): return (near, lax.ppermute(near, LAT, up + down))  6.91 us
    ppermute x2, starting transfers between devices, passed_on(): return (near, lax.ppermute(near, LAT, up + down))  6.21 us
    ppermute x2, starting transfers between devices, around(): near = lax.ppermute(value, 'core', [(0, 1), (1, 0)])  5.15 us
    ppermute x2, starting transfers between devices, passed_on(): near = lax.ppermute(value, 'yh', [(0, 1), (1, 0)])  3.92 us
    ppermute x2, starting transfers between devices, around(): lax.ppermute(value, LON, across + [(j, i) for i, j in across])  2.66 us
  transfers between devices with their start and end apart: 8, of which 3 were waited for; matrix products, arithmetic and copies ran while one was open for 0% of the time, Pallas kernels for 3%

profile of v9, /device:TPU:1, one launch (start us, length us, event | category | flops | bytes accessed | tf_op | source)
XLA Modules:
  0.0 85.2 jit_solution(14373990016419258603)
XLA Ops:
  0.6 0.7 copy-done.2
  1.3 1.1 %copy-done = f32[20,20,384]{2,1,0:T(8,128)S(1)} copy-done((f32[20,20,384]{2,1,0:T(8,128)S(1)}, f32[20,20,384]{2,1,0:T(8,128)}, u32[]{:S(2)}) %copy-start) | copy-done | bytes 614424
  2.4 0.6 early.1.own
  3.1 3.8 %collective-permute-start = (f32[400,128]{1,0:T(8,128)S(1)}, f32[400,128]{1,0:T(8,128)S(1)}, u32[]{:S(2)}, u32[]{:S(2)}) collective-permute-start(f32[400,128]{1,0:T(8,128)S(1)} %early.1.own), channel_id=1, source_target_pairs={{0,32},{32,0},{1,33},{33,1},{2,34},{34,2},{3,35},{35,3},{4,36},{36... | collective-permute-start | bytes 614408 | tf_op jit(solution)/shard_map/ppermute | solution.py:257
  6.9 0.1 add_convert_fusion.low
  7.0 0.7 copy-done.3
  7.7 0.0 copy-done.4
  7.7 1.2 %late.1 = (f32[400,128]{1,0:T(8,128)S(1)}, f32[40,120]{1,0:T(8,128)S(1)}, f32[40,120]{1,0:T(8,128)S(1)}, f32[40,120]{1,0:T(8,128)S(1)}) custom-call(s32[2]{0:T(128)S(1)} %add_convert_fusion.low, f32[20]{0:T(128)S(1)} %cosine_sqrt_fusion.weights, f32[1,129]{1,0:T(1,128)S(1)} %bitcast.10, f32[1,41]{1,0:T(1,128)S(1)} %bitcast.11, f32[1,41]{1,0:T(1,128)S(1)} %bitcast.12, ...), custom_call_target="tpu_custom_call" | custom-call | tf_op jit(solution)/shard_map/late/pallas_call | solution.py:237
  8.9 2.6 %collective-permute-start.5 = (f32[400,128]{1,0:T(8,128)S(1)}, f32[400,128]{1,0:T(8,128)S(1)}, u32[]{:S(2)}, u32[]{:S(2)}) collective-permute-start(f32[400,128]{1,0:T(8,128)S(1)} %get-tuple-element.11.own), channel_id=1, source_target_pairs={{1,2},{3,4},{5,6},{7,8},{9,10},{11,12},{13,14},{15,16},{17,18},{19... | collective-permute-start | bytes 614408 | tf_op jit(solution)/shard_map/ppermute | solution.py:252
  11.4 3.6 %collective-permute-start.4 = (f32[400,128]{1,0:T(8,128)S(1)}, f32[400,128]{1,0:T(8,128)S(1)}, u32[]{:S(2)}, u32[]{:S(2)}) collective-permute-start(f32[400,128]{1,0:T(8,128)S(1)} %get-tuple-element.11.own), channel_id=1, source_target_pairs={{0,1},{1,0},{2,3},{3,2},{4,5},{5,4},{6,7},{7,6},{8,9},{9,8},{10,11... | collective-permute-start | bytes 614408 | tf_op jit(solution)/shard_map/ppermute | solution.py:250
  15.1 0.0 collective-permute-done.near
  15.1 3.1 %collective-permute-start.1 = (f32[400,128]{1,0:T(8,128)S(1)}, f32[400,128]{1,0:T(8,128)S(1)}, u32[]{:S(2)}, u32[]{:S(2)}) collective-permute-start(f32[400,128]{1,0:T(8,128)S(1)} %collective-permute-done.near), channel_id=1, source_target_pairs={{0,64},{64,128},{128,192},{96,32},{160,96},{224,160},{1,65},{65,12... | collective-permute-start | bytes 614408 | tf_op jit(solution)/shard_map/ppermute | solution.py:260
  18.2 0.0 collective-permute-done.5.far
  18.2 0.0 collective-permute-done.4.near
  18.2 0.6 lon.1.refs_4_
  18.8 0.1 collective-permute-start.6
  18.9 3.7 %collective-permute-done.1.far = f32[400,128]{1,0:T(8,128)S(1)} collective-permute-done((f32[400,128]{1,0:T(8,128)S(1)}, f32[400,128]{1,0:T(8,128)S(1)}, u32[]{:S(2)}, u32[]{:S(2)}) %collective-permute-start.1) | collective-permute-done | bytes 204832 | tf_op jit(solution)/shard_map/ppermute | solution.py:260
  22.7 0.6 lat.1.refs_1_
  23.3 0.1 collective-permute-start.3
  23.4 1.5 %collective-permute-start.2 = (f32[400,128]{1,0:T(8,128)S(1)}, f32[400,128]{1,0:T(8,128)S(1)}, u32[]{:S(2)}, u32[]{:S(2)}) collective-permute-start(f32[400,128]{1,0:T(8,128)S(1)} %lat.1.refs_1_), channel_id=1, source_target_pairs={{0,1},{1,0},{2,3},{3,2},{4,5},{5,4},{6,7},{7,6},{8,9},{9,8},{10,11... | collective-permute-start | bytes 614408 | tf_op jit(solution)/shard_map/ppermute | solution.py:250
  24.9 1.9 %collective-permute-done.6.refs_3_ = f32[400,128]{1,0:T(8,128)S(1)} collective-permute-done((f32[400,128]{1,0:T(8,128)S(1)}, f32[400,128]{1,0:T(8,128)S(1)}, u32[]{:S(2)}, u32[]{:S(2)}) %collective-permute-start.6) | collective-permute-done | bytes 204832 | tf_op jit(solution)/shard_map/ppermute | solution.py:257
  26.8 3.1 %collective-permute-start.7 = (f32[400,128]{1,0:T(8,128)S(1)}, f32[400,128]{1,0:T(8,128)S(1)}, u32[]{:S(2)}, u32[]{:S(2)}) collective-permute-start(f32[400,128]{1,0:T(8,128)S(1)} %collective-permute-done.6.refs_3_), channel_id=1, source_target_pairs={{0,64},{64,128},{128,192},{96,32},{160,96},{224,160},{1,65},{65,12... | collective-permute-start | bytes 614408 | tf_op jit(solution)/shard_map/ppermute | solution.py:260
  29.9 0.0 collective-permute-done.3.refs_2_
  29.9 0.0 collective-permute-done.2.refs_0_
  29.9 3.2 %collective-permute-done.7.refs_5_ = f32[400,128]{1,0:T(8,128)S(1)} collective-permute-done((f32[400,128]{1,0:T(8,128)S(1)}, f32[400,128]{1,0:T(8,128)S(1)}, u32[]{:S(2)}, u32[]{:S(2)}) %collective-permute-start.7) | collective-permute-done | bytes 204832 | tf_op jit(solution)/shard_map/ppermute | solution.py:260
  33.1 2.5 %last.1 = (f32[2,400,128]{2,1,0:T(8,128)S(1)}, f32[320,128]{1,0:T(8,128)S(1)}) custom-call(f32[20]{0:T(128)S(1)} %cosine_sqrt_fusion.weights, f32[40,120]{1,0:T(8,128)S(1)} %get-tuple-element.8.band.lon_band, f32[40,120]{1,0:T(8,128)S(1)} %get-tuple-element.9.lat_band, f32[400,128]{1,0:T(8,128)S(1)} %collective-permute-done.2.refs_0_, ...), custom_call_target="tpu_custom_call" | custom-call | tf_op jit(solution)/shard_map/last/pallas_call | solution.py:237
  35.6 16.9 %all_to_all.15 = f32[32,1,1280]{2,1,0:T(1,128)S(1)} all-to-all(f32[32,1,1280]{2,1,0:T(1,128)S(1)} %bitcast.8), channel_id=1, replica_groups=mesh['x'=4,'yh'=2,'yl'=2,'z'=8,'core'=2] {'x','yh','yl','core'}, dimensions={0} | all-to-all | bytes 327680 | tf_op jit(solution)/shard_map/all_to_all | solution.py:27
  52.5 0.1 reduce_sum.18
  52.7 11.4 %all_to_all.16 = f32[8,1,1280]{2,1,0:T(1,128)S(1)} all-to-all(f32[8,1,1280]{2,1,0:T(1,128)S(1)} %broadcast_in_dim.25), channel_id=1, replica_groups=mesh['x'=4,'yh'=2,'yl'=2,'z'=8,'core'=2] {'z'}, dimensions={0} | all-to-all | bytes 81920 | tf_op jit(solution)/shard_map/all_to_all | solution.py:22
  64.1 0.1 broadcast_in_dim.26
  64.2 13.0 %all_to_all.17 = f32[32,1,1280]{2,1,0:T(1,128)S(1)} all-to-all(f32[32,1,1280]{2,1,0:T(1,128)S(1)} %broadcast_in_dim.26), channel_id=1, replica_groups=mesh['x'=4,'yh'=2,'yl'=2,'z'=8,'core'=2] {'x','yh','yl','core'}, dimensions={0} | all-to-all | bytes 327680 | tf_op jit(solution)/shard_map/all_to_all | solution.py:22
  77.1 8.0 %factor.1 = (f32[20,20,256]{2,1,0:T(8,128)}, f32[256,256]{1,0:T(8,128)}) custom-call(f32[320,128]{1,0:T(8,128)S(1)} %bitcast.7, f32[2,400,128]{2,1,0:T(8,128)S(1)} %get-tuple-element.13.matrix), custom_call_target="tpu_custom_call" | custom-call | tf_op jit(solution)/shard_map/factor/pallas_call | solution.py:237
  (9 shorter events, 0.1 us)
Async XLA Ops:
  0.6 0.7 copy-start.2
  1.3 1.1 %copy-start = (f32[20,20,384]{2,1,0:T(8,128)S(1)}, f32[20,20,384]{2,1,0:T(8,128)}, u32[]{:S(2)}) copy-start(f32[20,20,384]{2,1,0:T(8,128)} %field.3) | copy-start | bytes 1843204
  2.4 4.6 %copy-start.1 = (f32[20,20,384]{2,1,0:T(8,128)S(1)}, f32[20,20,384]{2,1,0:T(8,128)}, u32[]{:S(2)}) copy-start(f32[20,20,384]{2,1,0:T(8,128)} %field.3) | copy-start | bytes 1843204
  3.1 12.0 %collective-permute-start = (f32[400,128]{1,0:T(8,128)S(1)}, f32[400,128]{1,0:T(8,128)S(1)}, u32[]{:S(2)}, u32[]{:S(2)}) collective-permute-start(f32[400,128]{1,0:T(8,128)S(1)} %early.1.own), channel_id=1, source_target_pairs={{0,32},{32,0},{1,33},{33,1},{2,34},{34,2},{3,35},{35,3},{4,36},{36... | collective-permute-start | bytes 614408 | tf_op jit(solution)/shard_map/ppermute | solution.py:257
  7.0 0.7 copy-start.3
  7.0 0.7 copy-start.4
  8.9 9.3 %collective-permute-start.5 = (f32[400,128]{1,0:T(8,128)S(1)}, f32[400,128]{1,0:T(8,128)S(1)}, u32[]{:S(2)}, u32[]{:S(2)}) collective-permute-start(f32[400,128]{1,0:T(8,128)S(1)} %get-tuple-element.11.own), channel_id=1, source_target_pairs={{1,2},{3,4},{5,6},{7,8},{9,10},{11,12},{13,14},{15,16},{17,18},{19... | collective-permute-start | bytes 614408 | tf_op jit(solution)/shard_map/ppermute | solution.py:252
  11.4 6.7 %collective-permute-start.4 = (f32[400,128]{1,0:T(8,128)S(1)}, f32[400,128]{1,0:T(8,128)S(1)}, u32[]{:S(2)}, u32[]{:S(2)}) collective-permute-start(f32[400,128]{1,0:T(8,128)S(1)} %get-tuple-element.11.own), channel_id=1, source_target_pairs={{0,1},{1,0},{2,3},{3,2},{4,5},{5,4},{6,7},{7,6},{8,9},{9,8},{10,11... | collective-permute-start | bytes 614408 | tf_op jit(solution)/shard_map/ppermute | solution.py:250
  15.1 7.6 %collective-permute-start.1 = (f32[400,128]{1,0:T(8,128)S(1)}, f32[400,128]{1,0:T(8,128)S(1)}, u32[]{:S(2)}, u32[]{:S(2)}) collective-permute-start(f32[400,128]{1,0:T(8,128)S(1)} %collective-permute-done.near), channel_id=1, source_target_pairs={{0,64},{64,128},{128,192},{96,32},{160,96},{224,160},{1,65},{65,12... | collective-permute-start | bytes 614408 | tf_op jit(solution)/shard_map/ppermute | solution.py:260
  18.8 8.0 %collective-permute-start.6 = (f32[400,128]{1,0:T(8,128)S(1)}, f32[400,128]{1,0:T(8,128)S(1)}, u32[]{:S(2)}, u32[]{:S(2)}) collective-permute-start(f32[400,128]{1,0:T(8,128)S(1)} %lon.1.refs_4_), channel_id=1, source_target_pairs={{0,32},{32,0},{1,33},{33,1},{2,34},{34,2},{3,35},{35,3},{4,36},{36... | collective-permute-start | bytes 614408 | tf_op jit(solution)/shard_map/ppermute | solution.py:257
  23.3 6.6 %collective-permute-start.3 = (f32[400,128]{1,0:T(8,128)S(1)}, f32[400,128]{1,0:T(8,128)S(1)}, u32[]{:S(2)}, u32[]{:S(2)}) collective-permute-start(f32[400,128]{1,0:T(8,128)S(1)} %lat.1.refs_1_), channel_id=1, source_target_pairs={{1,2},{3,4},{5,6},{7,8},{9,10},{11,12},{13,14},{15,16},{17,18},{19... | collective-permute-start | bytes 614408 | tf_op jit(solution)/shard_map/ppermute | solution.py:252
  23.4 6.5 %collective-permute-start.2 = (f32[400,128]{1,0:T(8,128)S(1)}, f32[400,128]{1,0:T(8,128)S(1)}, u32[]{:S(2)}, u32[]{:S(2)}) collective-permute-start(f32[400,128]{1,0:T(8,128)S(1)} %lat.1.refs_1_), channel_id=1, source_target_pairs={{0,1},{1,0},{2,3},{3,2},{4,5},{5,4},{6,7},{7,6},{8,9},{9,8},{10,11... | collective-permute-start | bytes 614408 | tf_op jit(solution)/shard_map/ppermute | solution.py:250
  26.8 6.3 %collective-permute-start.7 = (f32[400,128]{1,0:T(8,128)S(1)}, f32[400,128]{1,0:T(8,128)S(1)}, u32[]{:S(2)}, u32[]{:S(2)}) collective-permute-start(f32[400,128]{1,0:T(8,128)S(1)} %collective-permute-done.6.refs_3_), channel_id=1, source_target_pairs={{0,64},{64,128},{128,192},{96,32},{160,96},{224,160},{1,65},{65,12... | collective-permute-start | bytes 614408 | tf_op jit(solution)/shard_map/ppermute | solution.py:260

commit v10 on v9

--- a/solution.py
+++ b/solution.py
@@ -168,7 +168,9 @@
     return product(padded[...].reshape(rows * cols, hours), skew, COLS)
 
 
-def early_kernel(taps, field, out, padded):
+def early_kernel(taps, lat_kernel, lon_kernel, field, out, lat_out, lon_out, padded):
+    lat_out[...] = lat_kernel[...]
+    lon_out[...] = lon_kernel[...]
     rows, side, _ = field.shape
     result = filtered(taps, field, padded, 0)
     for row in range(rows):
@@ -252,12 +254,21 @@
     return near, lax.ppermute(value, LON, across + [(j, i) for i, j in across])
 
 
+def partnered(value):
+    return lax.ppermute(value, "yh", [(0, 1), (1, 0)])
+
+
 def passed_on(value):
     spots, halves = (lax.axis_size("x"), lax.axis_size("yh"))
-    near = lax.ppermute(value, "yh", [(0, 1), (1, 0)])
+    near = partnered(value)
     up = [(x * halves, (x + 1) * halves) for x in range(spots - 1)]
     down = [((x + 1) * halves + 1, x * halves + 1) for x in range(spots - 1)]
     return near, lax.ppermute(near, LAT, up + down)
+
+
+def straight(value):
+    across = [(at, at + 1) for at in range(1, lax.axis_size(LAT) - 1, 2)]
+    return partnered(value), lax.ppermute(value, LAT, across + [(j, i) for i, j in across])
 
 
 def body(field, lat_kernel, lon_kernel, time_taps):
@@ -274,7 +285,17 @@
     half = (local, TILE)
     low = jnp.stack([lax.axis_index("yh") == 0, lax.axis_index("core") == 0]).astype(jnp.int32)
     padded = [pltpu.VMEM((rows_lat, tall, 2 * TILE), jnp.float32)]
-    (first,) = called(early_kernel, "early", [half], [], padded, time_taps[None], field)
+    first, lat_row, lon_row = called(
+        early_kernel,
+        "early",
+        [half, (1, 2 * SH + 1), (1, 2 * SH + 1)],
+        [],
+        padded,
+        time_taps[None],
+        lat_kernel[None],
+        lon_kernel[None],
+        field,
+    )
     second, lat_band, lon_band, lat_weighted = called(
         late_kernel,
         "late",
@@ -284,8 +305,8 @@
         low,
         weights,
         time_taps[None],
-        lat_kernel[None],
-        lon_kernel[None],
+        lat_row,
+        lon_row,
         field,
     )
     smooth = functools.partial(smooth_kernel, SH)
@@ -293,7 +314,7 @@
     beside, beyond = around(second)
     (second,) = called(smooth, "lon", [half], [], [], lon_band, beside, second, beyond)
     (first,) = called(smooth, "lat", [half], [], [], lat_band, near, first, far)
-    near, far = passed_on(second)
+    near, far = straight(second)
     beside, beyond = around(first)
     matrix, local_gram = called(
         functools.partial(last_kernel, SH),

time: 85.5 us -> 85.3 us (level)
  starting transfers between devices: 17.9 us -> 23.2 us
  waiting for transfers between devices: 8.8 us -> 3.55 us
    ppermute x2 -> x1, waiting for transfers between devices: 6.91 us -> 0.01 us  [passed_on(): return (near, lax.ppermute(near, LAT, up + down))]
    ppermute x2 -> x3, starting transfers between devices: 3.92 us -> 9.71 us  [the longest x2 9.04 us: partnered(): return lax.ppermute(value, 'yh', [(0, 1), (1, 0)])]
    ppermute x2 -> x1, starting transfers between devices: 6.21 us -> 3.12 us  [passed_on(): return (near, lax.ppermute(near, LAT, up + down))]
    ppermute x2 -> x3, waiting for transfers between devices: 1.87 us -> 3.53 us  [the longest x2 3.53 us: partnered(): return lax.ppermute(value, 'yh', [(0, 1), (1, 0)])]
    ppermute x2, starting transfers between devices: 5.15 us -> 6.81 us  [around(): near = lax.ppermute(value, 'core', [(0, 1), (1, 0)])]
    ppermute x2, starting transfers between devices: 2.66 us -> 3.61 us  [around(): lax.ppermute(value, LON, across + [(j, i) for i, j in across])]
  transfers between devices with their start and end apart: 8 -> 8, of which waited for: 3 -> 1; matrix products, arithmetic and copies ran while one was open for 0% -> 0% of each run, Pallas kernels for 3% -> 3%
where the time goes in v10:
time: 85.3 us; the launch traced here: 84.9 us
  blocking collectives  41.6 us (49%)
  starting transfers between devices  23.2 us (27%)
  Pallas kernels  13.6 us (16%)
  waiting for transfers between devices  3.55 us (4%)
  local copies, waits for them, and re-layouts  1.9 us (2%)
    all_to_all x2, blocking collectives, shared(): return lax.all_to_all(copies, axes, 0, 0)  25 us
    all_to_all x1, blocking collectives, summed(): lax.all_to_all(value.reshape(peers, 1, value.size // peers), PLANE, 0, 0)  16.6 us
    pallas_call x6, Pallas kernels, called(): pl.pallas_call(kernel, out_shape=[jax.ShapeDtypeStruct(shape, jnp.float32...  13.6 us
    ppermute x2, starting transfers between devices, partnered(): return lax.ppermute(value, 'yh', [(0, 1), (1, 0)])  9.04 us
    ppermute x2, starting transfers between devices, around(): near = lax.ppermute(value, 'core', [(0, 1), (1, 0)])  6.81 us
    ppermute x2, starting transfers between devices, around(): lax.ppermute(value, LON, across + [(j, i) for i, j in across])  3.61 us
    ppermute x2, waiting for transfers between devices, partnered(): return lax.ppermute(value, 'yh', [(0, 1), (1, 0)])  3.53 us
    ppermute x1, starting transfers between devices, passed_on(): return (near, lax.ppermute(near, LAT, up + down))  3.12 us
  transfers between devices with their start and end apart: 8, of which 1 were waited for; matrix products, arithmetic and copies ran while one was open for 0% of the time, Pallas kernels for 3%

profile of v10, /device:TPU:1, one launch (start us, length us, event | category | flops | bytes accessed | tf_op | source)
XLA Modules:
  0.0 84.9 jit_solution(11706575795063686622)
XLA Ops:
  0.6 0.0 copy-start.4
  0.7 0.6 copy-done.4
  1.3 0.0 copy-done.2
  1.3 1.1 %copy-done = f32[20,20,384]{2,1,0:T(8,128)S(1)} copy-done((f32[20,20,384]{2,1,0:T(8,128)S(1)}, f32[20,20,384]{2,1,0:T(8,128)}, u32[]{:S(2)}) %copy-start) | copy-done | bytes 614424
  2.4 0.6 early.1
  3.1 3.8 %collective-permute-start = (f32[400,128]{1,0:T(8,128)S(1)}, f32[400,128]{1,0:T(8,128)S(1)}, u32[]{:S(2)}, u32[]{:S(2)}) collective-permute-start(f32[400,128]{1,0:T(8,128)S(1)} %get-tuple-element.16.own), channel_id=1, source_target_pairs={{0,32},{32,0},{1,33},{33,1},{2,34},{34,2},{3,35},{35,3},{4,36},{36... | collective-permute-start | bytes 614408 | tf_op jit(solution)/shard_map/ppermute | solution.py:258
  7.0 0.1 add_convert_fusion.low
  7.1 1.2 %late.1 = (f32[400,128]{1,0:T(8,128)S(1)}, f32[40,120]{1,0:T(8,128)S(1)}, f32[40,120]{1,0:T(8,128)S(1)}, f32[40,120]{1,0:T(8,128)S(1)}) custom-call(s32[2]{0:T(128)S(1)} %add_convert_fusion.low, f32[20]{0:T(128)S(1)} %cosine_sqrt_fusion.weights, f32[1,129]{1,0:T(1,128)S(1)} %bitcast.10, f32[1,41]{1,0:T(1,128)S(1)} %get-tuple-element.11.lat_kernel, ...), custom_call_target="tpu_custom_call" | custom-call | tf_op jit(solution)/shard_map/late/pallas_call | solution.py:239
  8.2 2.6 %collective-permute-start.5 = (f32[400,128]{1,0:T(8,128)S(1)}, f32[400,128]{1,0:T(8,128)S(1)}, u32[]{:S(2)}, u32[]{:S(2)}) collective-permute-start(f32[400,128]{1,0:T(8,128)S(1)} %get-tuple-element.17.own), channel_id=1, source_target_pairs={{1,2},{3,4},{5,6},{7,8},{9,10},{11,12},{13,14},{15,16},{17,18},{19... | collective-permute-start | bytes 614408 | tf_op jit(solution)/shard_map/ppermute | solution.py:254
  10.8 3.6 %collective-permute-start.4 = (f32[400,128]{1,0:T(8,128)S(1)}, f32[400,128]{1,0:T(8,128)S(1)}, u32[]{:S(2)}, u32[]{:S(2)}) collective-permute-start(f32[400,128]{1,0:T(8,128)S(1)} %get-tuple-element.17.own), channel_id=1, source_target_pairs={{0,1},{1,0},{2,3},{3,2},{4,5},{5,4},{6,7},{7,6},{8,9},{9,8},{10,11... | collective-permute-start | bytes 614408 | tf_op jit(solution)/shard_map/ppermute | solution.py:252
  14.4 0.0 collective-permute-done.near
  14.4 3.1 %collective-permute-start.1 = (f32[400,128]{1,0:T(8,128)S(1)}, f32[400,128]{1,0:T(8,128)S(1)}, u32[]{:S(2)}, u32[]{:S(2)}) collective-permute-start(f32[400,128]{1,0:T(8,128)S(1)} %collective-permute-done.near), channel_id=1, source_target_pairs={{0,64},{64,128},{128,192},{96,32},{160,96},{224,160},{1,65},{65,12... | collective-permute-start | bytes 614408 | tf_op jit(solution)/shard_map/ppermute | solution.py:266
  17.5 0.0 collective-permute-done.5.far
  17.5 0.0 collective-permute-done.4.near
  17.6 0.6 lon.1.refs_4_
  18.2 0.7 collective-permute-start.7
  18.9 5.2 %collective-permute-start.6 = (f32[400,128]{1,0:T(8,128)S(1)}, f32[400,128]{1,0:T(8,128)S(1)}, u32[]{:S(2)}, u32[]{:S(2)}) collective-permute-start(f32[400,128]{1,0:T(8,128)S(1)} %lon.1.refs_4_), channel_id=1, source_target_pairs={{0,32},{32,0},{1,33},{33,1},{2,34},{34,2},{3,35},{35,3},{4,36},{36... | collective-permute-start | bytes 614408 | tf_op jit(solution)/shard_map/ppermute | solution.py:258
  24.1 0.0 collective-permute-done.1.far
  24.1 0.6 lat.1.refs_1_
  24.7 1.0 %collective-permute-start.3 = (f32[400,128]{1,0:T(8,128)S(1)}, f32[400,128]{1,0:T(8,128)S(1)}, u32[]{:S(2)}, u32[]{:S(2)}) collective-permute-start(f32[400,128]{1,0:T(8,128)S(1)} %lat.1.refs_1_), channel_id=1, source_target_pairs={{1,2},{3,4},{5,6},{7,8},{9,10},{11,12},{13,14},{15,16},{17,18},{19... | collective-permute-start | bytes 614408 | tf_op jit(solution)/shard_map/ppermute | solution.py:254
  25.8 3.2 %collective-permute-start.2 = (f32[400,128]{1,0:T(8,128)S(1)}, f32[400,128]{1,0:T(8,128)S(1)}, u32[]{:S(2)}, u32[]{:S(2)}) collective-permute-start(f32[400,128]{1,0:T(8,128)S(1)} %lat.1.refs_1_), channel_id=1, source_target_pairs={{0,1},{1,0},{2,3},{3,2},{4,5},{5,4},{6,7},{7,6},{8,9},{9,8},{10,11... | collective-permute-start | bytes 614408 | tf_op jit(solution)/shard_map/ppermute | solution.py:252
  28.9 0.0 collective-permute-done.7.refs_5_
  29.0 3.5 %collective-permute-done.6.refs_3_ = f32[400,128]{1,0:T(8,128)S(1)} collective-permute-done((f32[400,128]{1,0:T(8,128)S(1)}, f32[400,128]{1,0:T(8,128)S(1)}, u32[]{:S(2)}, u32[]{:S(2)}) %collective-permute-start.6) | collective-permute-done | bytes 204832 | tf_op jit(solution)/shard_map/ppermute | solution.py:258
  32.5 0.0 collective-permute-done.3.refs_2_
  32.5 0.0 collective-permute-done.2.refs_0_
  32.5 2.5 %last.1 = (f32[2,400,128]{2,1,0:T(8,128)S(1)}, f32[320,128]{1,0:T(8,128)S(1)}) custom-call(f32[20]{0:T(128)S(1)} %cosine_sqrt_fusion.weights, f32[40,120]{1,0:T(8,128)S(1)} %get-tuple-element.13.band.lon_band, f32[40,120]{1,0:T(8,128)S(1)} %get-tuple-element.14.lat_band, f32[400,128]{1,0:T(8,128)S(1)} %collective-permute-done.2.refs_0_, ...), custom_call_target="tpu_custom_call" | custom-call | tf_op jit(solution)/shard_map/last/pallas_call | solution.py:239
  35.0 16.6 %all_to_all.15 = f32[32,1,1280]{2,1,0:T(1,128)S(1)} all-to-all(f32[32,1,1280]{2,1,0:T(1,128)S(1)} %bitcast.8), channel_id=1, replica_groups=mesh['x'=4,'yh'=2,'yl'=2,'z'=8,'core'=2] {'x','yh','yl','core'}, dimensions={0} | all-to-all | bytes 327680 | tf_op jit(solution)/shard_map/all_to_all | solution.py:27
  51.6 0.1 reduce_sum.18
  51.8 12.0 %all_to_all.16 = f32[8,1,1280]{2,1,0:T(1,128)S(1)} all-to-all(f32[8,1,1280]{2,1,0:T(1,128)S(1)} %broadcast_in_dim.25), channel_id=1, replica_groups=mesh['x'=4,'yh'=2,'yl'=2,'z'=8,'core'=2] {'z'}, dimensions={0} | all-to-all | bytes 81920 | tf_op jit(solution)/shard_map/all_to_all | solution.py:22
  63.8 0.1 broadcast_in_dim.26
  63.9 13.0 %all_to_all.17 = f32[32,1,1280]{2,1,0:T(1,128)S(1)} all-to-all(f32[32,1,1280]{2,1,0:T(1,128)S(1)} %broadcast_in_dim.26), channel_id=1, replica_groups=mesh['x'=4,'yh'=2,'yl'=2,'z'=8,'core'=2] {'x','yh','yl','core'}, dimensions={0} | all-to-all | bytes 327680 | tf_op jit(solution)/shard_map/all_to_all | solution.py:22
  76.9 8.0 %factor.1 = (f32[20,20,256]{2,1,0:T(8,128)}, f32[256,256]{1,0:T(8,128)}) custom-call(f32[320,128]{1,0:T(8,128)S(1)} %bitcast.7, f32[2,400,128]{2,1,0:T(8,128)S(1)} %get-tuple-element.19.matrix), custom_call_target="tpu_custom_call" | custom-call | tf_op jit(solution)/shard_map/factor/pallas_call | solution.py:239
  (9 shorter events, 0.1 us)
Async XLA Ops:
  0.6 0.7 copy-start.4
  0.6 0.7 copy-start.2
  0.7 0.7 copy-start.3
  1.3 1.1 %copy-start = (f32[20,20,384]{2,1,0:T(8,128)S(1)}, f32[20,20,384]{2,1,0:T(8,128)}, u32[]{:S(2)}) copy-start(f32[20,20,384]{2,1,0:T(8,128)} %field.3) | copy-start | bytes 1843204
  2.4 4.6 %copy-start.1 = (f32[20,20,384]{2,1,0:T(8,128)S(1)}, f32[20,20,384]{2,1,0:T(8,128)}, u32[]{:S(2)}) copy-start(f32[20,20,384]{2,1,0:T(8,128)} %field.3) | copy-start | bytes 1843204
  3.1 11.3 %collective-permute-start = (f32[400,128]{1,0:T(8,128)S(1)}, f32[400,128]{1,0:T(8,128)S(1)}, u32[]{:S(2)}, u32[]{:S(2)}) collective-permute-start(f32[400,128]{1,0:T(8,128)S(1)} %get-tuple-element.16.own), channel_id=1, source_target_pairs={{0,32},{32,0},{1,33},{33,1},{2,34},{34,2},{3,35},{35,3},{4,36},{36... | collective-permute-start | bytes 614408 | tf_op jit(solution)/shard_map/ppermute | solution.py:258
  8.2 9.3 %collective-permute-start.5 = (f32[400,128]{1,0:T(8,128)S(1)}, f32[400,128]{1,0:T(8,128)S(1)}, u32[]{:S(2)}, u32[]{:S(2)}) collective-permute-start(f32[400,128]{1,0:T(8,128)S(1)} %get-tuple-element.17.own), channel_id=1, source_target_pairs={{1,2},{3,4},{5,6},{7,8},{9,10},{11,12},{13,14},{15,16},{17,18},{19... | collective-permute-start | bytes 614408 | tf_op jit(solution)/shard_map/ppermute | solution.py:254
  10.8 6.7 %collective-permute-start.4 = (f32[400,128]{1,0:T(8,128)S(1)}, f32[400,128]{1,0:T(8,128)S(1)}, u32[]{:S(2)}, u32[]{:S(2)}) collective-permute-start(f32[400,128]{1,0:T(8,128)S(1)} %get-tuple-element.17.own), channel_id=1, source_target_pairs={{0,1},{1,0},{2,3},{3,2},{4,5},{5,4},{6,7},{7,6},{8,9},{9,8},{10,11... | collective-permute-start | bytes 614408 | tf_op jit(solution)/shard_map/ppermute | solution.py:252
  14.4 9.7 %collective-permute-start.1 = (f32[400,128]{1,0:T(8,128)S(1)}, f32[400,128]{1,0:T(8,128)S(1)}, u32[]{:S(2)}, u32[]{:S(2)}) collective-permute-start(f32[400,128]{1,0:T(8,128)S(1)} %collective-permute-done.near), channel_id=1, source_target_pairs={{0,64},{64,128},{128,192},{96,32},{160,96},{224,160},{1,65},{65,12... | collective-permute-start | bytes 614408 | tf_op jit(solution)/shard_map/ppermute | solution.py:266
  18.2 10.8 %collective-permute-start.7 = (f32[400,128]{1,0:T(8,128)S(1)}, f32[400,128]{1,0:T(8,128)S(1)}, u32[]{:S(2)}, u32[]{:S(2)}) collective-permute-start(f32[400,128]{1,0:T(8,128)S(1)} %lon.1.refs_4_), channel_id=1, source_target_pairs={{32,64},{96,128},{160,192},{64,32},{128,96},{192,160},{33,65},{97,... | collective-permute-start | bytes 614408 | tf_op jit(solution)/shard_map/ppermute | solution.py:271
  18.9 13.6 %collective-permute-start.6 = (f32[400,128]{1,0:T(8,128)S(1)}, f32[400,128]{1,0:T(8,128)S(1)}, u32[]{:S(2)}, u32[]{:S(2)}) collective-permute-start(f32[400,128]{1,0:T(8,128)S(1)} %lon.1.refs_4_), channel_id=1, source_target_pairs={{0,32},{32,0},{1,33},{33,1},{2,34},{34,2},{3,35},{35,3},{4,36},{36... | collective-permute-start | bytes 614408 | tf_op jit(solution)/shard_map/ppermute | solution.py:258
  24.7 7.8 %collective-permute-start.3 = (f32[400,128]{1,0:T(8,128)S(1)}, f32[400,128]{1,0:T(8,128)S(1)}, u32[]{:S(2)}, u32[]{:S(2)}) collective-permute-start(f32[400,128]{1,0:T(8,128)S(1)} %lat.1.refs_1_), channel_id=1, source_target_pairs={{1,2},{3,4},{5,6},{7,8},{9,10},{11,12},{13,14},{15,16},{17,18},{19... | collective-permute-start | bytes 614408 | tf_op jit(solution)/shard_map/ppermute | solution.py:254
  25.8 6.7 %collective-permute-start.2 = (f32[400,128]{1,0:T(8,128)S(1)}, f32[400,128]{1,0:T(8,128)S(1)}, u32[]{:S(2)}, u32[]{:S(2)}) collective-permute-start(f32[400,128]{1,0:T(8,128)S(1)} %lat.1.refs_1_), channel_id=1, source_target_pairs={{0,1},{1,0},{2,3},{3,2},{4,5},{5,4},{6,7},{7,6},{8,9},{9,8},{10,11... | collective-permute-start | bytes 614408 | tf_op jit(solution)/shard_map/ppermute | solution.py:252

commit v11 on v10

--- a/solution.py
+++ b/solution.py
@@ -88,7 +88,7 @@
 PLAIN = ((1,), (0,))
 
 
-def factor_kernel(cells, gram, matrix, basis, merged, work):
+def factor_kernel(cells, gram, early, late, basis, merged, work):
     row = lax.broadcasted_iota(jnp.int32, (TILE, TILE), 0)
     col = lax.broadcasted_iota(jnp.int32, (TILE, TILE), 1)
     eye = jnp.where(row == col, 1.0, 0.0).astype(jnp.float32)
@@ -106,8 +106,8 @@
     r11, w11 = solve(mirrored(blocks[0], blocks[4]))
     r12 = product(w11, jnp.concatenate(blocks[1:3], axis=0), PLAIN)
     a22 = mirrored(blocks[3], pltpu.roll(blocks[4], PACK, 1)) - product(r12, r12, ROWS)
-    left = product(matrix[0], w11, COLS)
-    rest = matrix[1] - product(left, r12, PLAIN)
+    left = product(early[...], w11, COLS)
+    rest = late[...] - product(left, r12, PLAIN)
     r22, w22 = solve(a22)
     right = product(rest, w22 * scale, COLS)
     merged[:TILE, :TILE] = r11 * (1.0 / scale)
@@ -168,7 +168,8 @@
     return product(padded[...].reshape(rows * cols, hours), skew, COLS)
 
 
-def early_kernel(taps, lat_kernel, lon_kernel, field, out, lat_out, lon_out, padded):
+def early_kernel(taps, lat_kernel, lon_kernel, field, out, taps_out, lat_out, lon_out, padded):
+    taps_out[...] = taps[...]
     lat_out[...] = lat_kernel[...]
     lon_out[...] = lon_kernel[...]
     rows, side, _ = field.shape
@@ -178,12 +179,15 @@
         turned(out, row, side, result[at : at + side])
 
 
-def late_kernel(low, weights, taps, lat_kernel, lon_kernel, field, out, lat_band, lon_band, lat_weighted, padded):
+def late_kernel(taps, field, out, padded):
     rows, side, _ = field.shape
     result = filtered(taps, field, padded, TILE)
     for row in range(rows):
         at = row * padded.shape[1]
         out[row * side : (row + 1) * side, :] = result[at : at + side]
+
+
+def bands_kernel(low, weights, lat_kernel, lon_kernel, lat_band, lon_band, lat_weighted):
     lat_band[...] = ordered(low[0], lat_kernel, SH)
     lon_band[...] = ordered(low[1], lon_kernel, SH)
     row = lax.broadcasted_iota(jnp.int32, (2 * SH, 1), 0)
@@ -213,22 +217,25 @@
     return jnp.where((row >= PACK) & (lane < PACK), upper.T, upper)
 
 
-def last_kernel(side, weights, lon_band, lat_band, *refs):
-    parts, (out, gram) = (refs[:-2], refs[-2:])
+def early_last_kernel(side, weights, band, near, own, far, out, gram):
     pair = 2 * side
     row = lax.broadcasted_iota(jnp.int32, (pair, 1), 0)
-    for first in range(0, out.shape[1], pair):
+    for first in range(0, out.shape[0], pair):
         line = first // side
         weight = jnp.where(row < side, weights[line], weights[line + 1])
-        result = product(lon_band[...], stacked(*parts[:3], first, pair), PLAIN)
-        out[0, first : first + pair, :] = result * weight
-        result = product(lat_band[...], stacked(*parts[3:], first, pair), PLAIN)
-        for at in range(2):
-            turned(out.at[1], line + at, side, result[at * side : (at + 1) * side])
-    early, late = (out[0], out[1])
-    first = product(early, early, ROWS)
-    cross = product(early, late, ROWS)
-    second = product(late, late, ROWS)
+        result = product(band[...], stacked(near, own, far, first, pair), PLAIN)
+        out[first : first + pair, :] = result * weight
+    gram[...] = product(out[...], out[...], ROWS)
+
+
+def late_last_kernel(side, band, near, own, far, out, gram):
+    smooth_kernel(side, band, near, own, far, out)
+    gram[...] = product(out[...], out[...], ROWS)
+
+
+def cross_kernel(early, late, early_gram, late_gram, gram):
+    first, second = (early_gram[...], late_gram[...])
+    cross = product(early[...], late[...], ROWS)
     packed = packed_corner(first, second)
     for at, block in enumerate((first[:PACK], cross[:PACK], cross[PACK:], second[:PACK], packed)):
         gram[at * PACK : (at + 1) * PACK, :] = block
@@ -258,12 +265,16 @@
     return lax.ppermute(value, "yh", [(0, 1), (1, 0)])
 
 
-def passed_on(value):
+def handed_on(near):
     spots, halves = (lax.axis_size("x"), lax.axis_size("yh"))
-    near = partnered(value)
     up = [(x * halves, (x + 1) * halves) for x in range(spots - 1)]
     down = [((x + 1) * halves + 1, x * halves + 1) for x in range(spots - 1)]
-    return near, lax.ppermute(near, LAT, up + down)
+    return lax.ppermute(near, LAT, up + down)
+
+
+def passed_on(value):
+    near = partnered(value)
+    return near, handed_on(near)
 
 
 def straight(value):
@@ -285,10 +296,10 @@
     half = (local, TILE)
     low = jnp.stack([lax.axis_index("yh") == 0, lax.axis_index("core") == 0]).astype(jnp.int32)
     padded = [pltpu.VMEM((rows_lat, tall, 2 * TILE), jnp.float32)]
-    first, lat_row, lon_row = called(
+    first, taps_row, lat_row, lon_row = called(
         early_kernel,
         "early",
-        [half, (1, 2 * SH + 1), (1, 2 * SH + 1)],
+        [half, (1, 2 * TH + 1), (1, 2 * SH + 1), (1, 2 * SH + 1)],
         [],
         padded,
         time_taps[None],
@@ -296,41 +307,42 @@
         lon_kernel[None],
         field,
     )
-    second, lat_band, lon_band, lat_weighted = called(
-        late_kernel,
-        "late",
-        [half] + [(2 * SH, 6 * SH)] * 3,
-        [pltpu.SMEM] * 2,
-        padded,
-        low,
-        weights,
-        time_taps[None],
-        lat_row,
-        lon_row,
-        field,
+    (second,) = called(late_kernel, "late", [half], [], padded, taps_row, field)
+    lat_band, lon_band, lat_weighted = called(
+        bands_kernel, "bands", [(2 * SH, 6 * SH)] * 3, [pltpu.SMEM] * 2, [], low, weights, lat_row, lon_row
     )
     smooth = functools.partial(smooth_kernel, SH)
     near, far = passed_on(first)
     beside, beyond = around(second)
     (second,) = called(smooth, "lon", [half], [], [], lon_band, beside, second, beyond)
+    close, distant = straight(second)
     (first,) = called(smooth, "lat", [half], [], [], lat_band, near, first, far)
-    near, far = straight(second)
     beside, beyond = around(first)
-    matrix, local_gram = called(
-        functools.partial(last_kernel, SH),
-        "last",
-        [(2,) + half, (5 * PACK, TILE)],
+    early, early_gram = called(
+        functools.partial(early_last_kernel, SH),
+        "first",
+        [half, (TILE, TILE)],
         [pltpu.SMEM],
         [],
         weights,
         lon_band,
-        lat_weighted,
         beside,
         first,
         beyond,
-        near,
+    )
+    late, late_gram = called(
+        functools.partial(late_last_kernel, SH),
+        "second",
+        [half, (TILE, TILE)],
+        [],
+        [],
+        lat_weighted,
+        close,
         second,
-        far,
+        distant,
+    )
+    (local_gram,) = called(
+        cross_kernel, "cross", [(5 * PACK, TILE)], [], [], early, late, early_gram, late_gram
     )
     gram = summed(local_gram)
     basis, merged = called(
@@ -340,7 +352,8 @@
         [],
         [pltpu.VMEM((TILE, 2 * TILE), jnp.float32)],
         gram,
-        matrix,
+        early,
+        late,
     )
     return (basis, merged)
 

time: 85.3 us -> 86.7 us (1.016)
    pallas_call x6 -> x9, Pallas kernels: 13.6 us -> 14.3 us  [called(): pl.pallas_call(kernel, out_shape=[jax.ShapeDtypeStruct(shape, jnp.float32...]
  transfers between devices with their start and end apart: 8 -> 8, of which waited for: 1 -> 1; matrix products, arithmetic and copies ran while one was open for 0% -> 0% of each run, Pallas kernels for 3% -> 4%
where the time goes in v11:
time: 86.7 us; the launch traced here: 86.3 us
  blocking collectives  42.4 us (49%)
  starting transfers between devices  23.8 us (27%)
  Pallas kernels  14.3 us (16%)
  waiting for transfers between devices  2.9 us (3%)
  local copies, waits for them, and re-layouts  1.9 us (2%)
    all_to_all x2, blocking collectives, shared(): return lax.all_to_all(copies, axes, 0, 0)  25.7 us
    all_to_all x1, blocking collectives, summed(): lax.all_to_all(value.reshape(peers, 1, value.size // peers), PLANE, 0, 0)  16.7 us
    pallas_call x9, Pallas kernels, called(): pl.pallas_call(kernel, out_shape=[jax.ShapeDtypeStruct(shape, jnp.float32...  14.3 us
    ppermute x2, starting transfers between devices, partnered(): return lax.ppermute(value, 'yh', [(0, 1), (1, 0)])  9.04 us
    ppermute x2, starting transfers between devices, around(): near = lax.ppermute(value, 'core', [(0, 1), (1, 0)])  6.68 us
    ppermute x2, starting transfers between devices, around(): lax.ppermute(value, LON, across + [(j, i) for i, j in across])  4.28 us
    ppermute x1, starting transfers between devices, handed_on(): return lax.ppermute(near, LAT, up + down)  3.12 us
    ppermute x2, waiting for transfers between devices, partnered(): return lax.ppermute(value, 'yh', [(0, 1), (1, 0)])  2.89 us
  transfers between devices with their start and end apart: 8, of which 1 were waited for; matrix products, arithmetic and copies ran while one was open for 0% of the time, Pallas kernels for 4%

profile of v11, /device:TPU:1, one launch (start us, length us, event | category | flops | bytes accessed | tf_op | source)
XLA Modules:
  0.0 86.3 jit_solution(9839482351592668573)
XLA Ops:
  0.7 0.6 copy-done.4
  1.3 0.0 copy-done.2
  1.3 1.1 %copy-done = f32[20,20,384]{2,1,0:T(8,128)S(1)} copy-done((f32[20,20,384]{2,1,0:T(8,128)S(1)}, f32[20,20,384]{2,1,0:T(8,128)}, u32[]{:S(2)}) %copy-start) | copy-done | bytes 614424
  2.4 0.6 early.1
  3.1 3.8 %collective-permute-start = (f32[400,128]{1,0:T(8,128)S(1)}, f32[400,128]{1,0:T(8,128)S(1)}, u32[]{:S(2)}, u32[]{:S(2)}) collective-permute-start(f32[400,128]{1,0:T(8,128)S(1)} %get-tuple-element.17.own), channel_id=1, source_target_pairs={{0,32},{32,0},{1,33},{33,1},{2,34},{34,2},{3,35},{35,3},{4,36},{36... | collective-permute-start | bytes 614408 | tf_op jit(solution)/shard_map/ppermute | solution.py:265
  6.9 0.6 late.1.own
  7.6 2.6 %collective-permute-start.5 = (f32[400,128]{1,0:T(8,128)S(1)}, f32[400,128]{1,0:T(8,128)S(1)}, u32[]{:S(2)}, u32[]{:S(2)}) collective-permute-start(f32[400,128]{1,0:T(8,128)S(1)} %late.1.own), channel_id=1, source_target_pairs={{1,2},{3,4},{5,6},{7,8},{9,10},{11,12},{13,14},{15,16},{17,18},{19... | collective-permute-start | bytes 614408 | tf_op jit(solution)/shard_map/ppermute | solution.py:261
  10.1 3.6 %collective-permute-start.4 = (f32[400,128]{1,0:T(8,128)S(1)}, f32[400,128]{1,0:T(8,128)S(1)}, u32[]{:S(2)}, u32[]{:S(2)}) collective-permute-start(f32[400,128]{1,0:T(8,128)S(1)} %late.1.own), channel_id=1, source_target_pairs={{0,1},{1,0},{2,3},{3,2},{4,5},{5,4},{6,7},{7,6},{8,9},{9,8},{10,11... | collective-permute-start | bytes 614408 | tf_op jit(solution)/shard_map/ppermute | solution.py:259
  13.7 0.0 collective-permute-done.near
  13.7 3.1 %collective-permute-start.1 = (f32[400,128]{1,0:T(8,128)S(1)}, f32[400,128]{1,0:T(8,128)S(1)}, u32[]{:S(2)}, u32[]{:S(2)}) collective-permute-start(f32[400,128]{1,0:T(8,128)S(1)} %collective-permute-done.near), channel_id=1, source_target_pairs={{0,64},{64,128},{128,192},{96,32},{160,96},{224,160},{1,65},{65,12... | collective-permute-start | bytes 614408 | tf_op jit(solution)/shard_map/ppermute | solution.py:272
  16.9 0.1 add_convert_fusion.low
  17.0 0.7 bands.1
  17.7 0.0 collective-permute-done.5.far
  17.7 0.0 collective-permute-done.4.near
  17.7 0.6 lon.1.own
  18.4 0.7 collective-permute-start.7
  19.0 5.2 %collective-permute-start.6 = (f32[400,128]{1,0:T(8,128)S(1)}, f32[400,128]{1,0:T(8,128)S(1)}, u32[]{:S(2)}, u32[]{:S(2)}) collective-permute-start(f32[400,128]{1,0:T(8,128)S(1)} %lon.1.own), channel_id=1, source_target_pairs={{0,32},{32,0},{1,33},{33,1},{2,34},{34,2},{3,35},{35,3},{4,36},{36... | collective-permute-start | bytes 614408 | tf_op jit(solution)/shard_map/ppermute | solution.py:265
  24.3 0.0 collective-permute-done.1.far
  24.3 0.6 lat.1.own
  24.9 1.7 %collective-permute-start.3 = (f32[400,128]{1,0:T(8,128)S(1)}, f32[400,128]{1,0:T(8,128)S(1)}, u32[]{:S(2)}, u32[]{:S(2)}) collective-permute-start(f32[400,128]{1,0:T(8,128)S(1)} %lat.1.own), channel_id=1, source_target_pairs={{1,2},{3,4},{5,6},{7,8},{9,10},{11,12},{13,14},{15,16},{17,18},{19... | collective-permute-start | bytes 614408 | tf_op jit(solution)/shard_map/ppermute | solution.py:261
  26.6 3.1 %collective-permute-start.2 = (f32[400,128]{1,0:T(8,128)S(1)}, f32[400,128]{1,0:T(8,128)S(1)}, u32[]{:S(2)}, u32[]{:S(2)}) collective-permute-start(f32[400,128]{1,0:T(8,128)S(1)} %lat.1.own), channel_id=1, source_target_pairs={{0,1},{1,0},{2,3},{3,2},{4,5},{5,4},{6,7},{7,6},{8,9},{9,8},{10,11... | collective-permute-start | bytes 614408 | tf_op jit(solution)/shard_map/ppermute | solution.py:259
  29.7 2.9 %collective-permute-done.6.near = f32[400,128]{1,0:T(8,128)S(1)} collective-permute-done((f32[400,128]{1,0:T(8,128)S(1)}, f32[400,128]{1,0:T(8,128)S(1)}, u32[]{:S(2)}, u32[]{:S(2)}) %collective-permute-start.6) | collective-permute-done | bytes 204832 | tf_op jit(solution)/shard_map/ppermute | solution.py:265
  32.6 1.0 %second.1 = (f32[400,128]{1,0:T(8,128)S(1)}, f32[128,128]{1,0:T(8,128)S(1)}) custom-call(f32[40,120]{1,0:T(8,128)S(1)} %get-tuple-element.19.band, f32[400,128]{1,0:T(8,128)S(1)} %collective-permute-done.6.near, f32[400,128]{1,0:T(8,128)S(1)} %lon.1.own, f32[400,128]{1,0:T(8,128)S(1)} %collective-permute-done.7.far), custom_call_target="tpu_custom_call" | custom-call | tf_op jit(solution)/shard_map/second/pallas_call | solution.py:246
  33.6 0.0 collective-permute-done.3.far
  33.6 1.5 %first.1 = (f32[400,128]{1,0:T(8,128)S(1)}, f32[128,128]{1,0:T(8,128)S(1)}) custom-call(f32[20]{0:T(128)S(1)} %cosine_sqrt_fusion.weights, f32[40,120]{1,0:T(8,128)S(1)} %get-tuple-element.15.band, f32[400,128]{1,0:T(8,128)S(1)} %collective-permute-done.2.near, f32[400,128]{1,0:T(8,128)S(1)} %lat.1.own, f32[400,128]{1,0:T(8,128)S(1)} %collective-permute-done.3.far), custom_call_target="tpu_custom_call" | custom-call | tf_op jit(solution)/shard_map/first/pallas_call | solution.py:246
  35.2 0.4 cross.1
  35.6 16.7 %all_to_all.15 = f32[32,1,1280]{2,1,0:T(1,128)S(1)} all-to-all(f32[32,1,1280]{2,1,0:T(1,128)S(1)} %bitcast.8), channel_id=1, replica_groups=mesh['x'=4,'yh'=2,'yl'=2,'z'=8,'core'=2] {'x','yh','yl','core'}, dimensions={0} | all-to-all | bytes 327680 | tf_op jit(solution)/shard_map/all_to_all | solution.py:27
  52.3 0.1 reduce_sum.18
  52.5 12.7 %all_to_all.16 = f32[8,1,1280]{2,1,0:T(1,128)S(1)} all-to-all(f32[8,1,1280]{2,1,0:T(1,128)S(1)} %broadcast_in_dim.24), channel_id=1, replica_groups=mesh['x'=4,'yh'=2,'yl'=2,'z'=8,'core'=2] {'z'}, dimensions={0} | all-to-all | bytes 81920 | tf_op jit(solution)/shard_map/all_to_all | solution.py:22
  65.2 0.1 broadcast_in_dim.25
  65.3 13.0 %all_to_all.17 = f32[32,1,1280]{2,1,0:T(1,128)S(1)} all-to-all(f32[32,1,1280]{2,1,0:T(1,128)S(1)} %broadcast_in_dim.25), channel_id=1, replica_groups=mesh['x'=4,'yh'=2,'yl'=2,'z'=8,'core'=2] {'x','yh','yl','core'}, dimensions={0} | all-to-all | bytes 327680 | tf_op jit(solution)/shard_map/all_to_all | solution.py:22
  78.3 8.0 %factor.1 = (f32[20,20,256]{2,1,0:T(8,128)}, f32[256,256]{1,0:T(8,128)}) custom-call(f32[320,128]{1,0:T(8,128)S(1)} %bitcast.7, f32[400,128]{1,0:T(8,128)S(1)} %get-tuple-element.18.early, f32[400,128]{1,0:T(8,128)S(1)} %get-tuple-element.21.late), custom_call_target="tpu_custom_call" | custom-call | tf_op jit(solution)/shard_map/factor/pallas_call | solution.py:246
  (12 shorter events, 0.1 us)
Async XLA Ops:
  0.6 0.7 copy-start.4
  0.6 0.7 copy-start.2
  0.7 0.7 copy-start.3
  1.3 1.1 %copy-start = (f32[20,20,384]{2,1,0:T(8,128)S(1)}, f32[20,20,384]{2,1,0:T(8,128)}, u32[]{:S(2)}) copy-start(f32[20,20,384]{2,1,0:T(8,128)} %field.3) | copy-start | bytes 1843204
  2.4 4.5 %copy-start.1 = (f32[20,20,384]{2,1,0:T(8,128)S(1)}, f32[20,20,384]{2,1,0:T(8,128)}, u32[]{:S(2)}) copy-start(f32[20,20,384]{2,1,0:T(8,128)} %field.3) | copy-start | bytes 1843204
  3.1 10.6 %collective-permute-start = (f32[400,128]{1,0:T(8,128)S(1)}, f32[400,128]{1,0:T(8,128)S(1)}, u32[]{:S(2)}, u32[]{:S(2)}) collective-permute-start(f32[400,128]{1,0:T(8,128)S(1)} %get-tuple-element.17.own), channel_id=1, source_target_pairs={{0,32},{32,0},{1,33},{33,1},{2,34},{34,2},{3,35},{35,3},{4,36},{36... | collective-permute-start | bytes 614408 | tf_op jit(solution)/shard_map/ppermute | solution.py:265
  7.6 10.2 %collective-permute-start.5 = (f32[400,128]{1,0:T(8,128)S(1)}, f32[400,128]{1,0:T(8,128)S(1)}, u32[]{:S(2)}, u32[]{:S(2)}) collective-permute-start(f32[400,128]{1,0:T(8,128)S(1)} %late.1.own), channel_id=1, source_target_pairs={{1,2},{3,4},{5,6},{7,8},{9,10},{11,12},{13,14},{15,16},{17,18},{19... | collective-permute-start | bytes 614408 | tf_op jit(solution)/shard_map/ppermute | solution.py:261
  10.1 7.6 %collective-permute-start.4 = (f32[400,128]{1,0:T(8,128)S(1)}, f32[400,128]{1,0:T(8,128)S(1)}, u32[]{:S(2)}, u32[]{:S(2)}) collective-permute-start(f32[400,128]{1,0:T(8,128)S(1)} %late.1.own), channel_id=1, source_target_pairs={{0,1},{1,0},{2,3},{3,2},{4,5},{5,4},{6,7},{7,6},{8,9},{9,8},{10,11... | collective-permute-start | bytes 614408 | tf_op jit(solution)/shard_map/ppermute | solution.py:259
  13.7 10.5 %collective-permute-start.1 = (f32[400,128]{1,0:T(8,128)S(1)}, f32[400,128]{1,0:T(8,128)S(1)}, u32[]{:S(2)}, u32[]{:S(2)}) collective-permute-start(f32[400,128]{1,0:T(8,128)S(1)} %collective-permute-done.near), channel_id=1, source_target_pairs={{0,64},{64,128},{128,192},{96,32},{160,96},{224,160},{1,65},{65,12... | collective-permute-start | bytes 614408 | tf_op jit(solution)/shard_map/ppermute | solution.py:272
  18.4 11.3 %collective-permute-start.7 = (f32[400,128]{1,0:T(8,128)S(1)}, f32[400,128]{1,0:T(8,128)S(1)}, u32[]{:S(2)}, u32[]{:S(2)}) collective-permute-start(f32[400,128]{1,0:T(8,128)S(1)} %lon.1.own), channel_id=1, source_target_pairs={{32,64},{96,128},{160,192},{64,32},{128,96},{192,160},{33,65},{97,... | collective-permute-start | bytes 614408 | tf_op jit(solution)/shard_map/ppermute | solution.py:282
  19.0 13.5 %collective-permute-start.6 = (f32[400,128]{1,0:T(8,128)S(1)}, f32[400,128]{1,0:T(8,128)S(1)}, u32[]{:S(2)}, u32[]{:S(2)}) collective-permute-start(f32[400,128]{1,0:T(8,128)S(1)} %lon.1.own), channel_id=1, source_target_pairs={{0,32},{32,0},{1,33},{33,1},{2,34},{34,2},{3,35},{35,3},{4,36},{36... | collective-permute-start | bytes 614408 | tf_op jit(solution)/shard_map/ppermute | solution.py:265
  24.9 8.7 %collective-permute-start.3 = (f32[400,128]{1,0:T(8,128)S(1)}, f32[400,128]{1,0:T(8,128)S(1)}, u32[]{:S(2)}, u32[]{:S(2)}) collective-permute-start(f32[400,128]{1,0:T(8,128)S(1)} %lat.1.own), channel_id=1, source_target_pairs={{1,2},{3,4},{5,6},{7,8},{9,10},{11,12},{13,14},{15,16},{17,18},{19... | collective-permute-start | bytes 614408 | tf_op jit(solution)/shard_map/ppermute | solution.py:261
  26.6 7.0 %collective-permute-start.2 = (f32[400,128]{1,0:T(8,128)S(1)}, f32[400,128]{1,0:T(8,128)S(1)}, u32[]{:S(2)}, u32[]{:S(2)}) collective-permute-start(f32[400,128]{1,0:T(8,128)S(1)} %lat.1.own), channel_id=1, source_target_pairs={{0,1},{1,0},{2,3},{3,2},{4,5},{5,4},{6,7},{7,6},{8,9},{9,8},{10,11... | collective-permute-start | bytes 614408 | tf_op jit(solution)/shard_map/ppermute | solution.py:259

commit v12 on v10

--- a/solution.py
+++ b/solution.py
@@ -178,19 +178,18 @@
         turned(out, row, side, result[at : at + side])
 
 
-def late_kernel(low, weights, taps, lat_kernel, lon_kernel, field, out, lat_band, lon_band, lat_weighted, padded):
+def late_kernel(low, weights, taps, lat_kernel, lon_kernel, field, out, lat_band, lon_band, padded):
     rows, side, _ = field.shape
     result = filtered(taps, field, padded, TILE)
     for row in range(rows):
         at = row * padded.shape[1]
         out[row * side : (row + 1) * side, :] = result[at : at + side]
-    lat_band[...] = ordered(low[0], lat_kernel, SH)
     lon_band[...] = ordered(low[1], lon_kernel, SH)
     row = lax.broadcasted_iota(jnp.int32, (2 * SH, 1), 0)
     weight = jnp.zeros((2 * SH, 1), jnp.float32)
     for line in range(SH):
         weight = jnp.where((row == line) | (row == SH + line), weights[line], weight)
-    lat_weighted[...] = lat_band[...] * weight
+    lat_band[...] = ordered(low[0], lat_kernel, SH) * weight
 
 
 def smooth_kernel(side, band, near, own, far, out):
@@ -213,15 +212,12 @@
     return jnp.where((row >= PACK) & (lane < PACK), upper.T, upper)
 
 
-def last_kernel(side, weights, lon_band, lat_band, *refs):
+def last_kernel(side, lon_band, lat_band, *refs):
     parts, (out, gram) = (refs[:-2], refs[-2:])
     pair = 2 * side
-    row = lax.broadcasted_iota(jnp.int32, (pair, 1), 0)
     for first in range(0, out.shape[1], pair):
         line = first // side
-        weight = jnp.where(row < side, weights[line], weights[line + 1])
-        result = product(lon_band[...], stacked(*parts[:3], first, pair), PLAIN)
-        out[0, first : first + pair, :] = result * weight
+        out[0, first : first + pair, :] = product(lon_band[...], stacked(*parts[:3], first, pair), PLAIN)
         result = product(lat_band[...], stacked(*parts[3:], first, pair), PLAIN)
         for at in range(2):
             turned(out.at[1], line + at, side, result[at * side : (at + 1) * side])
@@ -296,10 +292,10 @@
         lon_kernel[None],
         field,
     )
-    second, lat_band, lon_band, lat_weighted = called(
+    second, lat_band, lon_band = called(
         late_kernel,
         "late",
-        [half] + [(2 * SH, 6 * SH)] * 3,
+        [half] + [(2 * SH, 6 * SH)] * 2,
         [pltpu.SMEM] * 2,
         padded,
         low,
@@ -320,11 +316,10 @@
         functools.partial(last_kernel, SH),
         "last",
         [(2,) + half, (5 * PACK, TILE)],
-        [pltpu.SMEM],
         [],
-        weights,
+        [],
         lon_band,
-        lat_weighted,
+        lat_band,
         beside,
         first,
         beyond,

time: 85.3 us -> 84.7 us (level)
  no operation moved by 1% of the time
where the time goes in v12:
time: 84.7 us; the launch traced here: 84.4 us
  blocking collectives  41.6 us (49%)
  starting transfers between devices  23.2 us (27%)
  Pallas kernels  13.1 us (15%)
  waiting for transfers between devices  3.55 us (4%)
  local copies, waits for them, and re-layouts  1.9 us (2%)
    all_to_all x2, blocking collectives, shared(): return lax.all_to_all(copies, axes, 0, 0)  25 us
    all_to_all x1, blocking collectives, summed(): lax.all_to_all(value.reshape(peers, 1, value.size // peers), PLANE, 0, 0)  16.6 us
    pallas_call x6, Pallas kernels, called(): pl.pallas_call(kernel, out_shape=[jax.ShapeDtypeStruct(shape, jnp.float32...  13.1 us
    ppermute x2, starting transfers between devices, partnered(): return lax.ppermute(value, 'yh', [(0, 1), (1, 0)])  9.04 us
    ppermute x2, starting transfers between devices, around(): near = lax.ppermute(value, 'core', [(0, 1), (1, 0)])  6.81 us
    ppermute x2, starting transfers between devices, around(): lax.ppermute(value, LON, across + [(j, i) for i, j in across])  3.61 us
    ppermute x2, waiting for transfers between devices, partnered(): return lax.ppermute(value, 'yh', [(0, 1), (1, 0)])  3.53 us
    ppermute x1, starting transfers between devices, passed_on(): return (near, lax.ppermute(near, LAT, up + down))  3.12 us
  transfers between devices with their start and end apart: 8, of which 1 were waited for; matrix products, arithmetic and copies ran while one was open for 0% of the time, Pallas kernels for 3%

profile of v12, /device:TPU:1, one launch (start us, length us, event | category | flops | bytes accessed | tf_op | source)
XLA Modules:
  0.0 84.4 jit_solution(10245171055710218750)
XLA Ops:
  0.6 0.0 copy-start.4
  0.7 0.6 copy-done.4
  1.3 0.0 copy-done.2
  1.3 1.1 %copy-done = f32[20,20,384]{2,1,0:T(8,128)S(1)} copy-done((f32[20,20,384]{2,1,0:T(8,128)S(1)}, f32[20,20,384]{2,1,0:T(8,128)}, u32[]{:S(2)}) %copy-start) | copy-done | bytes 614424
  2.4 0.6 early.1
  3.1 3.8 %collective-permute-start = (f32[400,128]{1,0:T(8,128)S(1)}, f32[400,128]{1,0:T(8,128)S(1)}, u32[]{:S(2)}, u32[]{:S(2)}) collective-permute-start(f32[400,128]{1,0:T(8,128)S(1)} %get-tuple-element.14.own), channel_id=1, source_target_pairs={{0,32},{32,0},{1,33},{33,1},{2,34},{34,2},{3,35},{35,3},{4,36},{36... | collective-permute-start | bytes 614408 | tf_op jit(solution)/shard_map/ppermute | solution.py:254
  7.0 0.1 add_convert_fusion.low
  7.1 1.2 %late.1 = (f32[400,128]{1,0:T(8,128)S(1)}, f32[40,120]{1,0:T(8,128)S(1)}, f32[40,120]{1,0:T(8,128)S(1)}) custom-call(s32[2]{0:T(128)S(1)} %add_convert_fusion.low, f32[20]{0:T(128)S(1)} %cosine_sqrt_fusion.weights, f32[1,129]{1,0:T(1,128)S(1)} %bitcast.10, f32[1,41]{1,0:T(1,128)S(1)} %get-tuple-element.10.lat_kernel, ...), custom_call_target="tpu_custom_call" | custom-call | tf_op jit(solution)/shard_map/late/pallas_call | solution.py:235
  8.2 2.6 %collective-permute-start.5 = (f32[400,128]{1,0:T(8,128)S(1)}, f32[400,128]{1,0:T(8,128)S(1)}, u32[]{:S(2)}, u32[]{:S(2)}) collective-permute-start(f32[400,128]{1,0:T(8,128)S(1)} %get-tuple-element.15.own), channel_id=1, source_target_pairs={{1,2},{3,4},{5,6},{7,8},{9,10},{11,12},{13,14},{15,16},{17,18},{19... | collective-permute-start | bytes 614408 | tf_op jit(solution)/shard_map/ppermute | solution.py:250
  10.8 3.6 %collective-permute-start.4 = (f32[400,128]{1,0:T(8,128)S(1)}, f32[400,128]{1,0:T(8,128)S(1)}, u32[]{:S(2)}, u32[]{:S(2)}) collective-permute-start(f32[400,128]{1,0:T(8,128)S(1)} %get-tuple-element.15.own), channel_id=1, source_target_pairs={{0,1},{1,0},{2,3},{3,2},{4,5},{5,4},{6,7},{7,6},{8,9},{9,8},{10,11... | collective-permute-start | bytes 614408 | tf_op jit(solution)/shard_map/ppermute | solution.py:248
  14.4 0.0 collective-permute-done.near
  14.4 3.1 %collective-permute-start.1 = (f32[400,128]{1,0:T(8,128)S(1)}, f32[400,128]{1,0:T(8,128)S(1)}, u32[]{:S(2)}, u32[]{:S(2)}) collective-permute-start(f32[400,128]{1,0:T(8,128)S(1)} %collective-permute-done.near), channel_id=1, source_target_pairs={{0,64},{64,128},{128,192},{96,32},{160,96},{224,160},{1,65},{65,12... | collective-permute-start | bytes 614408 | tf_op jit(solution)/shard_map/ppermute | solution.py:262
  17.5 0.0 collective-permute-done.5.far
  17.5 0.0 collective-permute-done.4.near
  17.6 0.6 lon.1.refs_4_
  18.2 0.7 collective-permute-start.7
  18.9 5.2 %collective-permute-start.6 = (f32[400,128]{1,0:T(8,128)S(1)}, f32[400,128]{1,0:T(8,128)S(1)}, u32[]{:S(2)}, u32[]{:S(2)}) collective-permute-start(f32[400,128]{1,0:T(8,128)S(1)} %lon.1.refs_4_), channel_id=1, source_target_pairs={{0,32},{32,0},{1,33},{33,1},{2,34},{34,2},{3,35},{35,3},{4,36},{36... | collective-permute-start | bytes 614408 | tf_op jit(solution)/shard_map/ppermute | solution.py:254
  24.1 0.0 collective-permute-done.1.far
  24.1 0.6 lat.1.refs_1_
  24.7 1.0 %collective-permute-start.3 = (f32[400,128]{1,0:T(8,128)S(1)}, f32[400,128]{1,0:T(8,128)S(1)}, u32[]{:S(2)}, u32[]{:S(2)}) collective-permute-start(f32[400,128]{1,0:T(8,128)S(1)} %lat.1.refs_1_), channel_id=1, source_target_pairs={{1,2},{3,4},{5,6},{7,8},{9,10},{11,12},{13,14},{15,16},{17,18},{19... | collective-permute-start | bytes 614408 | tf_op jit(solution)/shard_map/ppermute | solution.py:250
  25.8 3.2 %collective-permute-start.2 = (f32[400,128]{1,0:T(8,128)S(1)}, f32[400,128]{1,0:T(8,128)S(1)}, u32[]{:S(2)}, u32[]{:S(2)}) collective-permute-start(f32[400,128]{1,0:T(8,128)S(1)} %lat.1.refs_1_), channel_id=1, source_target_pairs={{0,1},{1,0},{2,3},{3,2},{4,5},{5,4},{6,7},{7,6},{8,9},{9,8},{10,11... | collective-permute-start | bytes 614408 | tf_op jit(solution)/shard_map/ppermute | solution.py:248
  28.9 0.0 collective-permute-done.7.refs_5_
  29.0 3.5 %collective-permute-done.6.refs_3_ = f32[400,128]{1,0:T(8,128)S(1)} collective-permute-done((f32[400,128]{1,0:T(8,128)S(1)}, f32[400,128]{1,0:T(8,128)S(1)}, u32[]{:S(2)}, u32[]{:S(2)}) %collective-permute-start.6) | collective-permute-done | bytes 204832 | tf_op jit(solution)/shard_map/ppermute | solution.py:254
  32.5 0.0 collective-permute-done.3.refs_2_
  32.5 0.0 collective-permute-done.2.refs_0_
  32.5 1.9 %last.1 = (f32[2,400,128]{2,1,0:T(8,128)S(1)}, f32[320,128]{1,0:T(8,128)S(1)}) custom-call(f32[40,120]{1,0:T(8,128)S(1)} %get-tuple-element.12.band.lon_band, f32[40,120]{1,0:T(8,128)S(1)} %get-tuple-element.13.band.lat_band, f32[400,128]{1,0:T(8,128)S(1)} %collective-permute-done.2.refs_0_, f32[400,128]{1,0:T(8,128)S(1)} %lat.1.refs_1_, ...), custom_call_target="tpu_custom_call" | custom-call | tf_op jit(solution)/shard_map/last/pallas_call | solution.py:235
  34.4 16.6 %all_to_all.15 = f32[32,1,1280]{2,1,0:T(1,128)S(1)} all-to-all(f32[32,1,1280]{2,1,0:T(1,128)S(1)} %bitcast.8), channel_id=1, replica_groups=mesh['x'=4,'yh'=2,'yl'=2,'z'=8,'core'=2] {'x','yh','yl','core'}, dimensions={0} | all-to-all | bytes 327680 | tf_op jit(solution)/shard_map/all_to_all | solution.py:27
  51.1 0.1 reduce_sum.18
  51.2 12.0 %all_to_all.16 = f32[8,1,1280]{2,1,0:T(1,128)S(1)} all-to-all(f32[8,1,1280]{2,1,0:T(1,128)S(1)} %broadcast_in_dim.25), channel_id=1, replica_groups=mesh['x'=4,'yh'=2,'yl'=2,'z'=8,'core'=2] {'z'}, dimensions={0} | all-to-all | bytes 81920 | tf_op jit(solution)/shard_map/all_to_all | solution.py:22
  63.2 0.1 broadcast_in_dim.26
  63.3 13.0 %all_to_all.17 = f32[32,1,1280]{2,1,0:T(1,128)S(1)} all-to-all(f32[32,1,1280]{2,1,0:T(1,128)S(1)} %broadcast_in_dim.26), channel_id=1, replica_groups=mesh['x'=4,'yh'=2,'yl'=2,'z'=8,'core'=2] {'x','yh','yl','core'}, dimensions={0} | all-to-all | bytes 327680 | tf_op jit(solution)/shard_map/all_to_all | solution.py:22
  76.3 8.0 %factor.1 = (f32[20,20,256]{2,1,0:T(8,128)}, f32[256,256]{1,0:T(8,128)}) custom-call(f32[320,128]{1,0:T(8,128)S(1)} %bitcast.7, f32[2,400,128]{2,1,0:T(8,128)S(1)} %get-tuple-element.17.matrix), custom_call_target="tpu_custom_call" | custom-call | tf_op jit(solution)/shard_map/factor/pallas_call | solution.py:235
  (9 shorter events, 0.1 us)
Async XLA Ops:
  0.6 0.7 copy-start.4
  0.6 0.7 copy-start.2
  0.7 0.7 copy-start.3
  1.3 1.1 %copy-start = (f32[20,20,384]{2,1,0:T(8,128)S(1)}, f32[20,20,384]{2,1,0:T(8,128)}, u32[]{:S(2)}) copy-start(f32[20,20,384]{2,1,0:T(8,128)} %field.3) | copy-start | bytes 1843204
  2.4 4.6 %copy-start.1 = (f32[20,20,384]{2,1,0:T(8,128)S(1)}, f32[20,20,384]{2,1,0:T(8,128)}, u32[]{:S(2)}) copy-start(f32[20,20,384]{2,1,0:T(8,128)} %field.3) | copy-start | bytes 1843204
  3.1 11.3 %collective-permute-start = (f32[400,128]{1,0:T(8,128)S(1)}, f32[400,128]{1,0:T(8,128)S(1)}, u32[]{:S(2)}, u32[]{:S(2)}) collective-permute-start(f32[400,128]{1,0:T(8,128)S(1)} %get-tuple-element.14.own), channel_id=1, source_target_pairs={{0,32},{32,0},{1,33},{33,1},{2,34},{34,2},{3,35},{35,3},{4,36},{36... | collective-permute-start | bytes 614408 | tf_op jit(solution)/shard_map/ppermute | solution.py:254
  8.2 9.3 %collective-permute-start.5 = (f32[400,128]{1,0:T(8,128)S(1)}, f32[400,128]{1,0:T(8,128)S(1)}, u32[]{:S(2)}, u32[]{:S(2)}) collective-permute-start(f32[400,128]{1,0:T(8,128)S(1)} %get-tuple-element.15.own), channel_id=1, source_target_pairs={{1,2},{3,4},{5,6},{7,8},{9,10},{11,12},{13,14},{15,16},{17,18},{19... | collective-permute-start | bytes 614408 | tf_op jit(solution)/shard_map/ppermute | solution.py:250
  10.8 6.7 %collective-permute-start.4 = (f32[400,128]{1,0:T(8,128)S(1)}, f32[400,128]{1,0:T(8,128)S(1)}, u32[]{:S(2)}, u32[]{:S(2)}) collective-permute-start(f32[400,128]{1,0:T(8,128)S(1)} %get-tuple-element.15.own), channel_id=1, source_target_pairs={{0,1},{1,0},{2,3},{3,2},{4,5},{5,4},{6,7},{7,6},{8,9},{9,8},{10,11... | collective-permute-start | bytes 614408 | tf_op jit(solution)/shard_map/ppermute | solution.py:248
  14.4 9.7 %collective-permute-start.1 = (f32[400,128]{1,0:T(8,128)S(1)}, f32[400,128]{1,0:T(8,128)S(1)}, u32[]{:S(2)}, u32[]{:S(2)}) collective-permute-start(f32[400,128]{1,0:T(8,128)S(1)} %collective-permute-done.near), channel_id=1, source_target_pairs={{0,64},{64,128},{128,192},{96,32},{160,96},{224,160},{1,65},{65,12... | collective-permute-start | bytes 614408 | tf_op jit(solution)/shard_map/ppermute | solution.py:262
  18.2 10.8 %collective-permute-start.7 = (f32[400,128]{1,0:T(8,128)S(1)}, f32[400,128]{1,0:T(8,128)S(1)}, u32[]{:S(2)}, u32[]{:S(2)}) collective-permute-start(f32[400,128]{1,0:T(8,128)S(1)} %lon.1.refs_4_), channel_id=1, source_target_pairs={{32,64},{96,128},{160,192},{64,32},{128,96},{192,160},{33,65},{97,... | collective-permute-start | bytes 614408 | tf_op jit(solution)/shard_map/ppermute | solution.py:267
  18.9 13.6 %collective-permute-start.6 = (f32[400,128]{1,0:T(8,128)S(1)}, f32[400,128]{1,0:T(8,128)S(1)}, u32[]{:S(2)}, u32[]{:S(2)}) collective-permute-start(f32[400,128]{1,0:T(8,128)S(1)} %lon.1.refs_4_), channel_id=1, source_target_pairs={{0,32},{32,0},{1,33},{33,1},{2,34},{34,2},{3,35},{35,3},{4,36},{36... | collective-permute-start | bytes 614408 | tf_op jit(solution)/shard_map/ppermute | solution.py:254
  24.7 7.8 %collective-permute-start.3 = (f32[400,128]{1,0:T(8,128)S(1)}, f32[400,128]{1,0:T(8,128)S(1)}, u32[]{:S(2)}, u32[]{:S(2)}) collective-permute-start(f32[400,128]{1,0:T(8,128)S(1)} %lat.1.refs_1_), channel_id=1, source_target_pairs={{1,2},{3,4},{5,6},{7,8},{9,10},{11,12},{13,14},{15,16},{17,18},{19... | collective-permute-start | bytes 614408 | tf_op jit(solution)/shard_map/ppermute | solution.py:250
  25.8 6.7 %collective-permute-start.2 = (f32[400,128]{1,0:T(8,128)S(1)}, f32[400,128]{1,0:T(8,128)S(1)}, u32[]{:S(2)}, u32[]{:S(2)}) collective-permute-start(f32[400,128]{1,0:T(8,128)S(1)} %lat.1.refs_1_), channel_id=1, source_target_pairs={{0,1},{1,0},{2,3},{3,2},{4,5},{5,4},{6,7},{7,6},{8,9},{9,8},{10,11... | collective-permute-start | bytes 614408 | tf_op jit(solution)/shard_map/ppermute | solution.py:248

commit v13 on v12

--- a/solution.py
+++ b/solution.py
@@ -47,8 +47,10 @@
     return jnp.broadcast_to(value, (STEP, TILE))
 
 
-def eliminate(work):
+def eliminate(work, tasks=()):
     for top in range(0, TILE, STEP):
+        for task in tasks[top // STEP : top // STEP + 1]:
+            task()
         flat = [wide(work[top + i:top + i + 1, :TILE]) for i in range(STEP)]
         left = {(i, j): wide(flat[i][:, top + j:top + j + 1]) for j in range(STEP) for i in range(j + 1)}
         rows = [[wide(work[top + i:top + i + 1, s:s + TILE]) for s in (0, TILE)] for i in range(STEP)]
@@ -94,10 +96,10 @@
     eye = jnp.where(row == col, 1.0, 0.0).astype(jnp.float32)
     scale = float(cells) ** 0.5
 
-    def solve(block):
+    def solve(block, tasks=()):
         work[:, :TILE] = block
         work[:, TILE:] = eye
-        eliminate(work)
+        eliminate(work, tasks)
         upper = jnp.where(row <= col, work[:, :TILE], 0.0)
         lower = jnp.where(row >= col, work[:, TILE:], 0.0)
         return upper, lower
@@ -106,18 +108,27 @@
     r11, w11 = solve(mirrored(blocks[0], blocks[4]))
     r12 = product(w11, jnp.concatenate(blocks[1:3], axis=0), PLAIN)
     a22 = mirrored(blocks[3], pltpu.roll(blocks[4], PACK, 1)) - product(r12, r12, ROWS)
-    left = product(matrix[0], w11, COLS)
-    rest = matrix[1] - product(left, r12, PLAIN)
-    r22, w22 = solve(a22)
-    right = product(rest, w22 * scale, COLS)
+    first, second = (matrix[0], matrix[1])
+    lines, side, _ = basis.shape
+    count = 4
+    rest = []
+
+    def early_part(start):
+        part = slice(start * side, (start + count) * side)
+        left = product(first[part], w11, COLS)
+        rest.append(second[part] - product(left, r12, PLAIN))
+        for line in range(count):
+            basis[start + line, :, :TILE] = left[line * side : (line + 1) * side] * scale
+
+    tasks = [functools.partial(early_part, start) for start in range(0, lines, count)]
+    r22, w22 = solve(a22, tasks)
+    right = product(jnp.concatenate(rest, axis=0), w22 * scale, COLS)
     merged[:TILE, :TILE] = r11 * (1.0 / scale)
     merged[:TILE, TILE:] = r12 * (1.0 / scale)
     merged[TILE:, :TILE] = jnp.zeros((TILE, TILE), jnp.float32)
     merged[TILE:, TILE:] = r22 * (1.0 / scale)
-    lines, side, _ = basis.shape
     for line in range(lines):
         part = slice(line * side, (line + 1) * side)
-        basis[line, :, :TILE] = left[part] * scale
         basis[line, :, TILE:] = right[part]
 
 
@@ -185,11 +196,7 @@
         at = row * padded.shape[1]
         out[row * side : (row + 1) * side, :] = result[at : at + side]
     lon_band[...] = ordered(low[1], lon_kernel, SH)
-    row = lax.broadcasted_iota(jnp.int32, (2 * SH, 1), 0)
-    weight = jnp.zeros((2 * SH, 1), jnp.float32)
-    for line in range(SH):
-        weight = jnp.where((row == line) | (row == SH + line), weights[line], weight)
-    lat_band[...] = ordered(low[0], lat_kernel, SH) * weight
+    lat_band[...] = ordered(low[0], lat_kernel, SH) * weights[...]
 
 
 def smooth_kernel(side, band, near, own, far, out):
@@ -275,7 +282,8 @@
     local = rows_lat * rows_lon
     cells = local * lax.axis_size(LAT) * lax.axis_size(LON)
     tall = -(-rows_lon // STEP) * STEP
-    globrow = (lat_place * rows_lat + jnp.arange(rows_lat, dtype=jnp.int32)).astype(jnp.float32)
+    line = lax.broadcasted_iota(jnp.int32, (2 * rows_lat, 1), 0) % rows_lat
+    globrow = (lat_place * rows_lat + line).astype(jnp.float32)
     latitude = jnp.pi * (globrow + 0.5) / total_lat - jnp.pi / 2
     weights = jnp.sqrt(jnp.cos(latitude))
     half = (local, TILE)
@@ -296,7 +304,7 @@
         late_kernel,
         "late",
         [half] + [(2 * SH, 6 * SH)] * 2,
-        [pltpu.SMEM] * 2,
+        [pltpu.SMEM],
         padded,
         low,
         weights,

time: 84.7 us -> 84.7 us (level)
  no operation moved by 1% of the time
where the time goes in v13:
time: 84.7 us; the launch traced here: 84.3 us
  blocking collectives  41.6 us (49%)
  starting transfers between devices  23.2 us (27%)
  Pallas kernels  13 us (15%)
  waiting for transfers between devices  3.54 us (4%)
  local copies, waits for them, and re-layouts  1.9 us (2%)
    all_to_all x2, blocking collectives, shared(): return lax.all_to_all(copies, axes, 0, 0)  24.9 us
    all_to_all x1, blocking collectives, summed(): lax.all_to_all(value.reshape(peers, 1, value.size // peers), PLANE, 0, 0)  16.6 us
    pallas_call x6, Pallas kernels, called(): pl.pallas_call(kernel, out_shape=[jax.ShapeDtypeStruct(shape, jnp.float32...  13 us
    ppermute x2, starting transfers between devices, partnered(): return lax.ppermute(value, 'yh', [(0, 1), (1, 0)])  9.04 us
    ppermute x2, starting transfers between devices, around(): near = lax.ppermute(value, 'core', [(0, 1), (1, 0)])  6.86 us
    ppermute x2, starting transfers between devices, around(): lax.ppermute(value, LON, across + [(j, i) for i, j in across])  3.55 us
    ppermute x2, waiting for transfers between devices, partnered(): return lax.ppermute(value, 'yh', [(0, 1), (1, 0)])  3.53 us
    ppermute x1, starting transfers between devices, passed_on(): return (near, lax.ppermute(near, LAT, up + down))  3.12 us
  transfers between devices with their start and end apart: 8, of which 1 were waited for; matrix products, arithmetic and copies ran while one was open for 0% of the time, Pallas kernels for 3%

profile of v13, /device:TPU:1, one launch (start us, length us, event | category | flops | bytes accessed | tf_op | source)
XLA Modules:
  0.0 84.3 jit_solution(10986311541253362370)
XLA Ops:
  0.7 0.6 copy-done.4
  1.3 0.0 copy-done.2
  1.3 1.1 %copy-done = f32[20,20,384]{2,1,0:T(8,128)S(1)} copy-done((f32[20,20,384]{2,1,0:T(8,128)S(1)}, f32[20,20,384]{2,1,0:T(8,128)}, u32[]{:S(2)}) %copy-start) | copy-done | bytes 614424
  2.4 0.6 early.1
  3.1 3.8 %collective-permute-start = (f32[400,128]{1,0:T(8,128)S(1)}, f32[400,128]{1,0:T(8,128)S(1)}, u32[]{:S(2)}, u32[]{:S(2)}) collective-permute-start(f32[400,128]{1,0:T(8,128)S(1)} %get-tuple-element.14.own), channel_id=1, source_target_pairs={{0,32},{32,0},{1,33},{33,1},{2,34},{34,2},{3,35},{35,3},{4,36},{36... | collective-permute-start | bytes 614408 | tf_op jit(solution)/shard_map/ppermute | solution.py:261
  6.9 0.1 add_convert_fusion.low
  7.0 0.1 fusion.6.weights
  7.1 1.2 %late.1 = (f32[400,128]{1,0:T(8,128)S(1)}, f32[40,120]{1,0:T(8,128)S(1)}, f32[40,120]{1,0:T(8,128)S(1)}) custom-call(s32[2]{0:T(128)S(1)} %add_convert_fusion.low, f32[40,1]{1,0:T(8,128)S(1)} %fusion.6.weights, f32[1,129]{1,0:T(1,128)S(1)} %bitcast.10, f32[1,41]{1,0:T(1,128)S(1)} %get-tuple-element.10.lat_kernel, f32[1,41]{1,0:T(1,128)S(1)} %get-tuple-element.11.lon_kernel, ...), custom_call_target="tpu_custom_call" | custom-call | tf_op jit(solution)/shard_map/late/pallas_call | solution.py:242
  8.3 2.6 %collective-permute-start.5 = (f32[400,128]{1,0:T(8,128)S(1)}, f32[400,128]{1,0:T(8,128)S(1)}, u32[]{:S(2)}, u32[]{:S(2)}) collective-permute-start(f32[400,128]{1,0:T(8,128)S(1)} %get-tuple-element.15.own), channel_id=1, source_target_pairs={{1,2},{3,4},{5,6},{7,8},{9,10},{11,12},{13,14},{15,16},{17,18},{19... | collective-permute-start | bytes 614408 | tf_op jit(solution)/shard_map/ppermute | solution.py:257
  10.9 3.6 %collective-permute-start.4 = (f32[400,128]{1,0:T(8,128)S(1)}, f32[400,128]{1,0:T(8,128)S(1)}, u32[]{:S(2)}, u32[]{:S(2)}) collective-permute-start(f32[400,128]{1,0:T(8,128)S(1)} %get-tuple-element.15.own), channel_id=1, source_target_pairs={{0,1},{1,0},{2,3},{3,2},{4,5},{5,4},{6,7},{7,6},{8,9},{9,8},{10,11... | collective-permute-start | bytes 614408 | tf_op jit(solution)/shard_map/ppermute | solution.py:255
  14.5 0.0 collective-permute-done.near
  14.5 3.1 %collective-permute-start.1 = (f32[400,128]{1,0:T(8,128)S(1)}, f32[400,128]{1,0:T(8,128)S(1)}, u32[]{:S(2)}, u32[]{:S(2)}) collective-permute-start(f32[400,128]{1,0:T(8,128)S(1)} %collective-permute-done.near), channel_id=1, source_target_pairs={{0,64},{64,128},{128,192},{96,32},{160,96},{224,160},{1,65},{65,12... | collective-permute-start | bytes 614408 | tf_op jit(solution)/shard_map/ppermute | solution.py:269
  17.6 0.0 collective-permute-done.5.far
  17.6 0.0 collective-permute-done.4.near
  17.6 0.6 lon.1.refs_4_
  18.2 0.7 collective-permute-start.7
  18.9 5.2 %collective-permute-start.6 = (f32[400,128]{1,0:T(8,128)S(1)}, f32[400,128]{1,0:T(8,128)S(1)}, u32[]{:S(2)}, u32[]{:S(2)}) collective-permute-start(f32[400,128]{1,0:T(8,128)S(1)} %lon.1.refs_4_), channel_id=1, source_target_pairs={{0,32},{32,0},{1,33},{33,1},{2,34},{34,2},{3,35},{35,3},{4,36},{36... | collective-permute-start | bytes 614408 | tf_op jit(solution)/shard_map/ppermute | solution.py:261
  24.1 0.0 collective-permute-done.1.far
  24.1 0.6 lat.1.refs_1_
  24.8 1.0 %collective-permute-start.3 = (f32[400,128]{1,0:T(8,128)S(1)}, f32[400,128]{1,0:T(8,128)S(1)}, u32[]{:S(2)}, u32[]{:S(2)}) collective-permute-start(f32[400,128]{1,0:T(8,128)S(1)} %lat.1.refs_1_), channel_id=1, source_target_pairs={{1,2},{3,4},{5,6},{7,8},{9,10},{11,12},{13,14},{15,16},{17,18},{19... | collective-permute-start | bytes 614408 | tf_op jit(solution)/shard_map/ppermute | solution.py:257
  25.8 3.3 %collective-permute-start.2 = (f32[400,128]{1,0:T(8,128)S(1)}, f32[400,128]{1,0:T(8,128)S(1)}, u32[]{:S(2)}, u32[]{:S(2)}) collective-permute-start(f32[400,128]{1,0:T(8,128)S(1)} %lat.1.refs_1_), channel_id=1, source_target_pairs={{0,1},{1,0},{2,3},{3,2},{4,5},{5,4},{6,7},{7,6},{8,9},{9,8},{10,11... | collective-permute-start | bytes 614408 | tf_op jit(solution)/shard_map/ppermute | solution.py:255
  29.0 0.0 collective-permute-done.7.refs_5_
  29.0 3.5 %collective-permute-done.6.refs_3_ = f32[400,128]{1,0:T(8,128)S(1)} collective-permute-done((f32[400,128]{1,0:T(8,128)S(1)}, f32[400,128]{1,0:T(8,128)S(1)}, u32[]{:S(2)}, u32[]{:S(2)}) %collective-permute-start.6) | collective-permute-done | bytes 204832 | tf_op jit(solution)/shard_map/ppermute | solution.py:261
  32.5 0.0 collective-permute-done.3.refs_2_
  32.5 0.0 collective-permute-done.2.refs_0_
  32.5 1.9 %last.1 = (f32[2,400,128]{2,1,0:T(8,128)S(1)}, f32[320,128]{1,0:T(8,128)S(1)}) custom-call(f32[40,120]{1,0:T(8,128)S(1)} %get-tuple-element.12.band.lon_band, f32[40,120]{1,0:T(8,128)S(1)} %get-tuple-element.13.band.lat_band, f32[400,128]{1,0:T(8,128)S(1)} %collective-permute-done.2.refs_0_, f32[400,128]{1,0:T(8,128)S(1)} %lat.1.refs_1_, ...), custom_call_target="tpu_custom_call" | custom-call | tf_op jit(solution)/shard_map/last/pallas_call | solution.py:242
  34.5 16.6 %all_to_all.15 = f32[32,1,1280]{2,1,0:T(1,128)S(1)} all-to-all(f32[32,1,1280]{2,1,0:T(1,128)S(1)} %bitcast.8), channel_id=1, replica_groups=mesh['x'=4,'yh'=2,'yl'=2,'z'=8,'core'=2] {'x','yh','yl','core'}, dimensions={0} | all-to-all | bytes 327680 | tf_op jit(solution)/shard_map/all_to_all | solution.py:27
  51.1 0.1 reduce_sum.18
  51.3 11.9 %all_to_all.16 = f32[8,1,1280]{2,1,0:T(1,128)S(1)} all-to-all(f32[8,1,1280]{2,1,0:T(1,128)S(1)} %broadcast_in_dim.25), channel_id=1, replica_groups=mesh['x'=4,'yh'=2,'yl'=2,'z'=8,'core'=2] {'z'}, dimensions={0} | all-to-all | bytes 81920 | tf_op jit(solution)/shard_map/all_to_all | solution.py:22
  63.2 0.1 broadcast_in_dim.26
  63.3 13.0 %all_to_all.17 = f32[32,1,1280]{2,1,0:T(1,128)S(1)} all-to-all(f32[32,1,1280]{2,1,0:T(1,128)S(1)} %broadcast_in_dim.26), channel_id=1, replica_groups=mesh['x'=4,'yh'=2,'yl'=2,'z'=8,'core'=2] {'x','yh','yl','core'}, dimensions={0} | all-to-all | bytes 327680 | tf_op jit(solution)/shard_map/all_to_all | solution.py:22
  76.3 8.0 %factor.1 = (f32[20,20,256]{2,1,0:T(8,128)}, f32[256,256]{1,0:T(8,128)}) custom-call(f32[320,128]{1,0:T(8,128)S(1)} %bitcast.7, f32[2,400,128]{2,1,0:T(8,128)S(1)} %get-tuple-element.17.matrix), custom_call_target="tpu_custom_call" | custom-call | tf_op jit(solution)/shard_map/factor/pallas_call | solution.py:242
  (9 shorter events, 0.1 us)
Async XLA Ops:
  0.6 0.7 copy-start.4
  0.6 0.7 copy-start.2
  0.7 0.7 copy-start.3
  1.3 1.1 %copy-start = (f32[20,20,384]{2,1,0:T(8,128)S(1)}, f32[20,20,384]{2,1,0:T(8,128)}, u32[]{:S(2)}) copy-start(f32[20,20,384]{2,1,0:T(8,128)} %field.3) | copy-start | bytes 1843204
  2.4 4.7 %copy-start.1 = (f32[20,20,384]{2,1,0:T(8,128)S(1)}, f32[20,20,384]{2,1,0:T(8,128)}, u32[]{:S(2)}) copy-start(f32[20,20,384]{2,1,0:T(8,128)} %field.3) | copy-start | bytes 1843204
  3.1 11.4 %collective-permute-start = (f32[400,128]{1,0:T(8,128)S(1)}, f32[400,128]{1,0:T(8,128)S(1)}, u32[]{:S(2)}, u32[]{:S(2)}) collective-permute-start(f32[400,128]{1,0:T(8,128)S(1)} %get-tuple-element.14.own), channel_id=1, source_target_pairs={{0,32},{32,0},{1,33},{33,1},{2,34},{34,2},{3,35},{35,3},{4,36},{36... | collective-permute-start | bytes 614408 | tf_op jit(solution)/shard_map/ppermute | solution.py:261
  8.3 9.3 %collective-permute-start.5 = (f32[400,128]{1,0:T(8,128)S(1)}, f32[400,128]{1,0:T(8,128)S(1)}, u32[]{:S(2)}, u32[]{:S(2)}) collective-permute-start(f32[400,128]{1,0:T(8,128)S(1)} %get-tuple-element.15.own), channel_id=1, source_target_pairs={{1,2},{3,4},{5,6},{7,8},{9,10},{11,12},{13,14},{15,16},{17,18},{19... | collective-permute-start | bytes 614408 | tf_op jit(solution)/shard_map/ppermute | solution.py:257
  10.9 6.7 %collective-permute-start.4 = (f32[400,128]{1,0:T(8,128)S(1)}, f32[400,128]{1,0:T(8,128)S(1)}, u32[]{:S(2)}, u32[]{:S(2)}) collective-permute-start(f32[400,128]{1,0:T(8,128)S(1)} %get-tuple-element.15.own), channel_id=1, source_target_pairs={{0,1},{1,0},{2,3},{3,2},{4,5},{5,4},{6,7},{7,6},{8,9},{9,8},{10,11... | collective-permute-start | bytes 614408 | tf_op jit(solution)/shard_map/ppermute | solution.py:255
  14.5 9.7 %collective-permute-start.1 = (f32[400,128]{1,0:T(8,128)S(1)}, f32[400,128]{1,0:T(8,128)S(1)}, u32[]{:S(2)}, u32[]{:S(2)}) collective-permute-start(f32[400,128]{1,0:T(8,128)S(1)} %collective-permute-done.near), channel_id=1, source_target_pairs={{0,64},{64,128},{128,192},{96,32},{160,96},{224,160},{1,65},{65,12... | collective-permute-start | bytes 614408 | tf_op jit(solution)/shard_map/ppermute | solution.py:269
  18.2 10.8 %collective-permute-start.7 = (f32[400,128]{1,0:T(8,128)S(1)}, f32[400,128]{1,0:T(8,128)S(1)}, u32[]{:S(2)}, u32[]{:S(2)}) collective-permute-start(f32[400,128]{1,0:T(8,128)S(1)} %lon.1.refs_4_), channel_id=1, source_target_pairs={{32,64},{96,128},{160,192},{64,32},{128,96},{192,160},{33,65},{97,... | collective-permute-start | bytes 614408 | tf_op jit(solution)/shard_map/ppermute | solution.py:274
  18.9 13.6 %collective-permute-start.6 = (f32[400,128]{1,0:T(8,128)S(1)}, f32[400,128]{1,0:T(8,128)S(1)}, u32[]{:S(2)}, u32[]{:S(2)}) collective-permute-start(f32[400,128]{1,0:T(8,128)S(1)} %lon.1.refs_4_), channel_id=1, source_target_pairs={{0,32},{32,0},{1,33},{33,1},{2,34},{34,2},{3,35},{35,3},{4,36},{36... | collective-permute-start | bytes 614408 | tf_op jit(solution)/shard_map/ppermute | solution.py:261
  24.8 7.8 %collective-permute-start.3 = (f32[400,128]{1,0:T(8,128)S(1)}, f32[400,128]{1,0:T(8,128)S(1)}, u32[]{:S(2)}, u32[]{:S(2)}) collective-permute-start(f32[400,128]{1,0:T(8,128)S(1)} %lat.1.refs_1_), channel_id=1, source_target_pairs={{1,2},{3,4},{5,6},{7,8},{9,10},{11,12},{13,14},{15,16},{17,18},{19... | collective-permute-start | bytes 614408 | tf_op jit(solution)/shard_map/ppermute | solution.py:257
  25.8 6.8 %collective-permute-start.2 = (f32[400,128]{1,0:T(8,128)S(1)}, f32[400,128]{1,0:T(8,128)S(1)}, u32[]{:S(2)}, u32[]{:S(2)}) collective-permute-start(f32[400,128]{1,0:T(8,128)S(1)} %lat.1.refs_1_), channel_id=1, source_target_pairs={{0,1},{1,0},{2,3},{3,2},{4,5},{5,4},{6,7},{7,6},{8,9},{9,8},{10,11... | collective-permute-start | bytes 614408 | tf_op jit(solution)/shard_map/ppermute | solution.py:255

commit v14 on v13

--- a/solution.py
+++ b/solution.py
@@ -179,11 +179,13 @@
     return product(padded[...].reshape(rows * cols, hours), skew, COLS)
 
 
-def early_kernel(taps, lat_kernel, lon_kernel, field, out, lat_out, lon_out, padded):
-    lat_out[...] = lat_kernel[...]
-    lon_out[...] = lon_kernel[...]
+def early_kernel(joined, field, out, taps_out, lat_out, lon_out, padded):
+    start = 0
+    for part in (taps_out, lat_out, lon_out):
+        part[...] = joined[:, start : start + part.shape[1]]
+        start += part.shape[1]
     rows, side, _ = field.shape
-    result = filtered(taps, field, padded, 0)
+    result = filtered(taps_out, field, padded, 0)
     for row in range(rows):
         at = row * padded.shape[1]
         turned(out, row, side, result[at : at + side])
@@ -289,15 +291,13 @@
     half = (local, TILE)
     low = jnp.stack([lax.axis_index("yh") == 0, lax.axis_index("core") == 0]).astype(jnp.int32)
     padded = [pltpu.VMEM((rows_lat, tall, 2 * TILE), jnp.float32)]
-    first, lat_row, lon_row = called(
+    first, taps_row, lat_row, lon_row = called(
         early_kernel,
         "early",
-        [half, (1, 2 * SH + 1), (1, 2 * SH + 1)],
+        [half, (1, 2 * TH + 1), (1, 2 * SH + 1), (1, 2 * SH + 1)],
         [],
         padded,
-        time_taps[None],
-        lat_kernel[None],
-        lon_kernel[None],
+        jnp.concatenate([time_taps, lat_kernel, lon_kernel])[None],
         field,
     )
     second, lat_band, lon_band = called(
@@ -308,7 +308,7 @@
         padded,
         low,
         weights,
-        time_taps[None],
+        taps_row,
         lat_row,
         lon_row,
         field,

time: 84.7 us -> 84.8 us (level)
    unnamed x10 -> x4, local copies, waits for them, and re-layouts: 1.79 us -> 1.12 us
where the time goes in v14:
time: 84.8 us; the launch traced here: 84.5 us
  blocking collectives  41.6 us (49%)
  starting transfers between devices  23.2 us (27%)
  Pallas kernels  13 us (15%)
  waiting for transfers between devices  3.54 us (4%)
  local copies, waits for them, and re-layouts  1.23 us (1%)
  other arithmetic  1.11 us (1%)
    all_to_all x2, blocking collectives, shared(): return lax.all_to_all(copies, axes, 0, 0)  24.9 us
    all_to_all x1, blocking collectives, summed(): lax.all_to_all(value.reshape(peers, 1, value.size // peers), PLANE, 0, 0)  16.6 us
    pallas_call x6, Pallas kernels, called(): pl.pallas_call(kernel, out_shape=[jax.ShapeDtypeStruct(shape, jnp.float32...  13 us
    ppermute x2, starting transfers between devices, partnered(): return lax.ppermute(value, 'yh', [(0, 1), (1, 0)])  9.04 us
    ppermute x2, starting transfers between devices, around(): near = lax.ppermute(value, 'core', [(0, 1), (1, 0)])  6.86 us
    ppermute x2, starting transfers between devices, around(): lax.ppermute(value, LON, across + [(j, i) for i, j in across])  3.55 us
    ppermute x2, waiting for transfers between devices, partnered(): return lax.ppermute(value, 'yh', [(0, 1), (1, 0)])  3.53 us
    ppermute x1, starting transfers between devices, passed_on(): return (near, lax.ppermute(near, LAT, up + down))  3.12 us
  transfers between devices with their start and end apart: 8, of which 1 were waited for; matrix products, arithmetic and copies ran while one was open for 0% of the time, Pallas kernels for 3%

profile of v14, /device:TPU:1, one launch (start us, length us, event | category | flops | bytes accessed | tf_op | source)
XLA Modules:
  0.0 84.5 jit_solution(9229239705364519802)
XLA Ops:
  0.6 0.8 pad_maximum_fusion
  1.4 1.1 %copy-done = f32[20,20,384]{2,1,0:T(8,128)S(1)} copy-done((f32[20,20,384]{2,1,0:T(8,128)S(1)}, f32[20,20,384]{2,1,0:T(8,128)}, u32[]{:S(2)}) %copy-start) | copy-done | bytes 614424
  2.5 0.6 early.1
  3.2 3.8 %collective-permute-start = (f32[400,128]{1,0:T(8,128)S(1)}, f32[400,128]{1,0:T(8,128)S(1)}, u32[]{:S(2)}, u32[]{:S(2)}) collective-permute-start(f32[400,128]{1,0:T(8,128)S(1)} %get-tuple-element.16.own), channel_id=1, source_target_pairs={{0,32},{32,0},{1,33},{33,1},{2,34},{34,2},{3,35},{35,3},{4,36},{36... | collective-permute-start | bytes 614408 | tf_op jit(solution)/shard_map/ppermute | solution.py:263
  7.0 0.1 add_convert_fusion.low
  7.1 0.1 fusion.6.weights
  7.2 0.0 copy-done.1
  7.2 1.2 %late.1 = (f32[400,128]{1,0:T(8,128)S(1)}, f32[40,120]{1,0:T(8,128)S(1)}, f32[40,120]{1,0:T(8,128)S(1)}) custom-call(s32[2]{0:T(128)S(1)} %add_convert_fusion.low, f32[40,1]{1,0:T(8,128)S(1)} %fusion.6.weights, f32[1,129]{1,0:T(1,128)S(1)} %get-tuple-element.11.taps, f32[1,41]{1,0:T(1,128)S(1)} %get-tuple-element.12.lat_kernel, ...), custom_call_target="tpu_custom_call" | custom-call | tf_op jit(solution)/shard_map/late/pallas_call | solution.py:244
  8.4 2.6 %collective-permute-start.5 = (f32[400,128]{1,0:T(8,128)S(1)}, f32[400,128]{1,0:T(8,128)S(1)}, u32[]{:S(2)}, u32[]{:S(2)}) collective-permute-start(f32[400,128]{1,0:T(8,128)S(1)} %get-tuple-element.17.own), channel_id=1, source_target_pairs={{1,2},{3,4},{5,6},{7,8},{9,10},{11,12},{13,14},{15,16},{17,18},{19... | collective-permute-start | bytes 614408 | tf_op jit(solution)/shard_map/ppermute | solution.py:259
  11.0 3.6 %collective-permute-start.4 = (f32[400,128]{1,0:T(8,128)S(1)}, f32[400,128]{1,0:T(8,128)S(1)}, u32[]{:S(2)}, u32[]{:S(2)}) collective-permute-start(f32[400,128]{1,0:T(8,128)S(1)} %get-tuple-element.17.own), channel_id=1, source_target_pairs={{0,1},{1,0},{2,3},{3,2},{4,5},{5,4},{6,7},{7,6},{8,9},{9,8},{10,11... | collective-permute-start | bytes 614408 | tf_op jit(solution)/shard_map/ppermute | solution.py:257
  14.6 0.0 collective-permute-done.near
  14.6 3.1 %collective-permute-start.1 = (f32[400,128]{1,0:T(8,128)S(1)}, f32[400,128]{1,0:T(8,128)S(1)}, u32[]{:S(2)}, u32[]{:S(2)}) collective-permute-start(f32[400,128]{1,0:T(8,128)S(1)} %collective-permute-done.near), channel_id=1, source_target_pairs={{0,64},{64,128},{128,192},{96,32},{160,96},{224,160},{1,65},{65,12... | collective-permute-start | bytes 614408 | tf_op jit(solution)/shard_map/ppermute | solution.py:271
  17.7 0.0 collective-permute-done.5.far
  17.7 0.0 collective-permute-done.4.near
  17.7 0.6 lon.1.refs_4_
  18.3 0.7 collective-permute-start.7
  19.0 5.2 %collective-permute-start.6 = (f32[400,128]{1,0:T(8,128)S(1)}, f32[400,128]{1,0:T(8,128)S(1)}, u32[]{:S(2)}, u32[]{:S(2)}) collective-permute-start(f32[400,128]{1,0:T(8,128)S(1)} %lon.1.refs_4_), channel_id=1, source_target_pairs={{0,32},{32,0},{1,33},{33,1},{2,34},{34,2},{3,35},{35,3},{4,36},{36... | collective-permute-start | bytes 614408 | tf_op jit(solution)/shard_map/ppermute | solution.py:263
  24.2 0.0 collective-permute-done.1.far
  24.2 0.6 lat.1.refs_1_
  24.9 1.0 %collective-permute-start.3 = (f32[400,128]{1,0:T(8,128)S(1)}, f32[400,128]{1,0:T(8,128)S(1)}, u32[]{:S(2)}, u32[]{:S(2)}) collective-permute-start(f32[400,128]{1,0:T(8,128)S(1)} %lat.1.refs_1_), channel_id=1, source_target_pairs={{1,2},{3,4},{5,6},{7,8},{9,10},{11,12},{13,14},{15,16},{17,18},{19... | collective-permute-start | bytes 614408 | tf_op jit(solution)/shard_map/ppermute | solution.py:259
  25.8 3.3 %collective-permute-start.2 = (f32[400,128]{1,0:T(8,128)S(1)}, f32[400,128]{1,0:T(8,128)S(1)}, u32[]{:S(2)}, u32[]{:S(2)}) collective-permute-start(f32[400,128]{1,0:T(8,128)S(1)} %lat.1.refs_1_), channel_id=1, source_target_pairs={{0,1},{1,0},{2,3},{3,2},{4,5},{5,4},{6,7},{7,6},{8,9},{9,8},{10,11... | collective-permute-start | bytes 614408 | tf_op jit(solution)/shard_map/ppermute | solution.py:257
  29.1 0.0 collective-permute-done.7.refs_5_
  29.1 3.5 %collective-permute-done.6.refs_3_ = f32[400,128]{1,0:T(8,128)S(1)} collective-permute-done((f32[400,128]{1,0:T(8,128)S(1)}, f32[400,128]{1,0:T(8,128)S(1)}, u32[]{:S(2)}, u32[]{:S(2)}) %collective-permute-start.6) | collective-permute-done | bytes 204832 | tf_op jit(solution)/shard_map/ppermute | solution.py:263
  32.6 0.0 collective-permute-done.3.refs_2_
  32.6 0.0 collective-permute-done.2.refs_0_
  32.6 1.9 %last.1 = (f32[2,400,128]{2,1,0:T(8,128)S(1)}, f32[320,128]{1,0:T(8,128)S(1)}) custom-call(f32[40,120]{1,0:T(8,128)S(1)} %get-tuple-element.14.band.lon_band, f32[40,120]{1,0:T(8,128)S(1)} %get-tuple-element.15.band.lat_band, f32[400,128]{1,0:T(8,128)S(1)} %collective-permute-done.2.refs_0_, f32[400,128]{1,0:T(8,128)S(1)} %lat.1.refs_1_, ...), custom_call_target="tpu_custom_call" | custom-call | tf_op jit(solution)/shard_map/last/pallas_call | solution.py:244
  34.6 16.6 %all_to_all.15 = f32[32,1,1280]{2,1,0:T(1,128)S(1)} all-to-all(f32[32,1,1280]{2,1,0:T(1,128)S(1)} %bitcast.6), channel_id=1, replica_groups=mesh['x'=4,'yh'=2,'yl'=2,'z'=8,'core'=2] {'x','yh','yl','core'}, dimensions={0} | all-to-all | bytes 327680 | tf_op jit(solution)/shard_map/all_to_all | solution.py:27
  51.2 0.1 reduce_sum.18
  51.4 11.9 %all_to_all.16 = f32[8,1,1280]{2,1,0:T(1,128)S(1)} all-to-all(f32[8,1,1280]{2,1,0:T(1,128)S(1)} %broadcast_in_dim.7), channel_id=1, replica_groups=mesh['x'=4,'yh'=2,'yl'=2,'z'=8,'core'=2] {'z'}, dimensions={0} | all-to-all | bytes 81920 | tf_op jit(solution)/shard_map/all_to_all | solution.py:22
  63.3 0.1 broadcast_in_dim.8
  63.4 13.0 %all_to_all.17 = f32[32,1,1280]{2,1,0:T(1,128)S(1)} all-to-all(f32[32,1,1280]{2,1,0:T(1,128)S(1)} %broadcast_in_dim.8), channel_id=1, replica_groups=mesh['x'=4,'yh'=2,'yl'=2,'z'=8,'core'=2] {'x','yh','yl','core'}, dimensions={0} | all-to-all | bytes 327680 | tf_op jit(solution)/shard_map/all_to_all | solution.py:22
  76.4 8.0 %factor.1 = (f32[20,20,256]{2,1,0:T(8,128)}, f32[256,256]{1,0:T(8,128)}) custom-call(f32[320,128]{1,0:T(8,128)S(1)} %bitcast.5, f32[2,400,128]{2,1,0:T(8,128)S(1)} %get-tuple-element.19.matrix), custom_call_target="tpu_custom_call" | custom-call | tf_op jit(solution)/shard_map/factor/pallas_call | solution.py:244
  (4 shorter events, 0.1 us)
Async XLA Ops:
  1.4 1.1 %copy-start = (f32[20,20,384]{2,1,0:T(8,128)S(1)}, f32[20,20,384]{2,1,0:T(8,128)}, u32[]{:S(2)}) copy-start(f32[20,20,384]{2,1,0:T(8,128)} %field.3) | copy-start | bytes 1843204
  2.5 4.7 %copy-start.1 = (f32[20,20,384]{2,1,0:T(8,128)S(1)}, f32[20,20,384]{2,1,0:T(8,128)}, u32[]{:S(2)}) copy-start(f32[20,20,384]{2,1,0:T(8,128)} %field.3) | copy-start | bytes 1843204
  3.2 11.4 %collective-permute-start = (f32[400,128]{1,0:T(8,128)S(1)}, f32[400,128]{1,0:T(8,128)S(1)}, u32[]{:S(2)}, u32[]{:S(2)}) collective-permute-start(f32[400,128]{1,0:T(8,128)S(1)} %get-tuple-element.16.own), channel_id=1, source_target_pairs={{0,32},{32,0},{1,33},{33,1},{2,34},{34,2},{3,35},{35,3},{4,36},{36... | collective-permute-start | bytes 614408 | tf_op jit(solution)/shard_map/ppermute | solution.py:263
  8.4 9.3 %collective-permute-start.5 = (f32[400,128]{1,0:T(8,128)S(1)}, f32[400,128]{1,0:T(8,128)S(1)}, u32[]{:S(2)}, u32[]{:S(2)}) collective-permute-start(f32[400,128]{1,0:T(8,128)S(1)} %get-tuple-element.17.own), channel_id=1, source_target_pairs={{1,2},{3,4},{5,6},{7,8},{9,10},{11,12},{13,14},{15,16},{17,18},{19... | collective-permute-start | bytes 614408 | tf_op jit(solution)/shard_map/ppermute | solution.py:259
  11.0 6.7 %collective-permute-start.4 = (f32[400,128]{1,0:T(8,128)S(1)}, f32[400,128]{1,0:T(8,128)S(1)}, u32[]{:S(2)}, u32[]{:S(2)}) collective-permute-start(f32[400,128]{1,0:T(8,128)S(1)} %get-tuple-element.17.own), channel_id=1, source_target_pairs={{0,1},{1,0},{2,3},{3,2},{4,5},{5,4},{6,7},{7,6},{8,9},{9,8},{10,11... | collective-permute-start | bytes 614408 | tf_op jit(solution)/shard_map/ppermute | solution.py:257
  14.6 9.7 %collective-permute-start.1 = (f32[400,128]{1,0:T(8,128)S(1)}, f32[400,128]{1,0:T(8,128)S(1)}, u32[]{:S(2)}, u32[]{:S(2)}) collective-permute-start(f32[400,128]{1,0:T(8,128)S(1)} %collective-permute-done.near), channel_id=1, source_target_pairs={{0,64},{64,128},{128,192},{96,32},{160,96},{224,160},{1,65},{65,12... | collective-permute-start | bytes 614408 | tf_op jit(solution)/shard_map/ppermute | solution.py:271
  18.3 10.8 %collective-permute-start.7 = (f32[400,128]{1,0:T(8,128)S(1)}, f32[400,128]{1,0:T(8,128)S(1)}, u32[]{:S(2)}, u32[]{:S(2)}) collective-permute-start(f32[400,128]{1,0:T(8,128)S(1)} %lon.1.refs_4_), channel_id=1, source_target_pairs={{32,64},{96,128},{160,192},{64,32},{128,96},{192,160},{33,65},{97,... | collective-permute-start | bytes 614408 | tf_op jit(solution)/shard_map/ppermute | solution.py:276
  19.0 13.6 %collective-permute-start.6 = (f32[400,128]{1,0:T(8,128)S(1)}, f32[400,128]{1,0:T(8,128)S(1)}, u32[]{:S(2)}, u32[]{:S(2)}) collective-permute-start(f32[400,128]{1,0:T(8,128)S(1)} %lon.1.refs_4_), channel_id=1, source_target_pairs={{0,32},{32,0},{1,33},{33,1},{2,34},{34,2},{3,35},{35,3},{4,36},{36... | collective-permute-start | bytes 614408 | tf_op jit(solution)/shard_map/ppermute | solution.py:263
  24.9 7.8 %collective-permute-start.3 = (f32[400,128]{1,0:T(8,128)S(1)}, f32[400,128]{1,0:T(8,128)S(1)}, u32[]{:S(2)}, u32[]{:S(2)}) collective-permute-start(f32[400,128]{1,0:T(8,128)S(1)} %lat.1.refs_1_), channel_id=1, source_target_pairs={{1,2},{3,4},{5,6},{7,8},{9,10},{11,12},{13,14},{15,16},{17,18},{19... | collective-permute-start | bytes 614408 | tf_op jit(solution)/shard_map/ppermute | solution.py:259
  25.8 6.8 %collective-permute-start.2 = (f32[400,128]{1,0:T(8,128)S(1)}, f32[400,128]{1,0:T(8,128)S(1)}, u32[]{:S(2)}, u32[]{:S(2)}) collective-permute-start(f32[400,128]{1,0:T(8,128)S(1)} %lat.1.refs_1_), channel_id=1, source_target_pairs={{0,1},{1,0},{2,3},{3,2},{4,5},{5,4},{6,7},{7,6},{8,9},{9,8},{10,11... | collective-permute-start | bytes 614408 | tf_op jit(solution)/shard_map/ppermute | solution.py:257

commit v15 on v13

--- a/solution.py
+++ b/solution.py
@@ -314,7 +314,7 @@
         field,
     )
     smooth = functools.partial(smooth_kernel, SH)
-    near, far = passed_on(first)
+    near, far = straight(first)
     beside, beyond = around(second)
     (second,) = called(smooth, "lon", [half], [], [], lon_band, beside, second, beyond)
     (first,) = called(smooth, "lat", [half], [], [], lat_band, near, first, far)

time: 84.7 us -> 93.5 us (1.10)
  waiting for transfers between devices: 3.54 us -> 11.5 us
  starting transfers between devices: 23.2 us -> 27.5 us
  blocking collectives: 41.6 us -> 38.2 us
    ppermute x2, waiting for transfers between devices: 3.53 us -> 11.5 us  [partnered(): return lax.ppermute(value, 'yh', [(0, 1), (1, 0)])]
    ppermute x2, starting transfers between devices: 9.04 us -> 13 us  [partnered(): return lax.ppermute(value, 'yh', [(0, 1), (1, 0)])]
    ppermute x2, starting transfers between devices: 6.86 us -> 10.3 us  [around(): near = lax.ppermute(value, 'core', [(0, 1), (1, 0)])]
    ppermute x1 -> x0, starting transfers between devices: 3.12 us -> none  [passed_on(): return (near, lax.ppermute(near, LAT, up + down))]
    all_to_all x2, blocking collectives: 24.9 us -> 22.1 us  [shared(): return lax.all_to_all(copies, axes, 0, 0)]
  transfers between devices with their start and end apart: 8 -> 8, of which waited for: 1 -> 2; matrix products, arithmetic and copies ran while one was open for 0% -> 0% of each run, Pallas kernels for 3% -> 3%
where the time goes in v15:
time: 93.5 us; the launch traced here: 93.2 us
  blocking collectives  38.2 us (41%)
  starting transfers between devices  27.5 us (29%)
  Pallas kernels  13 us (14%)
  waiting for transfers between devices  11.5 us (12%)
  local copies, waits for them, and re-layouts  1.9 us (2%)
    all_to_all x2, blocking collectives, shared(): return lax.all_to_all(copies, axes, 0, 0)  22.1 us
    all_to_all x1, blocking collectives, summed(): lax.all_to_all(value.reshape(peers, 1, value.size // peers), PLANE, 0, 0)  16.1 us
    pallas_call x6, Pallas kernels, called(): pl.pallas_call(kernel, out_shape=[jax.ShapeDtypeStruct(shape, jnp.float32...  13 us
    ppermute x2, starting transfers between devices, partnered(): return lax.ppermute(value, 'yh', [(0, 1), (1, 0)])  13 us
    ppermute x2, waiting for transfers between devices, partnered(): return lax.ppermute(value, 'yh', [(0, 1), (1, 0)])  11.5 us
    ppermute x2, starting transfers between devices, around(): near = lax.ppermute(value, 'core', [(0, 1), (1, 0)])  10.3 us
    ppermute x2, starting transfers between devices, around(): lax.ppermute(value, LON, across + [(j, i) for i, j in across])  2.94 us
  transfers between devices with their start and end apart: 8, of which 2 were waited for; matrix products, arithmetic and copies ran while one was open for 0% of the time, Pallas kernels for 3%

profile of v15, /device:TPU:1, one launch (start us, length us, event | category | flops | bytes accessed | tf_op | source)
XLA Modules:
  0.0 93.2 jit_solution(6739087001077464671)
XLA Ops:
  0.7 0.6 copy-done.4
  1.3 0.0 copy-done.2
  1.3 1.1 %copy-done = f32[20,20,384]{2,1,0:T(8,128)S(1)} copy-done((f32[20,20,384]{2,1,0:T(8,128)S(1)}, f32[20,20,384]{2,1,0:T(8,128)}, u32[]{:S(2)}) %copy-start) | copy-done | bytes 614424
  2.4 0.6 early.1
  3.1 0.7 collective-permute-start.1
  3.8 6.0 %collective-permute-start = (f32[400,128]{1,0:T(8,128)S(1)}, f32[400,128]{1,0:T(8,128)S(1)}, u32[]{:S(2)}, u32[]{:S(2)}) collective-permute-start(f32[400,128]{1,0:T(8,128)S(1)} %get-tuple-element.14.own), channel_id=1, source_target_pairs={{0,32},{32,0},{1,33},{33,1},{2,34},{34,2},{3,35},{35,3},{4,36},{36... | collective-permute-start | bytes 614408 | tf_op jit(solution)/shard_map/ppermute | solution.py:261
  9.8 0.1 fusion.6.weights
  9.9 0.1 add_convert_fusion.low
  10.0 1.2 %late.1 = (f32[400,128]{1,0:T(8,128)S(1)}, f32[40,120]{1,0:T(8,128)S(1)}, f32[40,120]{1,0:T(8,128)S(1)}) custom-call(s32[2]{0:T(128)S(1)} %add_convert_fusion.low, f32[40,1]{1,0:T(8,128)S(1)} %fusion.6.weights, f32[1,129]{1,0:T(1,128)S(1)} %bitcast.10, f32[1,41]{1,0:T(1,128)S(1)} %get-tuple-element.10.lat_kernel, f32[1,41]{1,0:T(1,128)S(1)} %get-tuple-element.11.lon_kernel, ...), custom_call_target="tpu_custom_call" | custom-call | tf_op jit(solution)/shard_map/late/pallas_call | solution.py:242
  11.2 2.8 %collective-permute-start.5 = (f32[400,128]{1,0:T(8,128)S(1)}, f32[400,128]{1,0:T(8,128)S(1)}, u32[]{:S(2)}, u32[]{:S(2)}) collective-permute-start(f32[400,128]{1,0:T(8,128)S(1)} %get-tuple-element.15.own), channel_id=1, source_target_pairs={{1,2},{3,4},{5,6},{7,8},{9,10},{11,12},{13,14},{15,16},{17,18},{19... | collective-permute-start | bytes 614408 | tf_op jit(solution)/shard_map/ppermute | solution.py:257
  14.0 4.2 %collective-permute-start.4 = (f32[400,128]{1,0:T(8,128)S(1)}, f32[400,128]{1,0:T(8,128)S(1)}, u32[]{:S(2)}, u32[]{:S(2)}) collective-permute-start(f32[400,128]{1,0:T(8,128)S(1)} %get-tuple-element.15.own), channel_id=1, source_target_pairs={{0,1},{1,0},{2,3},{3,2},{4,5},{5,4},{6,7},{7,6},{8,9},{9,8},{10,11... | collective-permute-start | bytes 614408 | tf_op jit(solution)/shard_map/ppermute | solution.py:255
  18.3 0.0 collective-permute-done.1.far
  18.3 2.7 %collective-permute-done.near = f32[400,128]{1,0:T(8,128)S(1)} collective-permute-done((f32[400,128]{1,0:T(8,128)S(1)}, f32[400,128]{1,0:T(8,128)S(1)}, u32[]{:S(2)}, u32[]{:S(2)}) %collective-permute-start) | collective-permute-done | bytes 204832 | tf_op jit(solution)/shard_map/ppermute | solution.py:261
  21.0 0.6 lat.1.refs_1_
  21.6 0.1 collective-permute-start.3
  21.7 6.1 %collective-permute-start.2 = (f32[400,128]{1,0:T(8,128)S(1)}, f32[400,128]{1,0:T(8,128)S(1)}, u32[]{:S(2)}, u32[]{:S(2)}) collective-permute-start(f32[400,128]{1,0:T(8,128)S(1)} %lat.1.refs_1_), channel_id=1, source_target_pairs={{0,1},{1,0},{2,3},{3,2},{4,5},{5,4},{6,7},{7,6},{8,9},{9,8},{10,11... | collective-permute-start | bytes 614408 | tf_op jit(solution)/shard_map/ppermute | solution.py:255
  27.8 0.0 collective-permute-done.5.far
  27.8 0.0 collective-permute-done.4.near
  27.8 0.6 lon.1.refs_4_
  28.4 0.7 collective-permute-start.7
  29.1 6.9 %collective-permute-start.6 = (f32[400,128]{1,0:T(8,128)S(1)}, f32[400,128]{1,0:T(8,128)S(1)}, u32[]{:S(2)}, u32[]{:S(2)}) collective-permute-start(f32[400,128]{1,0:T(8,128)S(1)} %lon.1.refs_4_), channel_id=1, source_target_pairs={{0,32},{32,0},{1,33},{33,1},{2,34},{34,2},{3,35},{35,3},{4,36},{36... | collective-permute-start | bytes 614408 | tf_op jit(solution)/shard_map/ppermute | solution.py:261
  36.0 0.0 collective-permute-done.3.refs_2_
  36.0 0.0 collective-permute-done.2.refs_0_
  36.0 0.0 collective-permute-done.7.refs_5_
  36.0 8.7 %collective-permute-done.6.refs_3_ = f32[400,128]{1,0:T(8,128)S(1)} collective-permute-done((f32[400,128]{1,0:T(8,128)S(1)}, f32[400,128]{1,0:T(8,128)S(1)}, u32[]{:S(2)}, u32[]{:S(2)}) %collective-permute-start.6) | collective-permute-done | bytes 204832 | tf_op jit(solution)/shard_map/ppermute | solution.py:261
  44.8 1.9 %last.1 = (f32[2,400,128]{2,1,0:T(8,128)S(1)}, f32[320,128]{1,0:T(8,128)S(1)}) custom-call(f32[40,120]{1,0:T(8,128)S(1)} %get-tuple-element.12.band.lon_band, f32[40,120]{1,0:T(8,128)S(1)} %get-tuple-element.13.band.lat_band, f32[400,128]{1,0:T(8,128)S(1)} %collective-permute-done.2.refs_0_, f32[400,128]{1,0:T(8,128)S(1)} %lat.1.refs_1_, ...), custom_call_target="tpu_custom_call" | custom-call | tf_op jit(solution)/shard_map/last/pallas_call | solution.py:242
  46.7 16.1 %all_to_all.15 = f32[32,1,1280]{2,1,0:T(1,128)S(1)} all-to-all(f32[32,1,1280]{2,1,0:T(1,128)S(1)} %bitcast.8), channel_id=1, replica_groups=mesh['x'=4,'yh'=2,'yl'=2,'z'=8,'core'=2] {'x','yh','yl','core'}, dimensions={0} | all-to-all | bytes 327680 | tf_op jit(solution)/shard_map/all_to_all | solution.py:27
  62.9 0.1 reduce_sum.18
  63.0 9.3 %all_to_all.16 = f32[8,1,1280]{2,1,0:T(1,128)S(1)} all-to-all(f32[8,1,1280]{2,1,0:T(1,128)S(1)} %broadcast_in_dim.25), channel_id=1, replica_groups=mesh['x'=4,'yh'=2,'yl'=2,'z'=8,'core'=2] {'z'}, dimensions={0} | all-to-all | bytes 81920 | tf_op jit(solution)/shard_map/all_to_all | solution.py:22
  72.4 0.1 broadcast_in_dim.26
  72.5 12.7 %all_to_all.17 = f32[32,1,1280]{2,1,0:T(1,128)S(1)} all-to-all(f32[32,1,1280]{2,1,0:T(1,128)S(1)} %broadcast_in_dim.26), channel_id=1, replica_groups=mesh['x'=4,'yh'=2,'yl'=2,'z'=8,'core'=2] {'x','yh','yl','core'}, dimensions={0} | all-to-all | bytes 327680 | tf_op jit(solution)/shard_map/all_to_all | solution.py:22
  85.2 8.0 %factor.1 = (f32[20,20,256]{2,1,0:T(8,128)}, f32[256,256]{1,0:T(8,128)}) custom-call(f32[320,128]{1,0:T(8,128)S(1)} %bitcast.7, f32[2,400,128]{2,1,0:T(8,128)S(1)} %get-tuple-element.17.matrix), custom_call_target="tpu_custom_call" | custom-call | tf_op jit(solution)/shard_map/factor/pallas_call | solution.py:242
  (9 shorter events, 0.1 us)
Async XLA Ops:
  0.6 0.7 copy-start.4
  0.6 0.7 copy-start.2
  0.7 0.7 copy-start.3
  1.3 1.1 %copy-start = (f32[20,20,384]{2,1,0:T(8,128)S(1)}, f32[20,20,384]{2,1,0:T(8,128)}, u32[]{:S(2)}) copy-start(f32[20,20,384]{2,1,0:T(8,128)} %field.3) | copy-start | bytes 1843204
  2.4 7.6 %copy-start.1 = (f32[20,20,384]{2,1,0:T(8,128)S(1)}, f32[20,20,384]{2,1,0:T(8,128)}, u32[]{:S(2)}) copy-start(f32[20,20,384]{2,1,0:T(8,128)} %field.3) | copy-start | bytes 1843204
  3.1 15.2 %collective-permute-start.1 = (f32[400,128]{1,0:T(8,128)S(1)}, f32[400,128]{1,0:T(8,128)S(1)}, u32[]{:S(2)}, u32[]{:S(2)}) collective-permute-start(f32[400,128]{1,0:T(8,128)S(1)} %get-tuple-element.14.own), channel_id=1, source_target_pairs={{32,64},{96,128},{160,192},{64,32},{128,96},{192,160},{33,65},{97,... | collective-permute-start | bytes 614408 | tf_op jit(solution)/shard_map/ppermute | solution.py:274
  3.8 17.2 %collective-permute-start = (f32[400,128]{1,0:T(8,128)S(1)}, f32[400,128]{1,0:T(8,128)S(1)}, u32[]{:S(2)}, u32[]{:S(2)}) collective-permute-start(f32[400,128]{1,0:T(8,128)S(1)} %get-tuple-element.14.own), channel_id=1, source_target_pairs={{0,32},{32,0},{1,33},{33,1},{2,34},{34,2},{3,35},{35,3},{4,36},{36... | collective-permute-start | bytes 614408 | tf_op jit(solution)/shard_map/ppermute | solution.py:261
  11.2 16.6 %collective-permute-start.5 = (f32[400,128]{1,0:T(8,128)S(1)}, f32[400,128]{1,0:T(8,128)S(1)}, u32[]{:S(2)}, u32[]{:S(2)}) collective-permute-start(f32[400,128]{1,0:T(8,128)S(1)} %get-tuple-element.15.own), channel_id=1, source_target_pairs={{1,2},{3,4},{5,6},{7,8},{9,10},{11,12},{13,14},{15,16},{17,18},{19... | collective-permute-start | bytes 614408 | tf_op jit(solution)/shard_map/ppermute | solution.py:257
  14.0 13.8 %collective-permute-start.4 = (f32[400,128]{1,0:T(8,128)S(1)}, f32[400,128]{1,0:T(8,128)S(1)}, u32[]{:S(2)}, u32[]{:S(2)}) collective-permute-start(f32[400,128]{1,0:T(8,128)S(1)} %get-tuple-element.15.own), channel_id=1, source_target_pairs={{0,1},{1,0},{2,3},{3,2},{4,5},{5,4},{6,7},{7,6},{8,9},{9,8},{10,11... | collective-permute-start | bytes 614408 | tf_op jit(solution)/shard_map/ppermute | solution.py:255
  21.6 14.4 %collective-permute-start.3 = (f32[400,128]{1,0:T(8,128)S(1)}, f32[400,128]{1,0:T(8,128)S(1)}, u32[]{:S(2)}, u32[]{:S(2)}) collective-permute-start(f32[400,128]{1,0:T(8,128)S(1)} %lat.1.refs_1_), channel_id=1, source_target_pairs={{1,2},{3,4},{5,6},{7,8},{9,10},{11,12},{13,14},{15,16},{17,18},{19... | collective-permute-start | bytes 614408 | tf_op jit(solution)/shard_map/ppermute | solution.py:257
  21.7 14.3 %collective-permute-start.2 = (f32[400,128]{1,0:T(8,128)S(1)}, f32[400,128]{1,0:T(8,128)S(1)}, u32[]{:S(2)}, u32[]{:S(2)}) collective-permute-start(f32[400,128]{1,0:T(8,128)S(1)} %lat.1.refs_1_), channel_id=1, source_target_pairs={{0,1},{1,0},{2,3},{3,2},{4,5},{5,4},{6,7},{7,6},{8,9},{9,8},{10,11... | collective-permute-start | bytes 614408 | tf_op jit(solution)/shard_map/ppermute | solution.py:255
  28.4 7.6 %collective-permute-start.7 = (f32[400,128]{1,0:T(8,128)S(1)}, f32[400,128]{1,0:T(8,128)S(1)}, u32[]{:S(2)}, u32[]{:S(2)}) collective-permute-start(f32[400,128]{1,0:T(8,128)S(1)} %lon.1.refs_4_), channel_id=1, source_target_pairs={{32,64},{96,128},{160,192},{64,32},{128,96},{192,160},{33,65},{97,... | collective-permute-start | bytes 614408 | tf_op jit(solution)/shard_map/ppermute | solution.py:274
  29.1 15.6 %collective-permute-start.6 = (f32[400,128]{1,0:T(8,128)S(1)}, f32[400,128]{1,0:T(8,128)S(1)}, u32[]{:S(2)}, u32[]{:S(2)}) collective-permute-start(f32[400,128]{1,0:T(8,128)S(1)} %lon.1.refs_4_), channel_id=1, source_target_pairs={{0,32},{32,0},{1,33},{33,1},{2,34},{34,2},{3,35},{35,3},{4,36},{36... | collective-permute-start | bytes 614408 | tf_op jit(solution)/shard_map/ppermute | solution.py:261
